TPU v7x, 32 devices: a whole 2x2x4 slice. The times are simulated.
32 devices in a mesh: strip: 4 (over x, core), img: 8 (over z, y).
Axes of the slice: x: 2, y: 2, z: 4, core: 2. Of those that a mesh axis runs over, the one named last changes fastest.
Arguments:
- features: bfloat16 [160, 32, 32, 256], P('img', 'strip'), may hold values from -6 to 6
- cotangent: bfloat16 [160, 32, 32, 256], P('img', 'strip'), may hold values from -6 to 6
- present: int32 [160], replicated, may hold values from 0 to 1, as said below
- owners: int32 [40], replicated, may hold values from 0 to 39, as said below
- tile_master: float32 [40, 128, 128], P('img'), may hold values from -0.3125 to 0.3125
- tile_mom1: float32 [40, 128, 128], P('img'), may hold values from -80 to 80
- tile_mom2: float32 [40, 128, 128], P('img'), may hold values from 336 to 5120
- stat_left: float32 [40, 128, 128], P('img'), may hold values from -182 to 182044, as said below
- stat_right: float32 [40, 128, 128], P('img'), may hold values from -182 to 182044, as said below
- basis_left: float32 [40, 128, 128], P('img'), may hold values from -1 to 1
- basis_right: float32 [40, 128, 128], P('img'), may hold values from -1 to 1
- proj_master: float32 [256, 64], replicated, may hold values from -0.375 to 0.375
- proj_mom1: float32 [256, 64], replicated, may hold values from -512 to 512
- proj_mom2: float32 [256, 64], replicated, may hold values from 4000 to 32000
- dec_master: float32 [64, 256], replicated, may hold values from -0.75 to 0.75
- dec_mom1: float32 [64, 256], replicated, may hold values from -80 to 80
- dec_mom2: float32 [64, 256], replicated, may hold values from 320 to 5120
- code_master: float32 [512, 64], replicated, may hold values from -3 to 3
- code_mom1: float32 [512, 64], replicated, may hold values from -40 to 40
- code_mom2: float32 [512, 64], replicated, may hold values from 64 to 960
Outputs:
- decoded: bfloat16 [160, 32, 32, 256], P('img', 'strip')
- input_grad: bfloat16 [160, 32, 32, 256], P('img', 'strip')
- quant_loss: float32 [], replicated
- tile_master_new: float32 [40, 128, 128], P('img')
- tile_mom1_new: float32 [40, 128, 128], P('img')
- tile_mom2_new: float32 [40, 128, 128], P('img')
- stat_left_new: float32 [40, 128, 128], P('img')
- stat_right_new: float32 [40, 128, 128], P('img')
- basis_left_new: float32 [40, 128, 128], P('img')
- basis_right_new: float32 [40, 128, 128], P('img')
- proj_new: float32 [256, 64], replicated
- proj_mom1_new: float32 [256, 64], replicated
- proj_mom2_new: float32 [256, 64], replicated
- dec_new: float32 [64, 256], replicated
- dec_mom1_new: float32 [64, 256], replicated
- dec_mom2_new: float32 [64, 256], replicated
- code_new: float32 [512, 64], replicated
- code_mom1_new: float32 [512, 64], replicated
- code_mom2_new: float32 [512, 64], replicated
Inputs may be any that keep to these rules, and one draw needn't show every extreme that they name: On each index of img its present images come first; every index has one or more, some index has all 20. `owners`: distinct slots; both 0 and 39 are used. `stat_left`: symmetric positive definite. `stat_right`: symmetric positive definite.
All inputs are finite; a program needn't handle non-finite values.
Results may differ from a plain program's by a relative error of at most 0.019.
The roundings to bfloat16 on the way count: a program that leaves them out, or rounds other values in their place, can miss the bound.
Values may be sent and summed in bfloat16 or wider, within the bound.
No kernel may reach another device: no remote copies, remote signals or barrier semaphores. Data moves between devices by JAX's collectives and lax.ppermute only.
A program may use at most 192 MiB of HBM per device.

v0:
```python
import jax
import jax.numpy as jnp
from jax import lax
from jax.sharding import PartitionSpec as P

STEP = 5


EXACT_PRECISION = lax.Precision.HIGHEST
BETA_ONE = 0.9
BETA_TWO = 0.95
EPSILON = 1e-08
WEIGHT_DECAY = 0.01
SOFTMAX_WARMTH = 4.0
LOSS_WEIGHT = 1.25
TILE_RATE = 0.05
PROJ_RATE = 0.05
DEC_RATE = 0.1
CODE_RATE = 0.3


def padded_2(cells, sides, width):
    for axis, dim in sides:
        count = lax.axis_size(axis)
        ends = count - 1
        head = lax.slice_in_dim(cells, 0, width, axis=dim)
        tail = lax.slice_in_dim(cells, cells.shape[dim] - width, cells.shape[dim], axis=dim)
        cells = jnp.concatenate(
            [
                lax.ppermute(tail, axis, [(i, (i + 1) % count) for i in range(ends)]),
                cells,
                lax.ppermute(head, axis, [((i + 1) % count, i) for i in range(ends)]),
            ],
            axis=dim,
        )
    return cells


def split_tiles(conv_three, conv_one):
    tile = conv_three.shape[1] // 2
    first = conv_three.reshape(9, 2, tile, 2, tile).transpose(0, 1, 3, 2, 4).reshape(36, tile, tile)
    second = conv_one.reshape(2, tile, 2, tile).transpose(0, 2, 1, 3).reshape(4, tile, tile)
    return jnp.concatenate([first, second], axis=0)


def join_tiles(tiles):
    tile = tiles.shape[1]
    conv_three = (
        tiles[:36]
        .reshape(9, 2, 2, tile, tile)
        .transpose(0, 1, 3, 2, 4)
        .reshape(9, 2 * tile, 2 * tile)
    )
    conv_one = (
        tiles[36:].reshape(2, 2, tile, tile).transpose(0, 2, 1, 3).reshape(2 * tile, 2 * tile)
    )
    return (conv_three, conv_one)


def conv_taps(framed, kernel, height, breadth):
    total = None
    for position in range(9):
        row_off = position // 3
        col_off = position % 3
        term = jnp.einsum(
            "nrcx,xy->nrcy",
            framed[:, row_off : row_off + height, col_off : col_off + breadth],
            kernel[position],
            preferred_element_type=jnp.float32,
        )
        total = term if total is None else total + term
    return total


def ortho_step(stats, basis):
    moved = jnp.einsum("sij,sjk->sik", stats, basis, precision=EXACT_PRECISION)
    gram = jnp.einsum("sji,sjk->sik", moved, moved, precision=EXACT_PRECISION)
    factor = jnp.linalg.cholesky(gram)
    solved = jax.scipy.linalg.solve_triangular(factor, jnp.swapaxes(moved, 1, 2), lower=True)
    return jnp.swapaxes(solved, 1, 2)


def rotated_adam(gradient, master, first, second, left, right, basis_left, basis_right):
    turned = jnp.einsum("sji,sjk->sik", basis_left, gradient, precision=EXACT_PRECISION)
    turned = jnp.einsum("sik,skl->sil", turned, basis_right, precision=EXACT_PRECISION)
    first_new = BETA_ONE * first + (1.0 - BETA_ONE) * turned
    second_new = BETA_TWO * second + (1.0 - BETA_TWO) * turned * turned
    ratio = (
        first_new
        / (1.0 - BETA_ONE**STEP)
        / (jnp.sqrt(second_new / (1.0 - BETA_TWO**STEP)) + EPSILON)
    )
    back = jnp.einsum("sij,sjk->sik", basis_left, ratio, precision=EXACT_PRECISION)
    back = jnp.einsum("sik,slk->sil", back, basis_right, precision=EXACT_PRECISION)
    master_new = master - TILE_RATE * (back + WEIGHT_DECAY * master)
    left_new = BETA_TWO * left + (1.0 - BETA_TWO) * jnp.einsum(
        "sik,sjk->sij", gradient, gradient, precision=EXACT_PRECISION
    )
    right_new = BETA_TWO * right + (1.0 - BETA_TWO) * jnp.einsum(
        "ski,skj->sij", gradient, gradient, precision=EXACT_PRECISION
    )
    return (
        master_new,
        first_new,
        second_new,
        left_new,
        right_new,
        ortho_step(left_new, basis_left),
        ortho_step(right_new, basis_right),
    )


def plain_adam(gradient, master, first, second, rate):
    first_new = BETA_ONE * first + (1.0 - BETA_ONE) * gradient
    second_new = BETA_TWO * second + (1.0 - BETA_TWO) * gradient * gradient
    ratio = (
        first_new
        / (1.0 - BETA_ONE**STEP)
        / (jnp.sqrt(second_new / (1.0 - BETA_TWO**STEP)) + EPSILON)
    )
    return (master - rate * (ratio + WEIGHT_DECAY * master), first_new, second_new)


def body(
    features,
    cotangent,
    present,
    owners,
    tile_master,
    tile_mom1,
    tile_mom2,
    stat_left,
    stat_right,
    basis_left,
    basis_right,
    proj_master,
    proj_mom1,
    proj_mom2,
    dec_master,
    dec_mom1,
    dec_mom2,
    code_master,
    code_mom1,
    code_mom2,
):
    images, height, breadth, channels = features.shape
    gathered = lax.all_gather(tile_master.astype(jnp.bfloat16), "img", axis=0, tiled=True)
    tiles = jnp.take(gathered, owners, axis=0)
    kernel, mixer = join_tiles(tiles)
    alive = lax.dynamic_slice_in_dim(present, lax.axis_index("img") * images, images).astype(
        jnp.float32
    )
    count = jnp.sum(present).astype(jnp.float32) * (height * lax.axis_size("strip") * breadth)
    mask = alive[:, None, None, None]
    feats = features.astype(jnp.float32)
    activated = jax.nn.gelu(feats).astype(jnp.bfloat16)
    padded = padded_2(activated, (("strip", 1),), 1)
    framed = jnp.pad(padded, ((0, 0), (0, 0), (1, 1), (0, 0)))
    preact = conv_taps(framed, kernel, height, breadth)
    inner = jax.nn.gelu(preact).astype(jnp.bfloat16)
    branch = jnp.einsum("nrcx,xy->nrcy", inner, mixer, preferred_element_type=jnp.float32)
    resid = feats + branch
    resid_low = resid.astype(jnp.bfloat16)
    proj_low = proj_master.astype(jnp.bfloat16)
    latent_features = jnp.einsum(
        "nrcx,xl->nrcl", resid_low, proj_low, preferred_element_type=jnp.float32
    )
    latent_low = latent_features.astype(jnp.bfloat16)
    codebook_reduced = code_master.astype(jnp.bfloat16)
    codebook_full_width = codebook_reduced.astype(jnp.float32)
    codeword_norms = jnp.sum(codebook_full_width * codebook_full_width, axis=1)
    assignment_scores = (
        2.0
        * jnp.einsum(
            "htzf,af->htza", latent_low, codebook_reduced, preferred_element_type=jnp.float32
        )
        - codeword_norms
    ) / SOFTMAX_WARMTH
    probs = jax.nn.softmax(assignment_scores, axis=-1)
    probs_low = probs.astype(jnp.bfloat16)
    quant = jnp.einsum(
        "nrck,kl->nrcl", probs_low, codebook_reduced, preferred_element_type=jnp.float32
    )
    quant_low = quant.astype(jnp.bfloat16)
    dec_low = dec_master.astype(jnp.bfloat16)
    decoded = (
        jnp.einsum("nrcl,ly->nrcy", quant_low, dec_low, preferred_element_type=jnp.float32) * mask
    ).astype(jnp.bfloat16)
    diff = latent_features - quant
    loss_part = jnp.sum(jnp.sum(diff * diff, axis=-1) * alive[:, None, None])
    back_out = (cotangent.astype(jnp.float32) * mask).astype(jnp.bfloat16)
    grad_dec = jnp.einsum("nrcl,nrcy->ly", quant_low, back_out, preferred_element_type=jnp.float32)
    scale = LOSS_WEIGHT / (count * latent_features.shape[-1])
    pulled = 2.0 * scale * diff * mask
    d_quant = (
        jnp.einsum("nrcy,ly->nrcl", back_out, dec_low, preferred_element_type=jnp.float32) - pulled
    )
    d_quant_low = d_quant.astype(jnp.bfloat16)
    codebook_gradient = jnp.einsum(
        "nrck,nrcl->kl", probs_low, d_quant_low, preferred_element_type=jnp.float32
    )
    d_probs = jnp.einsum(
        "htzf,af->htza", d_quant_low, codebook_reduced, preferred_element_type=jnp.float32
    )
    d_logits = probs * (d_probs - jnp.sum(probs * d_probs, axis=-1, keepdims=True))
    d_logits_low = d_logits.astype(jnp.bfloat16)
    column_totals_vector = jnp.sum(d_logits_low.astype(jnp.float32), axis=(0, 1, 2))
    codebook_gradient = codebook_gradient + 2.0 / SOFTMAX_WARMTH * jnp.einsum(
        "nrck,nrcl->kl", d_logits_low, latent_low, preferred_element_type=jnp.float32
    )
    codebook_gradient = (
        codebook_gradient
        - 2.0 / SOFTMAX_WARMTH * column_totals_vector[:, None] * codebook_full_width
    )
    d_latent = (
        2.0
        / SOFTMAX_WARMTH
        * jnp.einsum(
            "nrck,kl->nrcl", d_logits_low, codebook_reduced, preferred_element_type=jnp.float32
        )
        + pulled
    )
    d_latent_low = d_latent.astype(jnp.bfloat16)
    grad_proj = jnp.einsum(
        "nrcx,nrcl->xl", resid_low, d_latent_low, preferred_element_type=jnp.float32
    )
    d_resid = jnp.einsum(
        "nrcl,xl->nrcx", d_latent_low, proj_low, preferred_element_type=jnp.float32
    )
    d_branch_low = d_resid.astype(jnp.bfloat16)
    grad_mixer = jnp.einsum(
        "nrcx,nrcy->xy", inner, d_branch_low, preferred_element_type=jnp.float32
    )
    d_inner = jnp.einsum("nrcy,xy->nrcx", d_branch_low, mixer, preferred_element_type=jnp.float32)
    _, gelu_inner = jax.vjp(jax.nn.gelu, preact)
    d_pre_low = gelu_inner(d_inner)[0].astype(jnp.bfloat16)
    kernel_grads = []
    edged = jnp.pad(d_pre_low, ((0, 0), (2, 2), (2, 2), (0, 0)))
    d_framed = None
    for position in range(9):
        row_off = position // 3
        col_off = position % 3
        window = framed[:, row_off : row_off + height, col_off : col_off + breadth]
        kernel_grads.append(
            jnp.einsum("nrcx,nrcy->xy", window, d_pre_low, preferred_element_type=jnp.float32)
        )
        shifted = edged[:, 2 - row_off : 4 - row_off + height, 3 - col_off : 3 - col_off + breadth]
        term = jnp.einsum(
            "nrcy,xy->nrcx", shifted, kernel[position], preferred_element_type=jnp.float32
        )
        d_framed = term if d_framed is None else d_framed + term
    grad_kernel = jnp.stack(kernel_grads, axis=0)
    rims = jnp.stack([d_framed[:, 0], d_framed[:, height + 1]], axis=1)
    beside = padded_2(rims.astype(jnp.bfloat16), (("strip", 1),), 1).astype(rims.dtype)
    d_act = d_framed[:, 1 : height + 1]
    d_act = d_act.at[:, 0].add(beside[:, 0]).at[:, height - 1].add(beside[:, 3])
    _, gelu_outer = jax.vjp(jax.nn.gelu, feats)
    input_grad = (d_resid + gelu_outer(d_act)[0]).astype(jnp.bfloat16)
    local_tiles = split_tiles(grad_kernel, grad_mixer)
    slots_all = tile_master.shape[0] * lax.axis_size("img")
    stacked = (
        jnp.zeros((slots_all, local_tiles.shape[1], local_tiles.shape[2]), jnp.float32)
        .at[owners]
        .set(local_tiles)
    )
    summed = lax.psum(stacked.astype(jnp.bfloat16), "strip").astype(jnp.float32)
    owned = lax.psum_scatter(summed, "img", scatter_dimension=0, tiled=True)
    small = lax.psum((grad_proj, grad_dec, codebook_gradient, loss_part), ("strip", "img"))
    quant_loss = LOSS_WEIGHT * small[3] / (count * latent_features.shape[-1])
    tile_out = rotated_adam(
        owned, tile_master, tile_mom1, tile_mom2, stat_left, stat_right, basis_left, basis_right
    )
    proj_out = plain_adam(small[0], proj_master, proj_mom1, proj_mom2, PROJ_RATE)
    dec_out = plain_adam(small[1], dec_master, dec_mom1, dec_mom2, DEC_RATE)
    code_out = plain_adam(small[2], code_master, code_mom1, code_mom2, CODE_RATE)
    return (
        decoded,
        input_grad,
        quant_loss,
        tile_out[0],
        tile_out[1],
        tile_out[2],
        tile_out[3],
        tile_out[4],
        tile_out[5],
        tile_out[6],
        proj_out[0],
        proj_out[1],
        proj_out[2],
        dec_out[0],
        dec_out[1],
        dec_out[2],
        code_out[0],
        code_out[1],
        code_out[2],
    )


def solution(mesh):
    in_specs = (
        P("img", "strip", None, None),
        P("img", "strip", None, None),
        P(),
        P(),
        P("img", None, None),
        P("img", None, None),
        P("img", None, None),
        P("img", None, None),
        P("img", None, None),
        P("img", None, None),
        P("img", None, None),
        P(),
        P(),
        P(),
        P(),
        P(),
        P(),
        P(),
        P(),
        P(),
    )
    out_specs = (
        P("img", "strip", None, None),
        P("img", "strip", None, None),
        P(),
        P("img", None, None),
        P("img", None, None),
        P("img", None, None),
        P("img", None, None),
        P("img", None, None),
        P("img", None, None),
        P("img", None, None),
        P(),
        P(),
        P(),
        P(),
        P(),
        P(),
        P(),
        P(),
        P(),
    )
    return jax.shard_map(body, mesh=mesh, in_specs=in_specs, out_specs=out_specs, check_vma=False)
```

profile of v0, /device:TPU:0, one launch (start us, length us, event | category | flops | bytes accessed | tf_op | source)
XLA Modules:
  0.0 747.4 jit_solution(6281132317535199509)
XLA Ops:
  21.9 4.5 fusion.29
  26.4 29.3 %all-gather.2.cloned.1.call-done = bf16[40,128,128]{2,1,0:T(8,128)(2,1)} async-done(((bf16[5,128,128]{2,1,0:T(8,128)(2,1)}), bf16[40,128,128]{2,1,0:T(8,128)(2,1)}) %all-gather.2.cloned.1.call-update) | async-done | bytes 1310736 | tf_op jit(solution)/shard_map/all_gather | solution.py:147
  79.3 5.1 fusion.51
  100.4 4.1 fusion.69
  107.8 18.2 %add_add_fusion.1 = f32[20,8,32,256]{3,2,1,0:T(8,128)} fusion(f32[20,8,32,256]{3,2,1,0:T(8,128)} %fusion.69, f32[20,8,32,256]{3,2,1,0:T(8,128)} %fusion.51, f32[20,8,32,256]{3,2,1,0:T(8,128)} %fusion.55, f32[20,8,32,256]{3,2,1,0:T(8,128)} %fusion.144, f32[20,8,32,256]{3,2,1,0:T(8,128)} %fusion.59, f32[20,8,32,256]{3,2,1,0:T(8,128)} %fusion.63, ...), kind=kOutput, calls=%fused_computation.56 | convolution fusion | flops 681574400 | bytes 49938432 | tf_op jit(solution)/shard_map/nrcx,xy->nrcy/dot_general | solution.py:65
  126.0 4.6 fusion.19
  133.0 6.6 fusion.206
  139.6 5.4 multiply_reduce_fusion.1
  162.8 7.5 %fusion.100 = f32[256,256]{1,0:T(8,128)} fusion(f32[20,8,32,256]{3,2,1,0:T(8,128)S(1)} %fusion.167, f32[20,8,32,256]{3,2,1,0:T(8,128)} %add_add_fusion.1), kind=kOutput, calls=%fused_computation.132 | convolution fusion | flops 684195840 | bytes 10747904 | tf_op jit(solution)/shard_map/nrcx,nrcy->xy/dot_general | solution.py:231
  170.3 4.2 fusion.10
  186.4 3.8 fusion.31
  193.9 3.8 fusion.33
  248.4 8.7 %scatter_fusion = f32[40,128,128]{2,1,0:T(8,128)} fusion(f32[40,128,128]{2,1,0:T(8,128)} %broadcast_in_dim.30, s32[40]{0:T(128)S(1)} %copy-done.57, f32[40,128,128]{2,1,0:T(8,128)} %pad_maximum_fusion.2), kind=kCustom, calls=%fused_computation.1 | custom fusion | bytes 7864480 | tf_op jit(solution)/shard_map/scatter | solution.py:264
  260.3 5.0 fusion.107
  269.2 39.4 %psum.35 = f32[]{:T(128)} all-reduce(f32[]{:T(128)} %multiply_reduce_fusion.2), channel_id=1, replica_groups=mesh['strip'=4,'img'=8] {'strip','img'}, use_global_device_ids=true, to_apply=%region_7.8 | all-reduce | flops 1 | bytes 8 | tf_op jit(solution)/shard_map/psum | solution.py:268
  312.5 20.1 %fusion.215 = (bf16[20,10,32,256]{3,2,1,0:T(8,128)(2,1)S(1)}, f32[20,10,32,256]{3,2,1,0:T(8,128)}) fusion(bf16[256,256,1,1]{1,0,2,3:T(8,128)(2,1)S(1)} %copy-done.22, bf16[20,8,32,256]{3,2,1,0:T(8,128)(2,1)S(1)} %fusion.10, f32[20,10,32,256]{3,2,1,0:T(8,128)} %fusion.37, f32[20,10,32,256]{3,2,1,0:T(8,128)} %fusion.36, f32[20,10,32,256]{3,2,1,0:T(8,128)} %fusion.35, ...), kind=kOutput, calls=%fused_computation.273 | convolution fusion | flops 853606400 | bytes 65011712 | tf_op jit(solution)/shard_map/nrcy,xy->nrcx/dot_general | solution.py:248
  336.7 5.8 slice.263
  344.8 86.5 %all-reduce.8.cloned.1.call-done = (f32[256,64]{0,1:T(8,128)}, f32[64,256]{1,0:T(8,128)}, f32[512,64]{0,1:T(8,128)}) async-done(((f32[256,64]{0,1:T(8,128)}, f32[64,256]{1,0:T(8,128)}, f32[512,64]{0,1:T(8,128)}), (f32[256,64]{0,1:T(8,128)}, f32[64,256]{1,0:T(8,128)}, f32[512,64]{0,1:T(8,128)})) %all-reduce.8.cloned.1.call-update) | async-done | bytes 262160 | tf_op jit(solution)/shard_map/psum | solution.py:268
  440.7 7.8 %fusion.14 = bf16[20,8,32,256]{3,2,1,0:T(8,128)(2,1)} fusion(f32[20,8,32,256]{3,2,1,0:T(8,128)} %copy-done.9, bf16[20,8,32,256]{3,2,1,0:T(8,128)(2,1)S(1)} %copy-done.15, f32[20,8,32,256]{3,2,1,0:T(8,128)} %fusion.111), kind=kLoop, calls=%fused_computation.41 | loop fusion | flops 28835840 | bytes 15728640 | tf_op jit(solution)/shard_map/convert_element_type | solution.py:258
  448.6 55.7 %reduce-scatter.2.cloned.1.call-done = f32[5,128,128]{2,1,0:T(8,128)} async-done(((f32[40,128,128]{2,1,0:T(8,128)}), f32[5,128,128]{2,1,0:T(8,128)}) %reduce-scatter.2.cloned.1.call-update) | async-done | bytes 327696 | tf_op jit(solution)/shard_map/reduce_scatter | solution.py:267
  511.5 59.4 %custom-call.8 = f32[5,128,128]{2,1,0:T(8,128)S(1)} custom-call(f32[5,128,128]{2,1,0:T(8,128)} %fusion.121), custom_call_target="Cholesky" | custom-call | tf_op jit(solution)/shard_map/jit(cholesky)/cholesky | solution.py:78
  571.8 59.6 %custom-call.10 = f32[5,128,128]{2,1,0:T(8,128)S(1)} custom-call(f32[5,128,128]{2,1,0:T(8,128)} %fusion.118), custom_call_target="Cholesky" | custom-call | tf_op jit(solution)/shard_map/jit(cholesky)/cholesky | solution.py:78
  631.8 49.8 %custom-call.11 = f32[5,1,128,128]{2,3,1,0:T(8,128)} custom-call(f32[5,1,128,128]{3,2,1,0:T(8,128)S(1)} %get-tuple-element.154), custom_call_target="InvertDiagBlocksLowerTriangular" | custom-call | tf_op jit(solution)/shard_map/jit(_solve_triangular)/vmap()/triangular_solve | solution.py:79
  684.2 49.3 %custom-call.9 = f32[5,1,128,128]{2,3,1,0:T(8,128)S(1)} custom-call(f32[5,1,128,128]{3,2,1,0:T(8,128)S(1)} %get-tuple-element.155), custom_call_target="InvertDiagBlocksLowerTriangular" | custom-call | tf_op jit(solution)/shard_map/jit(_solve_triangular)/vmap()/triangular_solve | solution.py:79
  (255 shorter events, 185.7 us)
Async XLA Ops:
  7.2 499.0 %copy-start = (f32[5,128,128]{2,1,0:T(8,128)S(1)}, f32[5,128,128]{2,1,0:T(8,128)}, u32[]{:S(2)}) copy-start(f32[5,128,128]{2,1,0:T(8,128)} %param.37) | copy-start | bytes 983044
  7.2 48.4 %all-gather.2.cloned.1.call-start = ((), (), s32[]{:S(2)}) async-start(), calls=%async_computation.1 | async-start | bytes 1474560 | tf_op jit(solution)/shard_map/all_gather | solution.py:147
  9.0 300.2 %all-reduce.6.cloned.1.call-start = ((), (), s32[]{:S(2)}) async-start(), calls=%async_computation.2 | async-start | bytes 2621440 | tf_op jit(solution)/shard_map/psum | solution.py:266
  12.6 91.9 %copy-start.3 = (bf16[20,8,32,256]{3,2,1,0:T(8,128)(2,1)}, bf16[20,8,32,256]{3,2,1,0:T(8,128)(2,1)S(1)}, u32[]{:S(2)}) copy-start(bf16[20,8,32,256]{3,2,1,0:T(8,128)(2,1)S(1)} %fusion.18) | copy-start | bytes 7864324
  13.6 7.2 collective-permute-start
  15.9 6.0 collective-permute-start.1
  67.6 40.2 %copy-start.21 = (bf16[256,256,1,1]{1,0,2,3:T(8,128)(2,1)}, bf16[256,256,1,1]{1,0,2,3:T(8,128)(2,1)S(1)}, u32[]{:S(2)}) copy-start(bf16[256,256,1,1]{1,0,2,3:T(8,128)(2,1)S(1)} %reshape.218) | copy-start | bytes 393220
  132.9 24.0 %copy-start.6 = (f32[20,8,32,64]{3,2,1,0:T(8,128)}, f32[20,8,32,64]{3,2,1,0:T(8,128)S(1)}, u32[]{:S(2)}) copy-start(f32[20,8,32,64]{3,2,1,0:T(8,128)S(1)} %fusion.169) | copy-start | bytes 3932164
  260.2 171.2 %all-reduce.8.cloned.1.call-start = ((), (), s32[]{:S(2)}) async-start(), calls=%async_computation.4 | async-start | bytes 524288 | tf_op jit(solution)/shard_map/psum | solution.py:268
  265.3 238.9 %reduce-scatter.2.cloned.1.call-start = ((), (), s32[]{:S(2)}) async-start(), calls=%async_computation.3 | async-start | bytes 2949120 | tf_op jit(solution)/shard_map/reduce_scatter | solution.py:267
  269.1 43.3 %copy-start.22 = (bf16[256,256,1,1]{1,0,2,3:T(8,128)(2,1)S(1)}, bf16[256,256,1,1]{1,0,2,3:T(8,128)(2,1)}, u32[]{:S(2)}) copy-start(bf16[256,256,1,1]{1,0,2,3:T(8,128)(2,1)} %copy-done.21) | copy-start | bytes 393220
  333.4 103.0 %collective-permute-start.2 = (bf16[20,1,32,256]{3,2,1,0:T(8,128)(2,1)S(1)}, bf16[20,1,32,256]{3,2,1,0:T(8,128)(2,1)}, u32[]{:S(2)}, u32[]{:S(2)}) collective-permute-start(bf16[20,1,32,256]{3,2,1,0:T(8,128)(2,1)S(1)} %get-tuple-element.139), channel_id=1, source_target_pairs={{0,8},{8,16},{16,24},{1,9},{9,17},{17,25},{2,10},{10,18},{18,26},{... | collective-permute-start | bytes 983048 | tf_op jit(solution)/shard_map/ppermute | solution.py:30
  335.4 101.0 %collective-permute-start.3 = (bf16[20,1,32,256]{3,2,1,0:T(8,128)(2,1)}, bf16[20,1,32,256]{3,2,1,0:T(8,128)(2,1)}, u32[]{:S(2)}, u32[]{:S(2)}) collective-permute-start(bf16[20,1,32,256]{3,2,1,0:T(8,128)(2,1)} %get-tuple-element.140), channel_id=1, source_target_pairs={{8,0},{16,8},{24,16},{9,1},{17,9},{25,17},{10,2},{18,10},{26,18},{... | collective-permute-start | bytes 983048 | tf_op jit(solution)/shard_map/ppermute | solution.py:32
  342.5 88.8 %copy-start.44 = (f32[256,64]{0,1:T(8,128)S(1)}, f32[256,64]{0,1:T(8,128)}, u32[]{:S(2)}) copy-start(f32[256,64]{0,1:T(8,128)} %param.38) | copy-start | bytes 196612
  342.5 92.0 %copy-start.46 = (f32[512,64]{0,1:T(8,128)S(1)}, f32[512,64]{0,1:T(8,128)}, u32[]{:S(2)}) copy-start(f32[512,64]{0,1:T(8,128)} %param.44) | copy-start | bytes 393220
  344.8 95.9 %copy-start.15 = (bf16[20,8,32,256]{3,2,1,0:T(8,128)(2,1)S(1)}, bf16[20,8,32,256]{3,2,1,0:T(8,128)(2,1)}, u32[]{:S(2)}) copy-start(bf16[20,8,32,256]{3,2,1,0:T(8,128)(2,1)} %param.27) | copy-start | bytes 7864324
  448.5 60.8 %copy-start.20 = (f32[5,128,128]{2,1,0:T(8,128)S(1)}, f32[5,128,128]{2,1,0:T(8,128)}, u32[]{:S(2)}) copy-start(f32[5,128,128]{2,1,0:T(8,128)} %param.36) | copy-start | bytes 983044
  506.2 65.6 %copy-start.18 = (f32[5,128,128]{2,1,0:T(8,128)}, f32[5,128,128]{2,1,0:T(8,128)S(1)}, u32[]{:S(2)}) copy-start(f32[5,128,128]{2,1,0:T(8,128)S(1)} %fusion.80) | copy-start | bytes 983044
  506.2 125.2 %copy-start.55 = (pred[128,128]{1,0:T(8,128)(4,1)S(1)}, pred[128,128]{1,0:T(8,128)(4,1)}, u32[]{:S(2)}) copy-start(pred[128,128]{1,0:T(8,128)(4,1)} %iota_compare_fusion.3) | copy-start | bytes 49156
  506.7 125.0 %copy-start.54 = (pred[128,128]{1,0:T(8,128)(4,1)S(1)}, pred[128,128]{1,0:T(8,128)(4,1)}, u32[]{:S(2)}) copy-start(pred[128,128]{1,0:T(8,128)(4,1)} %iota_compare_fusion.2) | copy-start | bytes 49156
  509.4 173.9 %copy-start.19 = (f32[5,128,128]{2,1,0:T(8,128)}, f32[5,128,128]{2,1,0:T(8,128)S(1)}, u32[]{:S(2)}) copy-start(f32[5,128,128]{2,1,0:T(8,128)S(1)} %fusion.79) | copy-start | bytes 983044
  510.7 224.4 %copy-start.16 = (f32[5,128,128]{2,1,0:T(8,128)S(1)}, f32[5,128,128]{2,1,0:T(8,128)}, u32[]{:S(2)}) copy-start(f32[5,128,128]{2,1,0:T(8,128)} %reduce-scatter.2.cloned.1.call-done) | copy-start | bytes 983044
  631.8 106.2 %copy-start.17 = (f32[5,128,128]{2,1,0:T(8,128)S(1)}, f32[5,128,128]{2,1,0:T(8,128)}, u32[]{:S(2)}) copy-start(f32[5,128,128]{2,1,0:T(8,128)} %param.31) | copy-start | bytes 983044
  681.6 54.3 %copy-start.47 = (f32[5,128,128]{2,1,0:T(8,128)S(1)}, f32[5,128,128]{2,1,0:T(8,128)}, u32[]{:S(2)}) copy-start(f32[5,128,128]{2,1,0:T(8,128)} %param.32) | copy-start | bytes 983044
  (46 other events, 244.9 us)
Sparse Core Ops, SparseCore 0:
  10.8 44.7 all-gather.1
  260.3 37.9 all-reduce.5
  305.2 126.0 all-reduce.7
  434.7 69.5 reduce-scatter.1
where the time goes:
time: 752 us; the launch traced here: 747 us
  other arithmetic  262 us (35%)
  matrix products  175 us (23%)
  waiting for transfers between devices  173 us (23%)
  local copies, waits for them, and re-layouts  73.5 us (10%)
  blocking collectives  39.4 us (5%)
  between operations  17.4 us (2%)
    another operation x5, other arithmetic, ortho_step(): factor = jnp.linalg.cholesky(gram)  120 us
    another operation x4, other arithmetic, ortho_step(): jax.scipy.linalg.solve_triangular(factor, jnp.swapaxes(moved, 1, 2), lowe...  99.8 us
    psum x1, waiting for transfers between devices, body(): lax.psum((grad_proj, grad_dec, codebook_gradient, loss_part), ('strip', '...  86.5 us
    reduce_scatter x1, waiting for transfers between devices, body(): owned = lax.psum_scatter(summed, 'img', scatter_dimension=0, tiled=True)  55.7 us
    dot_general x9, matrix products, body(): jnp.einsum('nrcy,xy->nrcx', shifted, kernel[position], preferred_element_...  50.3 us
    dot_general x9, matrix products, conv_taps(): jnp.einsum('nrcx,xy->nrcy', framed[:, row_off:row_off + height, col_off:c...  46.6 us
    psum x1, blocking collectives, body(): lax.psum((grad_proj, grad_dec, codebook_gradient, loss_part), ('strip', '...  39.4 us
    all_gather x1, waiting for transfers between devices, body(): lax.all_gather(tile_master.astype(jnp.bfloat16), 'img', axis=0, tiled=True)  29.3 us
  transfers between devices with their start and end apart: 8, of which 4 were waited for; matrix products, arithmetic and copies ran while one was open for 9% of the time, Pallas kernels for 0%

commit v1 on v0

v1 whole, which is shorter than its diff:
```python
import jax
import jax.numpy as jnp
from jax import lax
from jax.experimental import pallas as pl
from jax.experimental.pallas import tpu as pltpu
from jax.sharding import PartitionSpec as P

STEP = 5
HIGHEST = lax.Precision.HIGHEST
BETA_ONE = 0.9
BETA_TWO = 0.95
EPSILON = 1e-08
WEIGHT_DECAY = 0.01
SOFTMAX_WARMTH = 4.0
LOSS_WEIGHT = 1.25
TILE_RATE = 0.05
PROJ_RATE = 0.05
DEC_RATE = 0.1
CODE_RATE = 0.3

F32 = jnp.float32
BF16 = jnp.bfloat16
NN = ((1,), (0,))
NT = ((1,), (1,))
TN = ((0,), (0,))
GELU_A = 0.7978845608028654
GELU_B = 0.044715
VMEM_LIMIT = 56 * 1024 * 1024


def dot(a, b, dims=NN, precision=None):
    return lax.dot_general(a, b, (dims, ((), ())), precision=precision, preferred_element_type=F32)


def gelu_tanh(x):
    return jnp.tanh(GELU_A * (x + GELU_B * (x * x * x)))


def gelu(x):
    return 0.5 * x * (1.0 + gelu_tanh(x))


def gelu_both(x):
    square = x * x
    t = jnp.tanh(GELU_A * x * (1.0 + GELU_B * square))
    half = 0.5 * (1.0 + t)
    slope = half + 0.5 * x * (1.0 - t * t) * (GELU_A + 3.0 * GELU_A * GELU_B * square)
    return x * half, slope


def column_shifts(rows, wide):
    count = rows.shape[0]
    column = lax.broadcasted_iota(jnp.int32, rows.shape, 0) % wide
    before = jnp.where(column == 0, 0.0, pltpu.roll(rows, 1, 0))
    after = jnp.where(column == wide - 1, 0.0, pltpu.roll(rows, count - 1, 0))
    return before, after


def place_weights(place, gathered, weights, mixer):
    tile = gathered.shape[1]
    for t in range(40):
        block = gathered[place[t]]
        i, j = (t // 2) % 2, t % 2
        if t < 36:
            p = t // 4
            row = (p % 3) * 2 * tile + i * tile
            weights[p // 3, row : row + tile, j * tile : (j + 1) * tile] = block
        else:
            mixer[i * tile : (i + 1) * tile, j * tile : (j + 1) * tile] = block


def main_kernel(
    place,
    slots,
    alive_all,
    pull_all,
    core,
    feat,
    above,
    below,
    cot,
    gathered,
    proj,
    dec,
    code,
    norms,
    decoded,
    d_pre_out,
    d_resid_out,
    keep,
    send,
    g_proj,
    g_dec,
    g_code,
    totals,
    loss,
    weights,
    mixer,
    framed,
    d_pre_turned,
    sums,
    g_mixer,
):
    step = pl.program_id(0)
    steps = pl.num_programs(0)
    height, wide, channels = feat.shape[1:]
    count = height * wide
    tile = gathered.shape[1]

    @pl.when(step == 0)
    def _():
        place_weights(place, gathered, weights, mixer)
        g_mixer[...] = jnp.zeros_like(g_mixer)
        g_proj[...] = jnp.zeros_like(g_proj)
        g_dec[...] = jnp.zeros_like(g_dec)
        g_code[...] = jnp.zeros_like(g_code)
        totals[...] = jnp.zeros_like(totals)
        loss[...] = jnp.zeros_like(loss)

    alive = alive_all[step]
    pull = pull_all[step]
    feats = feat[0].reshape(count, channels).astype(F32)
    column = jnp.concatenate(
        [above[0, 0].astype(F32), feats, below[0, 0].astype(F32)], axis=0
    )
    activated = gelu(column)
    before, after = column_shifts(activated, wide)
    framed[step, :, 0:channels] = before.astype(BF16)
    framed[step, :, channels : 2 * channels] = activated.astype(BF16)
    framed[step, :, 2 * channels : 3 * channels] = after.astype(BF16)
    preact = dot(framed[step, 0:count, :], weights[0])
    preact += dot(framed[step, wide : wide + count, :], weights[1])
    preact += dot(framed[step, 2 * wide : 2 * wide + count, :], weights[2])
    inner_full, slope = gelu_both(preact)
    inner = inner_full.astype(BF16)
    resid_low = (feats + dot(inner, mixer[...])).astype(BF16)
    latent = dot(resid_low, proj[...])
    latent_low = latent.astype(BF16)
    logits = (2.0 / SOFTMAX_WARMTH) * dot(latent_low, code[...], NT) - norms[...]
    powers = jnp.exp(logits - jnp.max(logits, axis=1, keepdims=True))
    probs = powers * (1.0 / jnp.sum(powers, axis=1, keepdims=True))
    probs_low = probs.astype(BF16)
    quant = dot(probs_low, code[...])
    quant_low = quant.astype(BF16)
    decoded[0] = (dot(quant_low, dec[...]) * alive).astype(BF16).reshape(height, wide, channels)
    diff = latent - quant
    loss[...] += alive * jnp.sum(diff * diff, axis=0, keepdims=True)
    back_out = (cot[0].reshape(count, channels).astype(F32) * alive).astype(BF16)
    g_dec[...] += dot(quant_low, back_out, TN)
    pulled = pull * diff
    d_quant = (dot(back_out, dec[...], NT) - pulled).astype(BF16)
    d_probs = dot(d_quant, code[...], NT)
    d_logits = probs * (d_probs - jnp.sum(probs * d_probs, axis=1, keepdims=True))
    d_logits = d_logits.astype(BF16)
    totals[...] += jnp.sum(d_logits.astype(F32), axis=0, keepdims=True)
    g_code[...] += dot(d_quant, probs_low, TN) + (2.0 / SOFTMAX_WARMTH) * dot(
        latent_low, d_logits, TN
    )
    d_latent = ((2.0 / SOFTMAX_WARMTH) * dot(d_logits, code[...]) + pulled).astype(BF16)
    g_proj[...] += dot(d_latent, resid_low, TN)
    d_resid = dot(d_latent, proj[...], NT).astype(BF16)
    d_resid_out[0] = d_resid.reshape(height, wide, channels)
    g_mixer[...] += dot(d_resid, inner, TN)
    d_pre = (slope * dot(d_resid, mixer[...], NT)).astype(BF16)
    d_pre_out[0] = d_pre.reshape(height, wide, channels)
    d_pre_turned[step] = d_pre.T

    @pl.when(step == steps - 1)
    def _():
        group = 4 if steps % 4 == 0 else 1
        sums[...] = jnp.zeros_like(sums)
        for line in range(3):

            def add(g, carry, line=line):
                total = None
                for n in range(group):
                    i = g * group + n
                    window = framed[i, line * wide : line * wide + count, :]
                    term = dot(d_pre_turned[i], window)
                    total = term if total is None else total + term
                sums[line] += total
                return carry

            lax.fori_loop(0, steps // group, add, 0)
        for ref in (keep, send):
            ref[...] = jnp.zeros_like(ref)
        quarter = tile // 4
        for t in range(40):
            i, j = (t // 2) % 2, t % 2
            if t < 36:
                p = t // 4
                left = (p % 3) * channels + i * tile
                block = sums[p // 3, j * tile : (j + 1) * tile, left : left + tile]
            else:
                block = g_mixer[j * tile : (j + 1) * tile, i * tile : (i + 1) * tile]
            block = block.astype(BF16)
            for q in range(4):
                part = block[q * quarter : (q + 1) * quarter]

                @pl.when(core[0] == q % 2)
                def _(part=part, q=q, t=t):
                    keep[q // 2, slots[t]] = part

                @pl.when(core[0] != q % 2)
                def _(part=part, q=q, t=t):
                    send[q // 2, slots[t]] = part


def main_call(place, slots, alive, pull, core, feat, above, below, cot, gathered, proj, dec, code, norms):
    images, height, wide, channels = feat.shape
    latent = proj.shape[1]
    words = code.shape[0]
    slot_count, tile = gathered.shape[:2]
    smem = pl.BlockSpec(memory_space=pltpu.SMEM)
    strip = pl.BlockSpec((1, height, wide, channels), lambda i: (i, 0, 0, 0))
    line = pl.BlockSpec((1, 1, wide, channels), lambda i: (i, 0, 0, 0))

    def whole(shape):
        return pl.BlockSpec(shape, lambda i: (0,) * len(shape))

    big = jax.ShapeDtypeStruct(feat.shape, BF16)
    part = (2, slot_count, tile // 4, tile)
    shapes = (
        big,
        big,
        big,
        jax.ShapeDtypeStruct(part, BF16),
        jax.ShapeDtypeStruct(part, BF16),
        jax.ShapeDtypeStruct((latent, channels), F32),
        jax.ShapeDtypeStruct((latent, channels), F32),
        jax.ShapeDtypeStruct((latent, words), F32),
        jax.ShapeDtypeStruct((1, words), F32),
        jax.ShapeDtypeStruct((1, latent), F32),
    )
    return pl.pallas_call(
        main_kernel,
        grid=(images,),
        in_specs=[smem] * 5
        + [strip, line, line, strip]
        + [whole(a.shape) for a in (gathered, proj, dec, code, norms)],
        out_specs=[strip] * 3 + [whole(s.shape) for s in shapes[3:]],
        out_shape=shapes,
        scratch_shapes=[
            pltpu.VMEM((3, 3 * channels, channels), BF16),
            pltpu.VMEM((channels, channels), BF16),
            pltpu.VMEM((images, (height + 2) * wide, 3 * channels), BF16),
            pltpu.VMEM((images, channels, height * wide), BF16),
            pltpu.VMEM((3, channels, 3 * channels), F32),
            pltpu.VMEM((channels, channels), F32),
        ],
        compiler_params=pltpu.CompilerParams(vmem_limit_bytes=VMEM_LIMIT),
    )(place, slots, alive, pull, core, feat, above, below, cot, gathered, proj, dec, code, norms)


def input_kernel(place, feat, d_resid, d_pre, above, below, gathered, out, weights, mixer):
    height, wide, channels = feat.shape[1:]
    count = height * wide

    @pl.when(pl.program_id(0) == 0)
    def _():
        place_weights(place, gathered, weights, mixer)

    column = jnp.concatenate(
        [
            above[0, 0].astype(F32),
            d_pre[0].reshape(count, channels).astype(F32),
            below[0, 0].astype(F32),
        ],
        axis=0,
    )
    before, after = column_shifts(column, wide)
    sides = (after.astype(BF16), column.astype(BF16), before.astype(BF16))
    d_act = None
    for line in range(3):
        for side in range(3):
            window = sides[side][(2 - line) * wide : (2 - line) * wide + count]
            term = dot(window, weights[line, side * channels : (side + 1) * channels, :], NT)
            d_act = term if d_act is None else d_act + term
    _, slope = gelu_both(feat[0].reshape(count, channels).astype(F32))
    total = d_resid[0].reshape(count, channels).astype(F32) + slope * d_act
    out[0] = total.astype(BF16).reshape(height, wide, channels)


def input_call(place, feat, d_resid, d_pre, above, below, gathered):
    images, height, wide, channels = feat.shape
    strip = pl.BlockSpec((1, height, wide, channels), lambda i: (i, 0, 0, 0))
    line = pl.BlockSpec((1, 1, wide, channels), lambda i: (i, 0, 0, 0))
    return pl.pallas_call(
        input_kernel,
        grid=(images,),
        in_specs=[
            pl.BlockSpec(memory_space=pltpu.SMEM),
            strip,
            strip,
            strip,
            line,
            line,
            pl.BlockSpec(gathered.shape, lambda i: (0, 0, 0)),
        ],
        out_specs=strip,
        out_shape=jax.ShapeDtypeStruct(feat.shape, BF16),
        scratch_shapes=[
            pltpu.VMEM((3, 3 * channels, channels), BF16),
            pltpu.VMEM((channels, channels), BF16),
        ],
        compiler_params=pltpu.CompilerParams(vmem_limit_bytes=VMEM_LIMIT),
    )(place, feat, d_resid, d_pre, above, below, gathered)


BLOCK = 32


def inverse_factors(blocks):
    size = BLOCK
    lane = lax.broadcasted_iota(jnp.int32, (8, 128), 1)
    sub = lax.broadcasted_iota(jnp.int32, (8, 128), 0)
    mats = []
    for block in blocks:
        wide = jnp.concatenate([block, jnp.zeros((size, 128 - size), F32)], axis=1)
        mats.append(
            [
                wide[8 * v : 8 * v + 8] + jnp.where(lane == sub + (8 * v + size), 1.0, 0.0)
                for v in range(size // 8)
            ]
        )
    for k in range(size):
        v0, s0 = k // 8, k % 8
        for rows in mats:
            pivot = rows[v0][s0 : s0 + 1, :]
            scaled = jnp.broadcast_to(pivot * (1.0 / pivot[:, k : k + 1]), (8, 128))
            for v in range(v0, size // 8):
                if v == v0 and s0 == 7:
                    continue
                col = jnp.broadcast_to(rows[v][:, k : k + 1], (8, 128))
                if v == v0:
                    col = jnp.where(sub > s0, col, 0.0)
                rows[v] = rows[v] - col * scaled
    out = []
    for rows in mats:
        done = []
        for v in range(size // 8):
            diagonal = jnp.where(lane == sub + 8 * v, rows[v], 0.0)
            diagonal = jnp.sum(diagonal, axis=1, keepdims=True)
            done.append((rows[v] * lax.rsqrt(diagonal))[:, size : 2 * size])
        out.append(jnp.concatenate(done, axis=0))
    return out


def tile_kernel(
    turned_grad, master, first, second, left, right, basis_left, basis_right,
    master_new, first_new, second_new, left_new, right_new, basis_left_new, basis_right_new,
    work,
):
    count, tile = master.shape[:2]
    for t in range(count):
        grad_t = turned_grad[t]
        left_new[t] = BETA_TWO * left[t] + (1.0 - BETA_TWO) * dot(grad_t, grad_t, TN, HIGHEST)
        right_new[t] = BETA_TWO * right[t] + (1.0 - BETA_TWO) * dot(grad_t, grad_t, NT, HIGHEST)
        for side, (stat, basis) in enumerate(((left_new, basis_left), (right_new, basis_right))):
            moved = dot(stat[t], basis[t], NN, HIGHEST)
            work[2 * t + side, :, :tile] = dot(moved, moved, TN, HIGHEST)
            work[2 * t + side, :, tile:] = moved.T
    for t in range(count):
        turned = dot(basis_left[t], turned_grad[t], ((0,), (1,)), HIGHEST)
        turned = dot(turned, basis_right[t], NN, HIGHEST)
        mom = BETA_ONE * first[t] + (1.0 - BETA_ONE) * turned
        var = BETA_TWO * second[t] + (1.0 - BETA_TWO) * turned * turned
        first_new[t] = mom
        second_new[t] = var
        ratio = mom / (1.0 - BETA_ONE**STEP) / (jnp.sqrt(var / (1.0 - BETA_TWO**STEP)) + EPSILON)
        back = dot(dot(basis_left[t], ratio, NN, HIGHEST), basis_right[t], NT, HIGHEST)
        master_new[t] = master[t] - TILE_RATE * (back + WEIGHT_DECAY * master[t])
    for low in range(0, tile, BLOCK):
        high = low + BLOCK
        factors = inverse_factors([work[n, low:high, low:high] for n in range(2 * count)])
        for n in range(2 * count):
            panel = dot(factors[n], work[n, low:high, :], NN, HIGHEST)
            work[n, low:high, :] = panel
            if high < tile:
                work[n, high:, :] = work[n, high:, :] - dot(panel[:, high:tile], panel, TN, HIGHEST)
    for t in range(count):
        basis_left_new[t] = work[2 * t, :, tile:].T
        basis_right_new[t] = work[2 * t + 1, :, tile:].T


def tile_call(turned_grad, *arrays):
    shape = jax.ShapeDtypeStruct(turned_grad.shape, F32)
    vmem = pl.BlockSpec(memory_space=pltpu.VMEM)
    count, tile = turned_grad.shape[:2]
    return pl.pallas_call(
        tile_kernel,
        in_specs=[vmem] * 8,
        out_specs=(vmem,) * 7,
        out_shape=(shape,) * 7,
        scratch_shapes=[pltpu.VMEM((2 * count, tile, 2 * tile), F32)],
        compiler_params=pltpu.CompilerParams(vmem_limit_bytes=VMEM_LIMIT),
    )(turned_grad, *arrays)


def plain_adam(gradient, master, first, second, rate):
    first_new = BETA_ONE * first + (1.0 - BETA_ONE) * gradient
    second_new = BETA_TWO * second + (1.0 - BETA_TWO) * gradient * gradient
    ratio = (
        first_new
        / (1.0 - BETA_ONE**STEP)
        / (jnp.sqrt(second_new / (1.0 - BETA_TWO**STEP)) + EPSILON)
    )
    return (master - rate * (ratio + WEIGHT_DECAY * master), first_new, second_new)


def swap(x, axis, distance):
    count = lax.axis_size(axis)
    return lax.ppermute(x, axis, [(i, i ^ distance) for i in range(count)])


def edges(rows):
    ends = lax.axis_size("strip") - 1
    above = lax.ppermute(rows[:, -1:], "strip", [(i, i + 1) for i in range(ends)])
    below = lax.ppermute(rows[:, :1], "strip", [(i + 1, i) for i in range(ends)])
    return above, below


def gather_tiles(mine):
    core = lax.axis_index("strip") % 2
    half = mine.shape[1] // 2
    part = lax.dynamic_slice_in_dim(mine, core * half, half, axis=1)
    parts = [part] + [swap(part, "img", d) for d in range(1, lax.axis_size("img"))]
    mine_half = jnp.stack(parts)
    other_half = swap(mine_half, "strip", 1)
    low = jnp.where(core == 0, mine_half, other_half)
    high = jnp.where(core == 0, other_half, mine_half)
    whole = jnp.concatenate([low, high], axis=2)
    return whole.reshape(-1, *mine.shape[1:])


def reduce_tiles(keep, send, tiles):
    strip = lax.axis_index("strip")
    across = strip // 2
    img = lax.axis_index("img")
    groups = lax.axis_size("img")
    half = keep + swap(send, "strip", 1)
    other = lax.dynamic_index_in_dim(half, 1 - across, 0, False)
    quarter = lax.dynamic_index_in_dim(half, across, 0, False) + swap(other, "strip", 2)
    quarter = quarter.reshape(groups, tiles, *quarter.shape[1:])
    total = lax.dynamic_index_in_dim(quarter, img, 0, False).astype(F32)
    for d in range(1, groups):
        piece = lax.dynamic_index_in_dim(quarter, img ^ d, 0, False)
        total = total + swap(piece, "img", d).astype(F32)
    parts = jnp.stack([total] + [swap(total, "strip", d) for d in range(1, 4)])
    ordered = [lax.dynamic_index_in_dim(parts, strip_of ^ strip, 0, False) for strip_of in range(4)]
    return ordered


def body(
    features,
    cotangent,
    present,
    owners,
    tile_master,
    tile_mom1,
    tile_mom2,
    stat_left,
    stat_right,
    basis_left,
    basis_right,
    proj_master,
    proj_mom1,
    proj_mom2,
    dec_master,
    dec_mom1,
    dec_mom2,
    code_master,
    code_mom1,
    code_mom2,
):
    images, height, wide, channels = features.shape
    tiles = tile_master.shape[0]
    img = lax.axis_index("img")
    strip = lax.axis_index("strip")
    gathered = gather_tiles(tile_master.astype(BF16))
    place = ((owners // tiles) ^ img) * tiles + owners % tiles
    alive = lax.dynamic_slice_in_dim(present, img * images, images).astype(F32)
    count = jnp.sum(present).astype(F32) * (height * lax.axis_size("strip") * wide)
    latent = proj_master.shape[1]
    scale = LOSS_WEIGHT / (count * latent)
    code_low = code_master.astype(BF16)
    code_full = code_low.astype(F32)
    norms = jnp.sum(code_full * code_full, axis=1)[None] / SOFTMAX_WARMTH
    above, below = edges(features)
    (decoded, d_pre, d_resid, keep, send, g_proj, g_dec, g_code, totals, loss) = main_call(
        place,
        owners,
        alive,
        2.0 * scale * alive,
        (strip % 2).reshape(1),
        features,
        above,
        below,
        cotangent,
        gathered,
        proj_master.astype(BF16),
        dec_master.astype(BF16),
        code_low,
        norms,
    )
    above, below = edges(d_pre)
    small = lax.psum((g_proj, g_dec, g_code, totals, loss), ("strip", "img"))
    input_grad = input_call(place, features, d_resid, d_pre, above, below, gathered)
    ordered = reduce_tiles(keep, send, tiles)
    owned = jnp.concatenate([ordered[0], ordered[1], ordered[2], ordered[3]], axis=1)
    tile_out = tile_call(
        owned, tile_master, tile_mom1, tile_mom2, stat_left, stat_right, basis_left, basis_right
    )
    quant_loss = scale * jnp.sum(small[4])
    g_code_all = small[2].T - (2.0 / SOFTMAX_WARMTH) * small[3][0][:, None] * code_full
    proj_out = plain_adam(small[0].T, proj_master, proj_mom1, proj_mom2, PROJ_RATE)
    dec_out = plain_adam(small[1], dec_master, dec_mom1, dec_mom2, DEC_RATE)
    code_out = plain_adam(g_code_all, code_master, code_mom1, code_mom2, CODE_RATE)
    return (decoded, input_grad, quant_loss, *tile_out, *proj_out, *dec_out, *code_out)


def solution(mesh):
    big = P("img", "strip", None, None)
    tile = P("img", None, None)
    in_specs = (big, big, P(), P()) + (tile,) * 7 + (P(),) * 9
    out_specs = (big, big, P()) + (tile,) * 7 + (P(),) * 9
    return jax.shard_map(body, mesh=mesh, in_specs=in_specs, out_specs=out_specs, check_vma=False)
```

time: 752 us -> 366 us (0.49)
  other arithmetic: 262 us -> 11.9 us
  matrix products: 175 us -> 0 us
  Pallas kernels: 0 us -> 124 us
  local copies, waits for them, and re-layouts: 73.5 us -> 6.62 us
  waiting for transfers between devices: 173 us -> 124 us
  starting transfers between devices: 7.29 us -> 37.8 us
    another operation x9 -> x1, other arithmetic: 220 us -> 0.02 us  [reduce_tiles(): parts = jnp.stack([total] + [swap(total, 'strip', d) for d in range(1, 4)])]
    dot_general x51 -> x0, matrix products: 166 us -> none  [the longest x9 50.3 us: body(): jnp.einsum('nrcy,xy->nrcx', shifted, kernel[position], preferred_element_...]
    pallas_call x0 -> x3, Pallas kernels: none -> 124 us  [the longest x1 73.8 us: main_call(): pl.pallas_call(main_kernel, grid=(images,), in_specs=[smem] * 5 + [strip,...]
    reduce_scatter x1 -> x0, waiting for transfers between devices: 55.7 us -> none  [body(): owned = lax.psum_scatter(summed, 'img', scatter_dimension=0, tiled=True)]
    ppermute x4 -> x24, starting transfers between devices: 7.12 us -> 37.8 us  [the longest x20 32.6 us: swap(): return lax.ppermute(x, axis, [(i, i ^ distance) for i in range(count)])]
    all_gather x1 -> x0, waiting for transfers between devices: 29.3 us -> none  [body(): lax.all_gather(tile_master.astype(jnp.bfloat16), 'img', axis=0, tiled=True)]
    psum x2 -> x1, waiting for transfers between devices: 86.5 us -> 115 us  [body(): small = lax.psum((g_proj, g_dec, g_code, totals, loss), ('strip', 'img'))]
    convert_element_type x6 -> x2, other arithmetic: 19.4 us -> 0.63 us  [the longest x1 0.62 us: body(): dec_master.astype(BF16)]
  transfers between devices with their start and end apart: 8 -> 25, of which waited for: 4 -> 4; matrix products, arithmetic and copies ran while one was open for 9% -> 4% of each run, Pallas kernels for 0% -> 5%
where the time goes in v1:
time: 366 us; the launch traced here: 362 us
  waiting for transfers between devices  124 us (34%)
  Pallas kernels  124 us (34%)
  blocking collectives  41.3 us (11%)
  starting transfers between devices  37.8 us (10%)
  between operations  17 us (5%)
  other arithmetic  11.9 us (3%)
  local copies, waits for them, and re-layouts  6.62 us (2%)
    psum x1, waiting for transfers between devices, body(): small = lax.psum((g_proj, g_dec, g_code, totals, loss), ('strip', 'img'))  115 us
    pallas_call x1, Pallas kernels, main_call(): pl.pallas_call(main_kernel, grid=(images,), in_specs=[smem] * 5 + [strip,...  73.8 us
    psum x1, blocking collectives, body(): small = lax.psum((g_proj, g_dec, g_code, totals, loss), ('strip', 'img'))  41.3 us
    ppermute x20, starting transfers between devices, swap(): return lax.ppermute(x, axis, [(i, i ^ distance) for i in range(count)])  32.6 us
    pallas_call x1, Pallas kernels, tile_call(): pl.pallas_call(tile_kernel, in_specs=[vmem] * 8, out_specs=(vmem,) * 7, o...  30.4 us
    pallas_call x1, Pallas kernels, input_call(): pl.pallas_call(input_kernel, grid=(images,), in_specs=[pl.BlockSpec(memor...  19.4 us
    ppermute x20, waiting for transfers between devices, swap(): return lax.ppermute(x, axis, [(i, i ^ distance) for i in range(count)])  9.04 us
  transfers between devices with their start and end apart: 25, of which 4 were waited for; matrix products, arithmetic and copies ran while one was open for 4% of the time, Pallas kernels for 5%

profile of v1, /device:TPU:0, one launch (start us, length us, event | category | flops | bytes accessed | tf_op | source)
XLA Modules:
  0.0 361.7 jit_solution(736030032930054870)
XLA Ops:
  8.3 3.0 collective-permute-start.2
  11.3 1.6 collective-permute-start.3
  12.9 3.0 collective-permute-start.5
  18.3 3.7 %collective-permute-start.7 = (bf16[5,64,128]{2,1,0:T(8,128)(2,1)S(1)}, bf16[5,64,128]{2,1,0:T(8,128)(2,1)S(1)}, u32[]{:S(2)}, u32[]{:S(2)}) collective-permute-start(bf16[5,64,128]{2,1,0:T(8,128)(2,1)S(1)} %get-tuple-element.89), channel_id=1, source_target_pairs={{0,6},{1,7},{2,4},{3,5},{4,2},{5,3},{6,0},{7,1},{8,14},{9,15},{10,... | collective-permute-start | bytes 245768 | tf_op jit(solution)/shard_map/ppermute | solution.py:413
  22.1 1.3 collective-permute-start
  24.8 3.5 collective-permute-done.6
  36.8 73.8 %shard_map.339 = (bf16[20,8,32,256]{3,2,1,0:T(8,128)(2,1)}, bf16[20,8,32,256]{3,2,1,0:T(8,128)(2,1)}, bf16[20,8,32,256]{3,2,1,0:T(8,128)(2,1)}, bf16[2,40,32,128...) custom-call(s32[40]{0:T(128)} %fusion.11.place, ...), custom_call_target="tpu_custom_call" | custom-call | tf_op jit(solution)/shard_map/pallas_call | solution.py:235
  111.1 41.3 %all-reduce = (f32[1,64]{1,0:T(1,128)S(1)}, f32[1,512]{1,0:T(1,128)S(1)}) all-reduce(f32[1,64]{1,0:T(1,128)} %get-tuple-element.39, f32[1,512]{1,0:T(1,128)} %get-tuple-element.52), channel_id=1, replica_groups=mesh['strip'=4,'img'=8] {'strip','img'}, use_global_device_ids=true, to_apply=%region_2.3 | all-reduce | flops 576 | bytes 4608 | tf_op jit(solution)/shard_map/psum | solution.py:507
  153.8 2.3 collective-permute-start.13
  158.6 4.5 %collective-permute-done.13 = bf16[40,32,128]{2,1,0:T(8,128)(2,1)S(1)} collective-permute-done((bf16[40,32,128]{2,1,0:T(8,128)(2,1)S(1)}, bf16[40,32,128]{2,1,0:T(8,128)(2,1)S(1)}, u32[]{:S(2)}, u32[]{:S(2)}) %collective-permute-start.13) | collective-permute-done | bytes 327712 | tf_op jit(solution)/shard_map/ppermute | solution.py:413
  163.2 3.5 collective-permute-start.20
  166.7 1.6 collective-permute-start.19
  168.3 114.6 %all-reduce.4.cloned.1.call-done = (f32[256,64]{0,1:T(8,128)}, f32[64,256]{1,0:T(8,128)}, f32[512,64]{0,1:T(8,128)}) async-done(((f32[256,64]{0,1:T(8,128)}, f32[64,256]{1,0:T(8,128)}, f32[512,64]{0,1:T(8,128)}), (f32[256,64]{0,1:T(8,128)}, f32[64,256]{1,0:T(8,128)}, f32[512,64]{0,1:T(8,128)})) %all-reduce.4.cloned.1.call-update) | async-done | bytes 262160 | tf_op jit(solution)/shard_map/psum | solution.py:507
  282.8 1.7 multiply_subtract_fusion
  284.5 2.3 collective-permute-start.18
  286.8 1.5 collective-permute-start.17
  288.4 1.3 collective-permute-start.16
  290.4 1.5 collective-permute-start.14
  291.9 1.5 multiply_subtract_fusion.2
  296.1 2.9 collective-permute-start.23
  299.0 1.7 collective-permute-start.22
  300.7 1.5 multiply_subtract_fusion.1
  303.1 19.4 %shard_map.340 = bf16[20,8,32,256]{3,2,1,0:T(8,128)(2,1)} custom-call(s32[40]{0:T(128)} %fusion.11.place, bf16[20,8,32,256]{3,2,1,0:T(8,128)(2,1)} %feat.3, bf16[20,8,32,256]{3,2,1,0:T(8,128)(2,1)} %get-tuple-element.37.d_resid, bf16[20,8,32,256]{3,2,1,0:T(8,128)(2,1)} %get-tuple-element.38.d_pre, bf16[20,1,32,256]{3,2,1,0:T(8,128)(2,1)} %copy-done.3, ...), custom_call_target="tpu_custom_call" | custom-call | tf_op jit(solution)/shard_map/pallas_call | solution.py:288
  323.4 30.4 %shard_map.341 = (f32[5,128,128]{2,1,0:T(8,128)}, f32[5,128,128]{2,1,0:T(8,128)}, f32[5,128,128]{2,1,0:T(8,128)}, f32[5,128,128]{2,1,0:T(8,128)}, f32[5,128,128]...) custom-call(f32[5,128,128]{2,1,0:T(8,128)} %pad_maximum_fusion.2.turned_grad, f32[5,128,128]{2,1,0:T(8,128)} %master.1, ...), custom_call_target="tpu_custom_call" | custom-call | tf_op jit(solution)/shard_map/pallas_call | solution.py:390
  (95 shorter events, 21.4 us)
Async XLA Ops:
  7.2 275.6 %all-reduce.4.cloned.1.call-start = ((), (), s32[]{:S(2)}) async-start(), calls=%async_computation | async-start | bytes 524288 | tf_op jit(solution)/shard_map/psum | solution.py:507
  8.3 10.0 %collective-permute-start.2 = (bf16[5,64,128]{2,1,0:T(8,128)(2,1)S(1)}, bf16[5,64,128]{2,1,0:T(8,128)(2,1)S(1)}, u32[]{:S(2)}, u32[]{:S(2)}) collective-permute-start(bf16[5,64,128]{2,1,0:T(8,128)(2,1)S(1)} %get-tuple-element.89), channel_id=1, source_target_pairs={{0,1},{1,0},{2,3},{3,2},{4,5},{5,4},{6,7},{7,6},{8,9},{9,8},{10,11... | collective-permute-start | bytes 245768 | tf_op jit(solution)/shard_map/ppermute | solution.py:413
  11.3 10.7 %collective-permute-start.3 = (bf16[5,64,128]{2,1,0:T(8,128)(2,1)S(1)}, bf16[5,64,128]{2,1,0:T(8,128)(2,1)S(1)}, u32[]{:S(2)}, u32[]{:S(2)}) collective-permute-start(bf16[5,64,128]{2,1,0:T(8,128)(2,1)S(1)} %get-tuple-element.89), channel_id=1, source_target_pairs={{0,2},{1,3},{2,0},{3,1},{4,6},{5,7},{6,4},{7,5},{8,10},{9,11},{10,... | collective-permute-start | bytes 245768 | tf_op jit(solution)/shard_map/ppermute | solution.py:413
  12.9 9.2 %collective-permute-start.4 = (bf16[5,64,128]{2,1,0:T(8,128)(2,1)S(1)}, bf16[5,64,128]{2,1,0:T(8,128)(2,1)S(1)}, u32[]{:S(2)}, u32[]{:S(2)}) collective-permute-start(bf16[5,64,128]{2,1,0:T(8,128)(2,1)S(1)} %get-tuple-element.89), channel_id=1, source_target_pairs={{0,3},{1,2},{2,1},{3,0},{4,7},{5,6},{6,5},{7,4},{8,11},{9,10},{10,... | collective-permute-start | bytes 245768 | tf_op jit(solution)/shard_map/ppermute | solution.py:413
  12.9 10.5 %collective-permute-start.5 = (bf16[5,64,128]{2,1,0:T(8,128)(2,1)S(1)}, bf16[5,64,128]{2,1,0:T(8,128)(2,1)S(1)}, u32[]{:S(2)}, u32[]{:S(2)}) collective-permute-start(bf16[5,64,128]{2,1,0:T(8,128)(2,1)S(1)} %get-tuple-element.89), channel_id=1, source_target_pairs={{0,4},{1,5},{2,6},{3,7},{4,0},{5,1},{6,2},{7,3},{8,12},{9,13},{10,... | collective-permute-start | bytes 245768 | tf_op jit(solution)/shard_map/ppermute | solution.py:413
  15.9 12.4 %collective-permute-start.6 = (bf16[5,64,128]{2,1,0:T(8,128)(2,1)S(1)}, bf16[5,64,128]{2,1,0:T(8,128)(2,1)S(1)}, u32[]{:S(2)}, u32[]{:S(2)}) collective-permute-start(bf16[5,64,128]{2,1,0:T(8,128)(2,1)S(1)} %get-tuple-element.89), channel_id=1, source_target_pairs={{0,5},{1,4},{2,7},{3,6},{4,1},{5,0},{6,3},{7,2},{8,13},{9,12},{10,... | collective-permute-start | bytes 245768 | tf_op jit(solution)/shard_map/ppermute | solution.py:413
  18.3 10.0 %collective-permute-start.7 = (bf16[5,64,128]{2,1,0:T(8,128)(2,1)S(1)}, bf16[5,64,128]{2,1,0:T(8,128)(2,1)S(1)}, u32[]{:S(2)}, u32[]{:S(2)}) collective-permute-start(bf16[5,64,128]{2,1,0:T(8,128)(2,1)S(1)} %get-tuple-element.89), channel_id=1, source_target_pairs={{0,6},{1,7},{2,4},{3,5},{4,2},{5,3},{6,0},{7,1},{8,14},{9,15},{10,... | collective-permute-start | bytes 245768 | tf_op jit(solution)/shard_map/ppermute | solution.py:413
  22.0 7.3 %collective-permute-start.8 = (bf16[5,64,128]{2,1,0:T(8,128)(2,1)S(1)}, bf16[5,64,128]{2,1,0:T(8,128)(2,1)S(1)}, u32[]{:S(2)}, u32[]{:S(2)}) collective-permute-start(bf16[5,64,128]{2,1,0:T(8,128)(2,1)S(1)} %get-tuple-element.89), channel_id=1, source_target_pairs={{0,7},{1,6},{2,5},{3,4},{4,3},{5,2},{6,1},{7,0},{8,15},{9,14},{10,... | collective-permute-start | bytes 245768 | tf_op jit(solution)/shard_map/ppermute | solution.py:413
  22.1 13.8 %collective-permute-start = (bf16[20,1,32,256]{3,2,1,0:T(8,128)(2,1)S(1)}, bf16[20,1,32,256]{3,2,1,0:T(8,128)(2,1)S(1)}, u32[]{:S(2)}, u32[]{:S(2)}) collective-permute-start(bf16[20,1,32,256]{3,2,1,0:T(8,128)(2,1)S(1)} %get-tuple-element.95), channel_id=1, source_target_pairs={{0,8},{8,16},{16,24},{1,9},{9,17},{17,25},{2,10},{10,18},{18,26},{... | collective-permute-start | bytes 983048 | tf_op jit(solution)/shard_map/ppermute | solution.py:418
  23.5 12.5 %collective-permute-start.1 = (bf16[20,1,32,256]{3,2,1,0:T(8,128)(2,1)S(1)}, bf16[20,1,32,256]{3,2,1,0:T(8,128)(2,1)S(1)}, u32[]{:S(2)}, u32[]{:S(2)}) collective-permute-start(bf16[20,1,32,256]{3,2,1,0:T(8,128)(2,1)S(1)} %get-tuple-element.94), channel_id=1, source_target_pairs={{8,0},{16,8},{24,16},{9,1},{17,9},{25,17},{10,2},{18,10},{26,18},{... | collective-permute-start | bytes 983048 | tf_op jit(solution)/shard_map/ppermute | solution.py:419
  110.6 41.9 %collective-permute-start.12 = (bf16[2,40,32,128]{3,2,1,0:T(8,128)(2,1)}, bf16[2,40,32,128]{3,2,1,0:T(8,128)(2,1)S(1)}, u32[]{:S(2)}, u32[]{:S(2)}) collective-permute-start(bf16[2,40,32,128]{3,2,1,0:T(8,128)(2,1)} %get-tuple-element.41), channel_id=1, source_target_pairs={{0,8},{8,0},{16,24},{24,16},{1,9},{9,1},{17,25},{25,17},{2,10},{10... | collective-permute-start | bytes 1966088 | tf_op jit(solution)/shard_map/ppermute | solution.py:413
  153.8 9.3 %collective-permute-start.13 = (bf16[40,32,128]{2,1,0:T(8,128)(2,1)S(1)}, bf16[40,32,128]{2,1,0:T(8,128)(2,1)S(1)}, u32[]{:S(2)}, u32[]{:S(2)}) collective-permute-start(bf16[40,32,128]{2,1,0:T(8,128)(2,1)S(1)} %dynamic-slice_bitcast_fusion), channel_id=1, source_target_pairs={{0,16},{8,24},{16,0},{24,8},{1,17},{9,25},{17,1},{25,9},{2,18},{10... | collective-permute-start | bytes 983048 | tf_op jit(solution)/shard_map/ppermute | solution.py:413
  163.2 126.5 %collective-permute-start.20 = (bf16[5,32,128]{2,1,0:T(8,128)(2,1)S(1)}, bf16[5,32,128]{2,1,0:T(8,128)(2,1)S(1)}, u32[]{:S(2)}, u32[]{:S(2)}) collective-permute-start(bf16[5,32,128]{2,1,0:T(8,128)(2,1)S(1)} %get-tuple-element.103), channel_id=1, source_target_pairs={{0,7},{1,6},{2,5},{3,4},{4,3},{5,2},{6,1},{7,0},{8,15},{9,14},{10,... | collective-permute-start | bytes 122888 | tf_op jit(solution)/shard_map/ppermute | solution.py:413
  166.7 123.7 %collective-permute-start.19 = (bf16[5,32,128]{2,1,0:T(8,128)(2,1)S(1)}, bf16[5,32,128]{2,1,0:T(8,128)(2,1)S(1)}, u32[]{:S(2)}, u32[]{:S(2)}) collective-permute-start(bf16[5,32,128]{2,1,0:T(8,128)(2,1)S(1)} %get-tuple-element.104), channel_id=1, source_target_pairs={{0,6},{1,7},{2,4},{3,5},{4,2},{5,3},{6,0},{7,1},{8,14},{9,15},{10,... | collective-permute-start | bytes 122888 | tf_op jit(solution)/shard_map/ppermute | solution.py:413
  284.5 8.9 %collective-permute-start.18 = (bf16[5,32,128]{2,1,0:T(8,128)(2,1)S(1)}, bf16[5,32,128]{2,1,0:T(8,128)(2,1)S(1)}, u32[]{:S(2)}, u32[]{:S(2)}) collective-permute-start(bf16[5,32,128]{2,1,0:T(8,128)(2,1)S(1)} %get-tuple-element.105), channel_id=1, source_target_pairs={{0,5},{1,4},{2,7},{3,6},{4,1},{5,0},{6,3},{7,2},{8,13},{9,12},{10,... | collective-permute-start | bytes 122888 | tf_op jit(solution)/shard_map/ppermute | solution.py:413
  286.8 7.9 %collective-permute-start.17 = (bf16[5,32,128]{2,1,0:T(8,128)(2,1)S(1)}, bf16[5,32,128]{2,1,0:T(8,128)(2,1)S(1)}, u32[]{:S(2)}, u32[]{:S(2)}) collective-permute-start(bf16[5,32,128]{2,1,0:T(8,128)(2,1)S(1)} %get-tuple-element.106), channel_id=1, source_target_pairs={{0,4},{1,5},{2,6},{3,7},{4,0},{5,1},{6,2},{7,3},{8,12},{9,13},{10,... | collective-permute-start | bytes 122888 | tf_op jit(solution)/shard_map/ppermute | solution.py:413
  288.4 7.7 %collective-permute-start.16 = (bf16[5,32,128]{2,1,0:T(8,128)(2,1)S(1)}, bf16[5,32,128]{2,1,0:T(8,128)(2,1)S(1)}, u32[]{:S(2)}, u32[]{:S(2)}) collective-permute-start(bf16[5,32,128]{2,1,0:T(8,128)(2,1)S(1)} %get-tuple-element.107), channel_id=1, source_target_pairs={{0,3},{1,2},{2,1},{3,0},{4,7},{5,6},{6,5},{7,4},{8,11},{9,10},{10,... | collective-permute-start | bytes 122888 | tf_op jit(solution)/shard_map/ppermute | solution.py:413
  289.7 6.4 %collective-permute-start.15 = (bf16[5,32,128]{2,1,0:T(8,128)(2,1)S(1)}, bf16[5,32,128]{2,1,0:T(8,128)(2,1)S(1)}, u32[]{:S(2)}, u32[]{:S(2)}) collective-permute-start(bf16[5,32,128]{2,1,0:T(8,128)(2,1)S(1)} %get-tuple-element.108), channel_id=1, source_target_pairs={{0,2},{1,3},{2,0},{3,1},{4,6},{5,7},{6,4},{7,5},{8,10},{9,11},{10,... | collective-permute-start | bytes 122888 | tf_op jit(solution)/shard_map/ppermute | solution.py:413
  290.4 5.7 %collective-permute-start.14 = (bf16[5,32,128]{2,1,0:T(8,128)(2,1)S(1)}, bf16[5,32,128]{2,1,0:T(8,128)(2,1)S(1)}, u32[]{:S(2)}, u32[]{:S(2)}) collective-permute-start(bf16[5,32,128]{2,1,0:T(8,128)(2,1)S(1)} %get-tuple-element.102), channel_id=1, source_target_pairs={{0,1},{1,0},{2,3},{3,2},{4,5},{5,4},{6,7},{7,6},{8,9},{9,8},{10,11... | collective-permute-start | bytes 122888 | tf_op jit(solution)/shard_map/ppermute | solution.py:413
  293.4 8.9 %collective-permute-start.10 = (bf16[20,1,32,256]{3,2,1,0:T(8,128)(2,1)S(1)}, bf16[20,1,32,256]{3,2,1,0:T(8,128)(2,1)S(1)}, u32[]{:S(2)}, u32[]{:S(2)}) collective-permute-start(bf16[20,1,32,256]{3,2,1,0:T(8,128)(2,1)S(1)} %get-tuple-element.93), channel_id=1, source_target_pairs={{0,8},{8,16},{16,24},{1,9},{9,17},{17,25},{2,10},{10,18},{18,26},{... | collective-permute-start | bytes 983048 | tf_op jit(solution)/shard_map/ppermute | solution.py:418
  294.7 7.6 %collective-permute-start.11 = (bf16[20,1,32,256]{3,2,1,0:T(8,128)(2,1)S(1)}, bf16[20,1,32,256]{3,2,1,0:T(8,128)(2,1)S(1)}, u32[]{:S(2)}, u32[]{:S(2)}) collective-permute-start(bf16[20,1,32,256]{3,2,1,0:T(8,128)(2,1)S(1)} %get-tuple-element.92), channel_id=1, source_target_pairs={{8,0},{16,8},{24,16},{9,1},{17,9},{25,17},{10,2},{18,10},{26,18},{... | collective-permute-start | bytes 983048 | tf_op jit(solution)/shard_map/ppermute | solution.py:419
  296.1 26.4 %collective-permute-start.23 = (f32[5,32,128]{2,1,0:T(8,128)S(1)}, f32[5,32,128]{2,1,0:T(8,128)S(1)}, u32[]{:S(2)}, u32[]{:S(2)}) collective-permute-start(f32[5,32,128]{2,1,0:T(8,128)S(1)} %fusion.8), channel_id=1, source_target_pairs={{0,24},{8,16},{16,8},{24,0},{1,25},{9,17},{17,9},{25,1},{2,26},{10... | collective-permute-start | bytes 245768 | tf_op jit(solution)/shard_map/ppermute | solution.py:413
  299.0 23.5 %collective-permute-start.22 = (f32[5,32,128]{2,1,0:T(8,128)S(1)}, f32[5,32,128]{2,1,0:T(8,128)S(1)}, u32[]{:S(2)}, u32[]{:S(2)}) collective-permute-start(f32[5,32,128]{2,1,0:T(8,128)S(1)} %fusion.8), channel_id=1, source_target_pairs={{0,16},{8,24},{16,0},{24,8},{1,17},{9,25},{17,1},{25,9},{2,18},{10... | collective-permute-start | bytes 245768 | tf_op jit(solution)/shard_map/ppermute | solution.py:413
  300.7 21.9 %collective-permute-start.21 = (f32[5,32,128]{2,1,0:T(8,128)S(1)}, f32[5,32,128]{2,1,0:T(8,128)S(1)}, u32[]{:S(2)}, u32[]{:S(2)}) collective-permute-start(f32[5,32,128]{2,1,0:T(8,128)S(1)} %fusion.8), channel_id=1, source_target_pairs={{0,8},{8,0},{16,24},{24,16},{1,9},{9,1},{17,25},{25,17},{2,10},{10... | collective-permute-start | bytes 245768 | tf_op jit(solution)/shard_map/ppermute | solution.py:413
  (16 other events, 957.9 us)
Sparse Core Ops, SparseCore 0:
  157.6 125.1 all-reduce.3

commit v2 on v1

v2 whole, which is shorter than its diff:
```python
import jax
import jax.numpy as jnp
from jax import lax
from jax.experimental import pallas as pl
from jax.experimental.pallas import tpu as pltpu
from jax.sharding import PartitionSpec as P

STEP = 5
HIGHEST = lax.Precision.HIGHEST
BETA_ONE = 0.9
BETA_TWO = 0.95
EPSILON = 1e-08
WEIGHT_DECAY = 0.01
SOFTMAX_WARMTH = 4.0
LOSS_WEIGHT = 1.25
TILE_RATE = 0.05
PROJ_RATE = 0.05
DEC_RATE = 0.1
CODE_RATE = 0.3

F32 = jnp.float32
BF16 = jnp.bfloat16
NN = ((1,), (0,))
NT = ((1,), (1,))
TN = ((0,), (0,))
GELU_A = 0.7978845608028654
GELU_B = 0.044715
VMEM_LIMIT = 56 * 1024 * 1024


def dot(a, b, dims=NN, precision=None):
    return lax.dot_general(a, b, (dims, ((), ())), precision=precision, preferred_element_type=F32)


def gelu_tanh(x):
    return jnp.tanh(GELU_A * (x + GELU_B * (x * x * x)))


def gelu(x):
    return 0.5 * x * (1.0 + gelu_tanh(x))


def gelu_both(x):
    square = x * x
    t = jnp.tanh(GELU_A * x * (1.0 + GELU_B * square))
    half = 0.5 * (1.0 + t)
    slope = half + 0.5 * x * (1.0 - t * t) * (GELU_A + 3.0 * GELU_A * GELU_B * square)
    return x * half, slope


def column_shifts(rows, wide):
    count = rows.shape[0]
    column = lax.broadcasted_iota(jnp.int32, rows.shape, 0) % wide
    before = jnp.where(column == 0, 0.0, pltpu.roll(rows, 1, 0))
    after = jnp.where(column == wide - 1, 0.0, pltpu.roll(rows, count - 1, 0))
    return before, after


def place_weights(place, parts, core, put):
    half = parts[0].shape[1]
    count = len(parts) // 2
    size = parts[0].shape[0]
    for t in range(40):
        which = place[t] // size
        index = place[t] % size
        for side in range(2):
            block = parts[side * count][index]
            for n in range(1, count):
                block = jnp.where(which == n, parts[side * count + n][index], block)
            put(t, block, pl.multiple_of((core ^ side) * half, half))


def shift_lines(line, first, last):
    wide = line.shape[0]
    before = jnp.where(first, 0.0, pltpu.roll(line, 1, 0)).astype(BF16)
    after = jnp.where(last, 0.0, pltpu.roll(line, wide - 1, 0)).astype(BF16)
    return before, after


def main_kernel(batch, part_count, *refs):
    place, slots, alive_all, pull_all, core = refs[:5]
    feat, near, far, cot = refs[5:9]
    parts = refs[9 : 9 + part_count]
    proj, dec, code, norms = refs[9 + part_count : 13 + part_count]
    (decoded, d_pre_out, d_resid_out, near_out, far_out, keep, send, small) = refs[
        13 + part_count : 21 + part_count
    ]
    (weights, mixer, framed, d_pre_turned, sums, g_mixer, g_proj, g_dec, g_code, totals, loss) = refs[
        21 + part_count :
    ]
    step = pl.program_id(0)
    steps = pl.num_programs(0)
    height, wide, channels = feat.shape[1:]
    count = height * wide
    tile = parts[0].shape[2]
    half = tile // 2
    images = framed.shape[0]
    lead = core[0] == 0

    @pl.when(step == 0)
    def _():
        def put(t, block, row):
            i, j = (t // 2) % 2, t % 2
            if t < 36:
                p = t // 4
                start = (p % 3) * channels + i * tile
                weights[p // 3, pl.ds(start + row, half), j * tile : (j + 1) * tile] = block
            else:
                mixer[pl.ds(i * tile + row, half), j * tile : (j + 1) * tile] = block

        place_weights(place, parts, core[0], put)
        for ref in (g_mixer, g_proj, g_dec, g_code, totals, loss):
            ref[...] = jnp.zeros_like(ref)

    column = lax.broadcasted_iota(jnp.int32, (wide, channels), 0)
    first = column == 0
    last = column == wide - 1

    def chain(n):
        image = step * batch + n
        alive = alive_all[image]
        pull = pull_all[image]
        for r in range(height + 2):
            if r == 0:
                line = jnp.where(lead, far[n].astype(F32), near[n].astype(F32))
            elif r == height + 1:
                line = jnp.where(lead, near[n].astype(F32), far[n].astype(F32))
            else:
                line = feat[n, r - 1].astype(F32)
            line = gelu(line)
            before, after = shift_lines(line, first, last)
            rows = slice(r * wide, (r + 1) * wide)
            framed[image, rows, 0:channels] = before
            framed[image, rows, channels : 2 * channels] = line.astype(BF16)
            framed[image, rows, 2 * channels :] = after
        yield
        preact = dot(framed[image, 0:count, :], weights[0])
        preact += dot(framed[image, wide : wide + count, :], weights[1])
        preact += dot(framed[image, 2 * wide : 2 * wide + count, :], weights[2])
        yield
        inner, slope = gelu_both(preact)
        inner = inner.astype(BF16)
        yield
        feats = feat[n].reshape(count, channels).astype(F32)
        resid = (feats + dot(inner, mixer[...])).astype(BF16)
        yield
        latent = dot(resid, proj[...])
        latent_low = latent.astype(BF16)
        yield
        logits = (2.0 / SOFTMAX_WARMTH) * dot(latent_low, code[...], NT) - norms[...]
        yield
        powers = jnp.exp(logits - jnp.max(logits, axis=1, keepdims=True))
        probs = powers * (1.0 / jnp.sum(powers, axis=1, keepdims=True))
        probs_low = probs.astype(BF16)
        yield
        quant = dot(probs_low, code[...])
        quant_low = quant.astype(BF16)
        yield
        out = (dot(quant_low, dec[...]) * alive).astype(BF16)
        decoded[n] = out.reshape(height, wide, channels)
        diff = latent - quant
        loss[...] += alive * jnp.sum(diff * diff, axis=0, keepdims=True)
        back_out = (cot[n].reshape(count, channels).astype(F32) * alive).astype(BF16)
        pulled = pull * diff
        d_quant = (dot(back_out, dec[...], NT) - pulled).astype(BF16)
        g_dec[...] += dot(quant_low, back_out, TN)
        yield
        d_probs = dot(d_quant, code[...], NT)
        yield
        d_logits = probs * (d_probs - jnp.sum(probs * d_probs, axis=1, keepdims=True))
        d_logits = d_logits.astype(BF16)
        totals[...] += jnp.sum(d_logits.astype(F32), axis=0, keepdims=True)
        yield
        d_latent = ((2.0 / SOFTMAX_WARMTH) * dot(d_logits, code[...]) + pulled).astype(BF16)
        yield
        d_resid = dot(d_latent, proj[...], NT).astype(BF16)
        d_resid_out[n] = d_resid.reshape(height, wide, channels)
        g_code[...] += dot(d_quant, probs_low, TN)
        g_code[...] += (2.0 / SOFTMAX_WARMTH) * dot(latent_low, d_logits, TN)
        yield
        d_pre = (slope * dot(d_resid, mixer[...], NT)).astype(BF16)
        g_proj[...] += dot(d_latent, resid, TN)
        yield
        d_pre_out[n] = d_pre.reshape(height, wide, channels)
        top, bottom = d_pre[:wide], d_pre[count - wide :]
        near_out[n] = jnp.where(lead, bottom, top)
        far_out[n] = jnp.where(lead, top, bottom)
        g_mixer[...] += dot(d_resid, inner, TN)
        yield
        d_pre_turned[image] = d_pre.T

    live = [chain(n) for n in range(batch)]
    while live:
        live = [c for c in live if next(c, True) is None]

    @pl.when(step == steps - 1)
    def _():
        group = 4 if images % 4 == 0 else 1
        sums[...] = jnp.zeros_like(sums)
        for line in range(3):

            def add(g, carry, line=line):
                total = None
                for n in range(group):
                    i = g * group + n
                    window = framed[i, line * wide : line * wide + count, :]
                    term = dot(d_pre_turned[i], window)
                    total = term if total is None else total + term
                sums[line] += total
                return carry

            lax.fori_loop(0, images // group, add, 0)
        for ref in (keep, send):
            ref[...] = jnp.zeros_like(ref)
        quarter = tile // 4
        for t in range(40):
            i, j = (t // 2) % 2, t % 2
            if t < 36:
                p = t // 4
                left = (p % 3) * channels + i * tile
                block = sums[p // 3, j * tile : (j + 1) * tile, left : left + tile]
            else:
                block = g_mixer[j * tile : (j + 1) * tile, i * tile : (i + 1) * tile]
            block = block.astype(BF16)
            for q in range(0, 4, 2):
                even = block[q * quarter : (q + 1) * quarter]
                odd = block[(q + 1) * quarter : (q + 2) * quarter]
                keep[q // 2, slots[t]] = jnp.where(lead, even, odd)
                send[q // 2, slots[t]] = jnp.where(lead, odd, even)
        code_turned = code[...].astype(F32).T
        g_words = g_code[...] - (2.0 / SOFTMAX_WARMTH) * totals[...] * code_turned
        row = 0
        for grad in (g_proj[...], g_dec[...], g_words):
            for left in range(0, grad.shape[1], 128):
                small[row : row + grad.shape[0]] = grad[:, left : left + 128].astype(BF16)
                row += grad.shape[0]
        small[row:] = jnp.zeros((small.shape[0] - row, 128), BF16)
        small[row : row + 16, 0 : loss.shape[1]] = jnp.broadcast_to(
            loss[...] * (1.0 / 16.0), (16, loss.shape[1])
        ).astype(BF16)


def main_call(place, slots, alive, pull, core, feat, near, far, cot, parts, proj, dec, code, norms):
    images, height, wide, channels = feat.shape
    latent = proj.shape[1]
    words = code.shape[0]
    size, half, tile = parts[0].shape
    slot_count = size * len(parts) // 2
    batch = 4 if images % 4 == 0 else 1
    smem = pl.BlockSpec(memory_space=pltpu.SMEM)
    strip = pl.BlockSpec((batch, height, wide, channels), lambda i: (i, 0, 0, 0))
    line = pl.BlockSpec((batch, wide, channels), lambda i: (i, 0, 0))

    def whole(shape):
        return pl.BlockSpec(shape, lambda i: (0,) * len(shape))

    big = jax.ShapeDtypeStruct(feat.shape, BF16)
    edge = jax.ShapeDtypeStruct(near.shape, BF16)
    part = jax.ShapeDtypeStruct((2, slot_count, tile // 4, tile), BF16)
    rows = (2 * latent * channels + latent * words) // 128 + 16
    shapes = (big, big, big, edge, edge, part, part, jax.ShapeDtypeStruct((rows, 128), BF16))
    return pl.pallas_call(
        lambda *refs: main_kernel(batch, len(parts), *refs),
        grid=(images // batch,),
        in_specs=[smem] * 5
        + [strip, line, line, strip]
        + [whole(a.shape) for a in (*parts, proj, dec, code, norms)],
        out_specs=[strip] * 3 + [line] * 2 + [whole(s.shape) for s in shapes[5:]],
        out_shape=shapes,
        scratch_shapes=[
            pltpu.VMEM((3, 3 * channels, channels), BF16),
            pltpu.VMEM((channels, channels), BF16),
            pltpu.VMEM((images, (height + 2) * wide, 3 * channels), BF16),
            pltpu.VMEM((images, channels, height * wide), BF16),
            pltpu.VMEM((3, channels, 3 * channels), F32),
            pltpu.VMEM((channels, channels), F32),
            pltpu.VMEM((latent, channels), F32),
            pltpu.VMEM((latent, channels), F32),
            pltpu.VMEM((latent, words), F32),
            pltpu.VMEM((1, words), F32),
            pltpu.VMEM((1, latent), F32),
        ],
        compiler_params=pltpu.CompilerParams(vmem_limit_bytes=VMEM_LIMIT),
        name="main",
    )(place, slots, alive, pull, core, feat, near, far, cot, *parts, proj, dec, code, norms)


def input_kernel(batch, part_count, *refs):
    place, core, feat, d_resid, d_pre, near, far = refs[:7]
    parts = refs[7 : 7 + part_count]
    out, weights = refs[7 + part_count :]
    height, wide, channels = feat.shape[1:]
    count = height * wide
    tile = parts[0].shape[2]
    half = tile // 2
    lead = core[0] == 0

    @pl.when(pl.program_id(0) == 0)
    def _():
        def put(t, block, row):
            if t < 36:
                i, j = (t // 2) % 2, t % 2
                p = t // 4
                start = (2 - p % 3) * channels + i * tile
                weights[2 - p // 3, pl.ds(start + row, half), j * tile : (j + 1) * tile] = block

        place_weights(place, parts, core[0], put)

    column = lax.broadcasted_iota(jnp.int32, (wide, channels), 0)
    first = column == 0
    last = column == wide - 1
    for n in range(batch):
        lines = []
        for r in range(height + 2):
            if r == 0:
                line = jnp.where(lead, far[n], near[n])
            elif r == height + 1:
                line = jnp.where(lead, near[n], far[n])
            else:
                line = d_pre[n, r - 1]
            before, after = shift_lines(line.astype(F32), first, last)
            lines.append((before, line, after))
        sides = [jnp.concatenate([l[s] for l in lines], axis=0) for s in range(3)]
        d_act = None
        for line in range(3):
            for side in range(3):
                window = sides[side][line * wide : line * wide + count]
                term = dot(window, weights[line, side * channels : (side + 1) * channels, :], NT)
                d_act = term if d_act is None else d_act + term
        _, slope = gelu_both(feat[n].reshape(count, channels).astype(F32))
        total = d_resid[n].reshape(count, channels).astype(F32) + slope * d_act
        out[n] = total.astype(BF16).reshape(height, wide, channels)


def input_call(place, core, feat, d_resid, d_pre, near, far, parts):
    images, height, wide, channels = feat.shape
    batch = 4 if images % 4 == 0 else 1
    smem = pl.BlockSpec(memory_space=pltpu.SMEM)
    strip = pl.BlockSpec((batch, height, wide, channels), lambda i: (i, 0, 0, 0))
    line = pl.BlockSpec((batch, wide, channels), lambda i: (i, 0, 0))
    return pl.pallas_call(
        lambda *refs: input_kernel(batch, len(parts), *refs),
        grid=(images // batch,),
        in_specs=[smem, smem, strip, strip, strip, line, line]
        + [pl.BlockSpec(p.shape, lambda i: (0, 0, 0)) for p in parts],
        out_specs=strip,
        out_shape=jax.ShapeDtypeStruct(feat.shape, BF16),
        scratch_shapes=[pltpu.VMEM((3, 3 * channels, channels), BF16)],
        compiler_params=pltpu.CompilerParams(vmem_limit_bytes=VMEM_LIMIT),
        name="input_grad",
    )(place, core, feat, d_resid, d_pre, near, far, *parts)


BLOCK = 32


def inverse_factors(blocks):
    size = BLOCK
    lane = lax.broadcasted_iota(jnp.int32, (8, 128), 1)
    sub = lax.broadcasted_iota(jnp.int32, (8, 128), 0)
    mats = []
    for block in blocks:
        wide = jnp.concatenate([block, jnp.zeros((size, 128 - size), F32)], axis=1)
        mats.append(
            [
                wide[8 * v : 8 * v + 8] + jnp.where(lane == sub + (8 * v + size), 1.0, 0.0)
                for v in range(size // 8)
            ]
        )
    for k in range(size):
        v0, s0 = k // 8, k % 8
        for rows in mats:
            pivot = rows[v0][s0 : s0 + 1, :]
            scaled = jnp.broadcast_to(pivot * (1.0 / pivot[:, k : k + 1]), (8, 128))
            for v in range(v0, size // 8):
                if v == v0 and s0 == 7:
                    continue
                col = jnp.broadcast_to(rows[v][:, k : k + 1], (8, 128))
                if v == v0:
                    col = jnp.where(sub > s0, col, 0.0)
                rows[v] = rows[v] - col * scaled
    out = []
    for rows in mats:
        done = []
        for v in range(size // 8):
            diagonal = jnp.where(lane == sub + 8 * v, rows[v], 0.0)
            diagonal = jnp.sum(diagonal, axis=1, keepdims=True)
            done.append((rows[v] * lax.rsqrt(diagonal))[:, size : 2 * size])
        out.append(jnp.concatenate(done, axis=0))
    return out


def tile_kernel(
    turned_grad, master, first, second, left, right, basis_left, basis_right,
    master_new, first_new, second_new, left_new, right_new, basis_left_new, basis_right_new,
    work,
):
    count, tile = master.shape[:2]
    for t in range(count):
        grad_t = turned_grad[t]
        left_new[t] = BETA_TWO * left[t] + (1.0 - BETA_TWO) * dot(grad_t, grad_t, TN, HIGHEST)
        right_new[t] = BETA_TWO * right[t] + (1.0 - BETA_TWO) * dot(grad_t, grad_t, NT, HIGHEST)
        for side, (stat, basis) in enumerate(((left_new, basis_left), (right_new, basis_right))):
            moved = dot(stat[t], basis[t], NN, HIGHEST)
            work[2 * t + side, :, :tile] = dot(moved, moved, TN, HIGHEST)
            work[2 * t + side, :, tile:] = moved.T
    for t in range(count):
        turned = dot(basis_left[t], turned_grad[t], ((0,), (1,)), HIGHEST)
        turned = dot(turned, basis_right[t], NN, HIGHEST)
        mom = BETA_ONE * first[t] + (1.0 - BETA_ONE) * turned
        var = BETA_TWO * second[t] + (1.0 - BETA_TWO) * turned * turned
        first_new[t] = mom
        second_new[t] = var
        ratio = mom / (1.0 - BETA_ONE**STEP) / (jnp.sqrt(var / (1.0 - BETA_TWO**STEP)) + EPSILON)
        back = dot(dot(basis_left[t], ratio, NN, HIGHEST), basis_right[t], NT, HIGHEST)
        master_new[t] = master[t] - TILE_RATE * (back + WEIGHT_DECAY * master[t])
    for low in range(0, tile, BLOCK):
        high = low + BLOCK
        factors = inverse_factors([work[n, low:high, low:high] for n in range(2 * count)])
        for n in range(2 * count):
            panel = dot(factors[n], work[n, low:high, :], NN, HIGHEST)
            work[n, low:high, :] = panel
            if high < tile:
                work[n, high:, :] = work[n, high:, :] - dot(panel[:, high:tile], panel, TN, HIGHEST)
    for t in range(count):
        basis_left_new[t] = work[2 * t, :, tile:].T
        basis_right_new[t] = work[2 * t + 1, :, tile:].T


def tile_call(turned_grad, *arrays):
    shape = jax.ShapeDtypeStruct(turned_grad.shape, F32)
    vmem = pl.BlockSpec(memory_space=pltpu.VMEM)
    count, tile = turned_grad.shape[:2]
    return pl.pallas_call(
        tile_kernel,
        in_specs=[vmem] * 8,
        out_specs=(vmem,) * 7,
        out_shape=(shape,) * 7,
        scratch_shapes=[pltpu.VMEM((2 * count, tile, 2 * tile), F32)],
        compiler_params=pltpu.CompilerParams(vmem_limit_bytes=VMEM_LIMIT),
    )(turned_grad, *arrays)


def plain_adam(gradient, master, first, second, rate):
    first_new = BETA_ONE * first + (1.0 - BETA_ONE) * gradient
    second_new = BETA_TWO * second + (1.0 - BETA_TWO) * gradient * gradient
    ratio = (
        first_new
        / (1.0 - BETA_ONE**STEP)
        / (jnp.sqrt(second_new / (1.0 - BETA_TWO**STEP)) + EPSILON)
    )
    return (master - rate * (ratio + WEIGHT_DECAY * master), first_new, second_new)


def small_kernel(scale, one, two, *refs):
    arrays, outs = refs[:9], refs[9:]
    total = one[...].astype(F32) + two[...].astype(F32)
    row = 0
    for n, (rate, turned) in enumerate(((PROJ_RATE, True), (DEC_RATE, False), (CODE_RATE, True))):
        shape = arrays[3 * n].shape
        rows, columns = shape[::-1] if turned else shape
        pieces = []
        for _ in range(columns // 128):
            piece = total[row : row + rows]
            pieces.append(piece.T if turned else piece)
            row += rows
        grad = jnp.concatenate(pieces, axis=0 if turned else 1)
        new = plain_adam(grad, *(a[...] for a in arrays[3 * n : 3 * n + 3]), rate)
        for out, value in zip(outs[3 * n : 3 * n + 3], new):
            out[...] = value
    outs[9][...] = jnp.sum(total[row:], axis=(0, 1), keepdims=True) * scale[0]


def small_call(scale, one, two, arrays):
    smem = pl.BlockSpec(memory_space=pltpu.SMEM)
    vmem = pl.BlockSpec(memory_space=pltpu.VMEM)
    shapes = [jax.ShapeDtypeStruct(a.shape, F32) for a in arrays]
    shapes.append(jax.ShapeDtypeStruct((1, 1), F32))
    return pl.pallas_call(
        small_kernel,
        in_specs=[smem] + [vmem] * 11,
        out_specs=[vmem] * 10,
        out_shape=shapes,
        compiler_params=pltpu.CompilerParams(vmem_limit_bytes=VMEM_LIMIT),
        name="small_adam",
    )(scale, one, two, *arrays)


def swap(x, axis, distance):
    count = lax.axis_size(axis)
    return lax.ppermute(x, axis, [(i, i ^ distance) for i in range(count)])


def radices(count):
    out = []
    stride = 1
    while stride < count:
        left = (count // stride).bit_length() - 1
        radix = 2 if left % 2 else 4
        out.append((radix, stride))
        stride *= radix
    return out


def swap_edges(near, far):
    return swap(near, "strip", 1), lax.ppermute(far, "strip", [(1, 2), (2, 1)])


def gather_tiles(mine):
    core = lax.axis_index("strip") % 2
    half = mine.shape[1] // 2
    part = lax.dynamic_slice_in_dim(mine, core * half, half, axis=1)
    steps = radices(lax.axis_size("img"))[::-1]
    for number, (radix, stride) in enumerate(steps):
        parts = [part] + [swap(part, "img", d * stride) for d in range(1, radix)]
        if number < len(steps) - 1:
            part = jnp.concatenate(parts, axis=0)
    return parts + [swap(p, "strip", 1) for p in parts]


def tile_place(owners, tiles):
    distance = (owners // tiles) ^ lax.axis_index("img")
    place = jnp.zeros_like(owners)
    size = 1
    for radix, stride in radices(lax.axis_size("img"))[::-1]:
        place = place + size * ((distance // stride) % radix)
        size *= radix
    return place * tiles + owners % tiles


def reduce_tiles(keep, send, tiles):
    strip = lax.axis_index("strip")
    across = strip // 2
    img = lax.axis_index("img")
    groups = lax.axis_size("img")
    half = keep + swap(send, "strip", 1)
    other = lax.dynamic_index_in_dim(half, 1 - across, 0, False)
    part = lax.dynamic_index_in_dim(half, across, 0, False) + swap(other, "strip", 2)
    left = groups
    for radix, stride in radices(groups):
        part = part.reshape(left // radix, radix, -1, *part.shape[-2:])
        low = (img // stride) % radix
        total = lax.dynamic_index_in_dim(part, low, 1, False).astype(F32)
        for d in range(1, radix):
            piece = lax.dynamic_index_in_dim(part, low ^ d, 1, False)
            total = total + swap(piece, "img", d * stride).astype(F32)
        part = total.astype(BF16)
        left //= radix
    total = total.reshape(tiles, *total.shape[-2:])
    parts = jnp.stack([total] + [swap(total, "strip", d) for d in range(1, 4)])
    ordered = [lax.dynamic_index_in_dim(parts, n ^ strip, 0, False) for n in range(4)]
    return jnp.concatenate(ordered, axis=1)


def reduce_small(small):
    steps = [("strip", 1), ("strip", 2)]
    for radix, stride in radices(lax.axis_size("img")):
        steps += [("img", stride << n) for n in range(radix.bit_length() - 1)]
    for number, (axis, distance) in enumerate(steps):
        other = swap(small, axis, distance)
        if number == len(steps) - 1:
            return small, other
        small = (small.astype(F32) + other.astype(F32)).astype(BF16)


def body(
    features,
    cotangent,
    present,
    owners,
    tile_master,
    tile_mom1,
    tile_mom2,
    stat_left,
    stat_right,
    basis_left,
    basis_right,
    proj_master,
    proj_mom1,
    proj_mom2,
    dec_master,
    dec_mom1,
    dec_mom2,
    code_master,
    code_mom1,
    code_mom2,
):
    images, height, wide, channels = features.shape
    tiles = tile_master.shape[0]
    img = lax.axis_index("img")
    strip = lax.axis_index("strip")
    core = strip % 2
    parts = gather_tiles(tile_master.astype(BF16))
    place = tile_place(owners, tiles)
    alive = lax.dynamic_slice_in_dim(present, img * images, images).astype(F32)
    count = jnp.sum(present).astype(F32) * (height * lax.axis_size("strip") * wide)
    latent = proj_master.shape[1]
    scale = LOSS_WEIGHT / (count * latent)
    code_low = code_master.astype(BF16)
    code_full = code_low.astype(F32)
    norms = jnp.sum(code_full * code_full, axis=1)[None] / SOFTMAX_WARMTH
    top, bottom = features[:, 0], features[:, height - 1]
    near, far = swap_edges(jnp.where(core == 0, bottom, top), jnp.where(core == 0, top, bottom))
    (decoded, d_pre, d_resid, near_out, far_out, keep, send, small) = main_call(
        place,
        owners,
        alive,
        2.0 * scale * alive,
        core.reshape(1),
        features,
        near,
        far,
        cotangent,
        parts,
        proj_master.astype(BF16),
        dec_master.astype(BF16),
        code_low,
        norms,
    )
    near, far = swap_edges(near_out, far_out)
    one, two = reduce_small(small)
    input_grad = input_call(place, core.reshape(1), features, d_resid, d_pre, near, far, parts)
    owned = reduce_tiles(keep, send, tiles)
    tile_out = tile_call(
        owned, tile_master, tile_mom1, tile_mom2, stat_left, stat_right, basis_left, basis_right
    )
    small_out = small_call(
        scale.reshape(1),
        one,
        two,
        [
            proj_master,
            proj_mom1,
            proj_mom2,
            dec_master,
            dec_mom1,
            dec_mom2,
            code_master,
            code_mom1,
            code_mom2,
        ],
    )
    return (decoded, input_grad, small_out[9].reshape(()), *tile_out, *small_out[:9])


def solution(mesh):
    big = P("img", "strip", None, None)
    tile = P("img", None, None)
    in_specs = (big, big, P(), P()) + (tile,) * 7 + (P(),) * 9
    out_specs = (big, big, P()) + (tile,) * 7 + (P(),) * 9
    return jax.shard_map(body, mesh=mesh, in_specs=in_specs, out_specs=out_specs, check_vma=False)
```

time: 366 us -> 162 us (0.44)
  waiting for transfers between devices: 124 us -> 22.4 us
  blocking collectives: 41.3 us -> 0 us
  Pallas kernels: 124 us -> 85.9 us
  starting transfers between devices: 37.8 us -> 21.3 us
  between operations: 17 us -> 1.69 us
  local copies, waits for them, and re-layouts: 6.62 us -> 18.9 us
    psum x1 -> x0, waiting for transfers between devices: 115 us -> none  [body(): small = lax.psum((g_proj, g_dec, g_code, totals, loss), ('strip', 'img'))]
    psum x1 -> x0, blocking collectives: 41.3 us -> none  [body(): small = lax.psum((g_proj, g_dec, g_code, totals, loss), ('strip', 'img'))]
    pallas_call x2 -> x3, Pallas kernels: 93.2 us -> 55.5 us  [the longest x1 39.6 us: main_call(): pl.pallas_call(lambda *refs: main_kernel(batch, len(parts), *refs), grid=...]
    unnamed x37 -> x48, local copies, waits for them, and re-layouts: 2.76 us -> 17.1 us
    ppermute x20 -> x22, waiting for transfers between devices: 9.04 us -> 22.4 us  [swap(): return lax.ppermute(x, axis, [(i, i ^ distance) for i in range(count)])]
    ppermute x20 -> x22, starting transfers between devices: 32.6 us -> 19.8 us  [swap(): return lax.ppermute(x, axis, [(i, i ^ distance) for i in range(count)])]
    sub x3 -> x0, other arithmetic: 4.78 us -> none  [plain_adam(): master - rate * (ratio + WEIGHT_DECAY * master)]
    ppermute x4 -> x2, starting transfers between devices: 5.19 us -> 1.53 us  [swap_edges(): lax.ppermute(far, 'strip', [(1, 2), (2, 1)])]
  transfers between devices with their start and end apart: 25 -> 24, of which waited for: 4 -> 9; matrix products, arithmetic and copies ran while one was open for 4% -> 16% of each run, Pallas kernels for 5% -> 10%
where the time goes in v2:
time: 162 us; the launch traced here: 161 us
  Pallas kernels  85.9 us (53%)
  waiting for transfers between devices  22.4 us (14%)
  starting transfers between devices  21.3 us (13%)
  local copies, waits for them, and re-layouts  18.9 us (12%)
  other arithmetic  11 us (7%)
  between operations  1.69 us (1%)
    pallas_call x1, Pallas kernels, main_call(): pl.pallas_call(lambda *refs: main_kernel(batch, len(parts), *refs), grid=...  39.6 us
    pallas_call x1, Pallas kernels, tile_call(): pl.pallas_call(tile_kernel, in_specs=[vmem] * 8, out_specs=(vmem,) * 7, o...  30.4 us
    ppermute x22, waiting for transfers between devices, swap(): return lax.ppermute(x, axis, [(i, i ^ distance) for i in range(count)])  22.4 us
    ppermute x22, starting transfers between devices, swap(): return lax.ppermute(x, axis, [(i, i ^ distance) for i in range(count)])  19.8 us
    unnamed x48, local copies, waits for them, and re-layouts  17.1 us
    pallas_call x1, Pallas kernels, input_call(): pl.pallas_call(lambda *refs: input_kernel(batch, len(parts), *refs), grid...  13.1 us
  transfers between devices with their start and end apart: 24, of which 9 were waited for; matrix products, arithmetic and copies ran while one was open for 16% of the time, Pallas kernels for 10%

profile of v2, /device:TPU:0, one launch (start us, length us, event | category | flops | bytes accessed | tf_op | source)
XLA Modules:
  0.0 161.2 jit_solution(7476496516310734328)
XLA Ops:
  1.6 5.1 %collective-permute-start.4 = (bf16[5,64,128]{2,1,0:T(8,128)(2,1)S(1)}, bf16[5,64,128]{2,1,0:T(8,128)(2,1)S(1)}, u32[]{:S(2)}, u32[]{:S(2)}) collective-permute-start(bf16[5,64,128]{2,1,0:T(8,128)(2,1)S(1)} %dynamic-slice_convert_fusion), channel_id=1, source_target_pairs={{0,6},{1,7},{2,4},{3,5},{4,2},{5,3},{6,0},{7,1},{8,14},{9,15},{10,... | collective-permute-start | bytes 245768 | tf_op jit(solution)/shard_map/ppermute | solution.py:491
  9.8 3.8 %collective-permute-done.3 = bf16[5,64,128]{2,1,0:T(8,128)(2,1)S(1)} collective-permute-done((bf16[5,64,128]{2,1,0:T(8,128)(2,1)S(1)}, bf16[5,64,128]{2,1,0:T(8,128)(2,1)S(1)}, u32[]{:S(2)}, u32[]{:S(2)}) %collective-permute-start.3) | collective-permute-done | bytes 81952 | tf_op jit(solution)/shard_map/ppermute | solution.py:491
  13.7 1.6 collective-permute-start.5
  20.0 1.5 convert_element_type.87.refs_14_
  26.1 39.6 %main.1 = (bf16[20,8,32,256]{3,2,1,0:T(8,128)(2,1)}, bf16[20,8,32,256]{3,2,1,0:T(8,128)(2,1)}, bf16[20,8,32,256]{3,2,1,0:T(8,128)(2,1)}, bf16[20,32,256]{2,1,0:T...) custom-call(s32[40]{0:T(128)} %fusion.4.refs_0_, ...), custom_call_target="tpu_custom_call" | custom-call | tf_op jit(solution)/shard_map/main/pallas_call | solution.py:262
  66.3 2.0 %collective-permute-done.10 = bf16[528,128]{1,0:T(8,128)(2,1)S(1)} collective-permute-done((bf16[528,128]{1,0:T(8,128)(2,1)}, bf16[528,128]{1,0:T(8,128)(2,1)S(1)}, u32[]{:S(2)}, u32[]{:S(2)}) %collective-permute-start.10) | collective-permute-done | bytes 135200 | tf_op jit(solution)/shard_map/ppermute | solution.py:491
  69.2 1.5 collective-permute-start.11
  73.6 1.5 collective-permute-done.11
  76.1 5.9 %collective-permute-done.16 = bf16[40,32,128]{2,1,0:T(8,128)(2,1)S(1)} collective-permute-done((bf16[40,32,128]{2,1,0:T(8,128)(2,1)S(1)}, bf16[40,32,128]{2,1,0:T(8,128)(2,1)S(1)}, u32[]{:S(2)}, u32[]{:S(2)}) %collective-permute-start.16) | collective-permute-done | bytes 327712 | tf_op jit(solution)/shard_map/ppermute | solution.py:491
  83.6 3.9 %collective-permute-done.17 = bf16[4,5,32,128]{3,2,1,0:T(8,128)(2,1)S(1)} collective-permute-done((bf16[4,5,32,128]{3,2,1,0:T(8,128)(2,1)S(1)}, bf16[4,5,32,128]{3,2,1,0:T(8,128)(2,1)S(1)}, u32[]{:S(2)}, u32[]{:S(2)}) %collective-permute-start.17) | collective-permute-done | bytes 163872 | tf_op jit(solution)/shard_map/ppermute | solution.py:491
  87.5 2.7 %collective-permute-start.20 = (bf16[1,5,32,128]{3,2,1,0:T(8,128)(2,1)S(1)}, bf16[1,5,32,128]{3,2,1,0:T(8,128)(2,1)S(1)}, u32[]{:S(2)}, u32[]{:S(2)}) collective-permute-start(bf16[1,5,32,128]{3,2,1,0:T(8,128)(2,1)S(1)} %get-tuple-element.137), channel_id=1, source_target_pairs={{0,6},{1,7},{2,4},{3,5},{4,2},{5,3},{6,0},{7,1},{8,14},{9,15},{10,... | collective-permute-start | bytes 122888 | tf_op jit(solution)/shard_map/ppermute | solution.py:491
  90.3 1.7 %collective-permute-start.18 = (bf16[1,5,32,128]{3,2,1,0:T(8,128)(2,1)S(1)}, bf16[1,5,32,128]{3,2,1,0:T(8,128)(2,1)S(1)}, u32[]{:S(2)}, u32[]{:S(2)}) collective-permute-start(bf16[1,5,32,128]{3,2,1,0:T(8,128)(2,1)S(1)} %get-tuple-element.136), channel_id=1, source_target_pairs={{0,2},{1,3},{2,0},{3,1},{4,6},{5,7},{6,4},{7,5},{8,10},{9,11},{10,... | collective-permute-start | bytes 122888 | tf_op jit(solution)/shard_map/ppermute | solution.py:491
  92.0 1.6 collective-permute-done.20
  93.6 2.8 %collective-permute-done.19 = bf16[1,5,32,128]{3,2,1,0:T(8,128)(2,1)S(1)} collective-permute-done((bf16[1,5,32,128]{3,2,1,0:T(8,128)(2,1)S(1)}, bf16[1,5,32,128]{3,2,1,0:T(8,128)(2,1)S(1)}, u32[]{:S(2)}, u32[]{:S(2)}) %collective-permute-start.19) | collective-permute-done | bytes 40992 | tf_op jit(solution)/shard_map/ppermute | solution.py:491
  96.5 2.1 %collective-permute-start.22 = (f32[5,32,128]{2,1,0:T(8,128)S(1)}, f32[5,32,128]{2,1,0:T(8,128)S(1)}, u32[]{:S(2)}, u32[]{:S(2)}) collective-permute-start(f32[5,32,128]{2,1,0:T(8,128)S(1)} %bitcast.43), channel_id=1, source_target_pairs={{0,16},{8,24},{16,0},{24,8},{1,17},{9,25},{17,1},{25,9},{2,18},{10... | collective-permute-start | bytes 245768 | tf_op jit(solution)/shard_map/ppermute | solution.py:491
  103.5 13.1 %input_grad.1 = bf16[20,8,32,256]{3,2,1,0:T(8,128)(2,1)} custom-call(s32[40]{0:T(128)} %fusion.4.refs_0_, s32[1]{0:T(128)} %bitcast.refs_4_.refs_1_, bf16[20,8,32,256]{3,2,1,0:T(8,128)(2,1)} %refs_2_.2, bf16[20,8,32,256]{3,2,1,0:T(8,128)(2,1)} %get-tuple-element.45.refs_3_, bf16[20,8,32,256]{3,2,1,0:T(8,128)(2,1)} %get-tuple-element.46.refs_4_, ...), custom_call_target="tpu_custom_call" | custom-call | tf_op jit(solution)/shard_map/input_grad/pallas_call | solution.py:341
  117.2 2.8 %small_adam.1 = (f32[256,64]{1,0:T(8,128)}, f32[256,64]{1,0:T(8,128)}, f32[256,64]{1,0:T(8,128)}, f32[64,256]{1,0:T(8,128)}, f32[64,256]{1,0:T(8,128)}, /*index=...) custom-call(f32[1]{0:T(128)} %bitcast.4.scale, ...), custom_call_target="tpu_custom_call" | custom-call | tf_op jit(solution)/shard_map/small_adam/pallas_call | solution.py:479
  120.0 1.6 %copy.81 = f32[256,64]{0,1:T(8,128)} copy(f32[256,64]{1,0:T(8,128)} %get-tuple-element.117) | data formatting | bytes 131072
  121.6 1.6 %copy.82 = f32[256,64]{0,1:T(8,128)} copy(f32[256,64]{1,0:T(8,128)} %get-tuple-element.118) | data formatting | bytes 131072
  123.2 1.6 %copy.83 = f32[256,64]{0,1:T(8,128)} copy(f32[256,64]{1,0:T(8,128)} %get-tuple-element.119) | data formatting | bytes 131072
  124.8 1.7 %copy.84 = f32[512,64]{0,1:T(8,128)} copy(f32[512,64]{1,0:T(8,128)} %get-tuple-element.123) | data formatting | bytes 262144
  126.6 1.7 %copy.85 = f32[512,64]{0,1:T(8,128)} copy(f32[512,64]{1,0:T(8,128)} %get-tuple-element.124) | data formatting | bytes 262144
  128.3 1.7 %copy.86 = f32[512,64]{0,1:T(8,128)} copy(f32[512,64]{1,0:T(8,128)} %get-tuple-element.125) | data formatting | bytes 262144
  130.8 30.4 %shard_map.339 = (f32[5,128,128]{2,1,0:T(8,128)}, f32[5,128,128]{2,1,0:T(8,128)}, f32[5,128,128]{2,1,0:T(8,128)}, f32[5,128,128]{2,1,0:T(8,128)}, f32[5,128,128]...) custom-call(f32[5,128,128]{2,1,0:T(8,128)} %pad_maximum_fusion.2.turned_grad, f32[5,128,128]{2,1,0:T(8,128)} %master.1, ...), custom_call_target="tpu_custom_call" | custom-call | tf_op jit(solution)/shard_map/pallas_call | solution.py:434
  (101 shorter events, 25.9 us)
Async XLA Ops:
  1.6 8.1 %collective-permute-start.4 = (bf16[5,64,128]{2,1,0:T(8,128)(2,1)S(1)}, bf16[5,64,128]{2,1,0:T(8,128)(2,1)S(1)}, u32[]{:S(2)}, u32[]{:S(2)}) collective-permute-start(bf16[5,64,128]{2,1,0:T(8,128)(2,1)S(1)} %dynamic-slice_convert_fusion), channel_id=1, source_target_pairs={{0,6},{1,7},{2,4},{3,5},{4,2},{5,3},{6,0},{7,1},{8,14},{9,15},{10,... | collective-permute-start | bytes 245768 | tf_op jit(solution)/shard_map/ppermute | solution.py:491
  6.7 6.9 %collective-permute-start.3 = (bf16[5,64,128]{2,1,0:T(8,128)(2,1)S(1)}, bf16[5,64,128]{2,1,0:T(8,128)(2,1)S(1)}, u32[]{:S(2)}, u32[]{:S(2)}) collective-permute-start(bf16[5,64,128]{2,1,0:T(8,128)(2,1)S(1)} %dynamic-slice_convert_fusion), channel_id=1, source_target_pairs={{0,4},{1,5},{2,6},{3,7},{4,0},{5,1},{6,2},{7,3},{8,12},{9,13},{10,... | collective-permute-start | bytes 245768 | tf_op jit(solution)/shard_map/ppermute | solution.py:491
  6.7 6.9 %collective-permute-start.2 = (bf16[5,64,128]{2,1,0:T(8,128)(2,1)S(1)}, bf16[5,64,128]{2,1,0:T(8,128)(2,1)S(1)}, u32[]{:S(2)}, u32[]{:S(2)}) collective-permute-start(bf16[5,64,128]{2,1,0:T(8,128)(2,1)S(1)} %dynamic-slice_convert_fusion), channel_id=1, source_target_pairs={{0,2},{1,3},{2,0},{3,1},{4,6},{5,7},{6,4},{7,5},{8,10},{9,11},{10,... | collective-permute-start | bytes 245768 | tf_op jit(solution)/shard_map/ppermute | solution.py:491
  8.5 16.4 %collective-permute-start = (bf16[20,32,256]{2,1,0:T(8,128)(2,1)S(1)}, bf16[20,32,256]{2,1,0:T(8,128)(2,1)S(1)}, u32[]{:S(2)}, u32[]{:S(2)}) collective-permute-start(bf16[20,32,256]{2,1,0:T(8,128)(2,1)S(1)} %get-tuple-element.131), channel_id=1, source_target_pairs={{0,8},{8,0},{16,24},{24,16},{1,9},{9,1},{17,25},{25,17},{2,10},{10... | collective-permute-start | bytes 983048 | tf_op jit(solution)/shard_map/ppermute | solution.py:491
  8.6 16.3 %collective-permute-start.1 = (bf16[20,32,256]{2,1,0:T(8,128)(2,1)S(1)}, bf16[20,32,256]{2,1,0:T(8,128)(2,1)S(1)}, u32[]{:S(2)}, u32[]{:S(2)}) collective-permute-start(bf16[20,32,256]{2,1,0:T(8,128)(2,1)S(1)} %get-tuple-element.130), channel_id=1, source_target_pairs={{8,16},{16,8},{9,17},{17,9},{10,18},{18,10},{11,19},{19,11},{12,20... | collective-permute-start | bytes 983048 | tf_op jit(solution)/shard_map/ppermute | solution.py:506
  13.7 9.6 %collective-permute-start.5 = (bf16[20,64,128]{2,1,0:T(8,128)(2,1)S(1)}, bf16[20,64,128]{2,1,0:T(8,128)(2,1)S(1)}, u32[]{:S(2)}, u32[]{:S(2)}) collective-permute-start(bf16[20,64,128]{2,1,0:T(8,128)(2,1)S(1)} %pad_maximum_fusion.refs_9_.refs_7_), channel_id=1, source_target_pairs={{0,1},{1,0},{2,3},{3,2},{4,5},{5,4},{6,7},{7,6},{8,9},{9,8},{10,11... | collective-permute-start | bytes 983048 | tf_op jit(solution)/shard_map/ppermute | solution.py:491
  23.2 1.7 %collective-permute-start.6 = (bf16[20,64,128]{2,1,0:T(8,128)(2,1)S(1)}, bf16[20,64,128]{2,1,0:T(8,128)(2,1)S(1)}, u32[]{:S(2)}, u32[]{:S(2)}) collective-permute-start(bf16[20,64,128]{2,1,0:T(8,128)(2,1)S(1)} %pad_maximum_fusion.refs_9_.refs_7_), channel_id=1, source_target_pairs={{0,8},{8,0},{16,24},{24,16},{1,9},{9,1},{17,25},{25,17},{2,10},{10... | collective-permute-start | bytes 983048 | tf_op jit(solution)/shard_map/ppermute | solution.py:491
  23.2 2.1 %collective-permute-start.7 = (bf16[20,64,128]{2,1,0:T(8,128)(2,1)S(1)}, bf16[20,64,128]{2,1,0:T(8,128)(2,1)S(1)}, u32[]{:S(2)}, u32[]{:S(2)}) collective-permute-start(bf16[20,64,128]{2,1,0:T(8,128)(2,1)S(1)} %collective-permute-done.5.refs_10_.refs_8_), channel_id=1, source_target_pairs={{0,8},{8,0},{16,24},{24,16},{1,9},{9,1},{17,25},{25,17},{2,10},{10... | collective-permute-start | bytes 983048 | tf_op jit(solution)/shard_map/ppermute | solution.py:491
  65.7 5.1 %collective-permute-start.15 = (bf16[2,40,32,128]{3,2,1,0:T(8,128)(2,1)}, bf16[2,40,32,128]{3,2,1,0:T(8,128)(2,1)S(1)}, u32[]{:S(2)}, u32[]{:S(2)}) collective-permute-start(bf16[2,40,32,128]{3,2,1,0:T(8,128)(2,1)} %get-tuple-element.52), channel_id=1, source_target_pairs={{0,8},{8,0},{16,24},{24,16},{1,9},{9,1},{17,25},{25,17},{2,10},{10... | collective-permute-start | bytes 1966088 | tf_op jit(solution)/shard_map/ppermute | solution.py:491
  65.9 2.4 %collective-permute-start.10 = (bf16[528,128]{1,0:T(8,128)(2,1)}, bf16[528,128]{1,0:T(8,128)(2,1)S(1)}, u32[]{:S(2)}, u32[]{:S(2)}) collective-permute-start(bf16[528,128]{1,0:T(8,128)(2,1)} %get-tuple-element.49), channel_id=1, source_target_pairs={{0,8},{8,0},{16,24},{24,16},{1,9},{9,1},{17,25},{25,17},{2,10},{10... | collective-permute-start | bytes 405512 | tf_op jit(solution)/shard_map/ppermute | solution.py:491
  69.2 5.9 %collective-permute-start.11 = (bf16[528,128]{1,0:T(8,128)(2,1)S(1)}, bf16[528,128]{1,0:T(8,128)(2,1)S(1)}, u32[]{:S(2)}, u32[]{:S(2)}) collective-permute-start(bf16[528,128]{1,0:T(8,128)(2,1)S(1)} %add_convert_fusion.3), channel_id=1, source_target_pairs={{0,16},{8,24},{16,0},{24,8},{1,17},{9,25},{17,1},{25,9},{2,18},{10... | collective-permute-start | bytes 405512 | tf_op jit(solution)/shard_map/ppermute | solution.py:491
  72.1 9.8 %collective-permute-start.16 = (bf16[40,32,128]{2,1,0:T(8,128)(2,1)S(1)}, bf16[40,32,128]{2,1,0:T(8,128)(2,1)S(1)}, u32[]{:S(2)}, u32[]{:S(2)}) collective-permute-start(bf16[40,32,128]{2,1,0:T(8,128)(2,1)S(1)} %dynamic-slice_bitcast_fusion), channel_id=1, source_target_pairs={{0,16},{8,24},{16,0},{24,8},{1,17},{9,25},{17,1},{25,9},{2,18},{10... | collective-permute-start | bytes 983048 | tf_op jit(solution)/shard_map/ppermute | solution.py:491
  72.8 25.9 %collective-permute-start.8 = (bf16[20,32,256]{2,1,0:T(8,128)(2,1)}, bf16[20,32,256]{2,1,0:T(8,128)(2,1)S(1)}, u32[]{:S(2)}, u32[]{:S(2)}) collective-permute-start(bf16[20,32,256]{2,1,0:T(8,128)(2,1)} %get-tuple-element.47), channel_id=1, source_target_pairs={{0,8},{8,0},{16,24},{24,16},{1,9},{9,1},{17,25},{25,17},{2,10},{10... | collective-permute-start | bytes 983048 | tf_op jit(solution)/shard_map/ppermute | solution.py:491
  72.8 30.0 %collective-permute-start.9 = (bf16[20,32,256]{2,1,0:T(8,128)(2,1)S(1)}, bf16[20,32,256]{2,1,0:T(8,128)(2,1)S(1)}, u32[]{:S(2)}, u32[]{:S(2)}) collective-permute-start(bf16[20,32,256]{2,1,0:T(8,128)(2,1)S(1)} %copy-done.17), channel_id=1, source_target_pairs={{8,16},{16,8},{9,17},{17,9},{10,18},{18,10},{11,19},{19,11},{12,20... | collective-permute-start | bytes 983048 | tf_op jit(solution)/shard_map/ppermute | solution.py:506
  75.2 7.8 %collective-permute-start.12 = (bf16[528,128]{1,0:T(8,128)(2,1)S(1)}, bf16[528,128]{1,0:T(8,128)(2,1)S(1)}, u32[]{:S(2)}, u32[]{:S(2)}) collective-permute-start(bf16[528,128]{1,0:T(8,128)(2,1)S(1)} %add_convert_fusion.2), channel_id=1, source_target_pairs={{0,1},{1,0},{2,3},{3,2},{4,5},{5,4},{6,7},{7,6},{8,9},{9,8},{10,11... | collective-permute-start | bytes 405512 | tf_op jit(solution)/shard_map/ppermute | solution.py:491
  82.0 5.4 %collective-permute-start.17 = (bf16[4,5,32,128]{3,2,1,0:T(8,128)(2,1)S(1)}, bf16[4,5,32,128]{3,2,1,0:T(8,128)(2,1)S(1)}, u32[]{:S(2)}, u32[]{:S(2)}) collective-permute-start(bf16[4,5,32,128]{3,2,1,0:T(8,128)(2,1)S(1)} %dynamic-slice_bitcast_fusion.1), channel_id=1, source_target_pairs={{0,1},{1,0},{2,3},{3,2},{4,5},{5,4},{6,7},{7,6},{8,9},{9,8},{10,11... | collective-permute-start | bytes 491528 | tf_op jit(solution)/shard_map/ppermute | solution.py:491
  83.0 7.3 %collective-permute-start.13 = (bf16[528,128]{1,0:T(8,128)(2,1)S(1)}, bf16[528,128]{1,0:T(8,128)(2,1)S(1)}, u32[]{:S(2)}, u32[]{:S(2)}) collective-permute-start(bf16[528,128]{1,0:T(8,128)(2,1)S(1)} %add_convert_fusion.1), channel_id=1, source_target_pairs={{0,2},{1,3},{2,0},{3,1},{4,6},{5,7},{6,4},{7,5},{8,10},{9,11},{10,... | collective-permute-start | bytes 405512 | tf_op jit(solution)/shard_map/ppermute | solution.py:491
  87.5 6.1 %collective-permute-start.20 = (bf16[1,5,32,128]{3,2,1,0:T(8,128)(2,1)S(1)}, bf16[1,5,32,128]{3,2,1,0:T(8,128)(2,1)S(1)}, u32[]{:S(2)}, u32[]{:S(2)}) collective-permute-start(bf16[1,5,32,128]{3,2,1,0:T(8,128)(2,1)S(1)} %get-tuple-element.137), channel_id=1, source_target_pairs={{0,6},{1,7},{2,4},{3,5},{4,2},{5,3},{6,0},{7,1},{8,14},{9,15},{10,... | collective-permute-start | bytes 122888 | tf_op jit(solution)/shard_map/ppermute | solution.py:491
  90.2 6.2 %collective-permute-start.19 = (bf16[1,5,32,128]{3,2,1,0:T(8,128)(2,1)S(1)}, bf16[1,5,32,128]{3,2,1,0:T(8,128)(2,1)S(1)}, u32[]{:S(2)}, u32[]{:S(2)}) collective-permute-start(bf16[1,5,32,128]{3,2,1,0:T(8,128)(2,1)S(1)} %get-tuple-element.138), channel_id=1, source_target_pairs={{0,4},{1,5},{2,6},{3,7},{4,0},{5,1},{6,2},{7,3},{8,12},{9,13},{10,... | collective-permute-start | bytes 122888 | tf_op jit(solution)/shard_map/ppermute | solution.py:491
  90.3 6.2 %collective-permute-start.18 = (bf16[1,5,32,128]{3,2,1,0:T(8,128)(2,1)S(1)}, bf16[1,5,32,128]{3,2,1,0:T(8,128)(2,1)S(1)}, u32[]{:S(2)}, u32[]{:S(2)}) collective-permute-start(bf16[1,5,32,128]{3,2,1,0:T(8,128)(2,1)S(1)} %get-tuple-element.136), channel_id=1, source_target_pairs={{0,2},{1,3},{2,0},{3,1},{4,6},{5,7},{6,4},{7,5},{8,10},{9,11},{10,... | collective-permute-start | bytes 122888 | tf_op jit(solution)/shard_map/ppermute | solution.py:491
  93.6 23.0 %collective-permute-start.14 = (bf16[528,128]{1,0:T(8,128)(2,1)S(1)}, bf16[528,128]{1,0:T(8,128)(2,1)S(1)}, u32[]{:S(2)}, u32[]{:S(2)}) collective-permute-start(bf16[528,128]{1,0:T(8,128)(2,1)S(1)} %add_convert_fusion.one), channel_id=1, source_target_pairs={{0,4},{1,5},{2,6},{3,7},{4,0},{5,1},{6,2},{7,3},{8,12},{9,13},{10,... | collective-permute-start | bytes 405512 | tf_op jit(solution)/shard_map/ppermute | solution.py:491
  96.5 33.5 %collective-permute-start.23 = (f32[5,32,128]{2,1,0:T(8,128)S(1)}, f32[5,32,128]{2,1,0:T(8,128)S(1)}, u32[]{:S(2)}, u32[]{:S(2)}) collective-permute-start(f32[5,32,128]{2,1,0:T(8,128)S(1)} %bitcast.42), channel_id=1, source_target_pairs={{0,24},{8,16},{16,8},{24,0},{1,25},{9,17},{17,9},{25,1},{2,26},{10... | collective-permute-start | bytes 245768 | tf_op jit(solution)/shard_map/ppermute | solution.py:491
  96.5 33.5 %collective-permute-start.22 = (f32[5,32,128]{2,1,0:T(8,128)S(1)}, f32[5,32,128]{2,1,0:T(8,128)S(1)}, u32[]{:S(2)}, u32[]{:S(2)}) collective-permute-start(f32[5,32,128]{2,1,0:T(8,128)S(1)} %bitcast.43), channel_id=1, source_target_pairs={{0,16},{8,24},{16,0},{24,8},{1,17},{9,25},{17,1},{25,9},{2,18},{10... | collective-permute-start | bytes 245768 | tf_op jit(solution)/shard_map/ppermute | solution.py:491
  98.7 31.3 %collective-permute-start.21 = (f32[5,32,128]{2,1,0:T(8,128)S(1)}, f32[5,32,128]{2,1,0:T(8,128)S(1)}, u32[]{:S(2)}, u32[]{:S(2)}) collective-permute-start(f32[5,32,128]{2,1,0:T(8,128)S(1)} %bitcast.44), channel_id=1, source_target_pairs={{0,8},{8,0},{16,24},{24,16},{1,9},{9,1},{17,25},{25,17},{2,10},{10... | collective-permute-start | bytes 245768 | tf_op jit(solution)/shard_map/ppermute | solution.py:491
  (18 other events, 261.5 us)

commit v3 on v2

--- a/solution.py
+++ b/solution.py
@@ -6,7 +6,6 @@
 from jax.sharding import PartitionSpec as P
 
 STEP = 5
-HIGHEST = lax.Precision.HIGHEST
 BETA_ONE = 0.9
 BETA_TWO = 0.95
 EPSILON = 1e-08
@@ -28,8 +27,8 @@
 VMEM_LIMIT = 56 * 1024 * 1024
 
 
-def dot(a, b, dims=NN, precision=None):
-    return lax.dot_general(a, b, (dims, ((), ())), precision=precision, preferred_element_type=F32)
+def dot(a, b, dims=NN):
+    return lax.dot_general(a, b, (dims, ((), ())), preferred_element_type=F32)
 
 
 def gelu_tanh(x):
@@ -144,16 +143,16 @@
         feats = feat[n].reshape(count, channels).astype(F32)
         resid = (feats + dot(inner, mixer[...])).astype(BF16)
         yield
-        latent = dot(resid, proj[...])
+        latent = dot(resid, proj[...], NT)
         latent_low = latent.astype(BF16)
         yield
-        logits = (2.0 / SOFTMAX_WARMTH) * dot(latent_low, code[...], NT) - norms[...]
+        logits = (2.0 / SOFTMAX_WARMTH) * dot(latent_low, code[...]) - norms[...]
         yield
         powers = jnp.exp(logits - jnp.max(logits, axis=1, keepdims=True))
         probs = powers * (1.0 / jnp.sum(powers, axis=1, keepdims=True))
         probs_low = probs.astype(BF16)
         yield
-        quant = dot(probs_low, code[...])
+        quant = dot(probs_low, code[...], NT)
         quant_low = quant.astype(BF16)
         yield
         out = (dot(quant_low, dec[...]) * alive).astype(BF16)
@@ -165,15 +164,15 @@
         d_quant = (dot(back_out, dec[...], NT) - pulled).astype(BF16)
         g_dec[...] += dot(quant_low, back_out, TN)
         yield
-        d_probs = dot(d_quant, code[...], NT)
+        d_probs = dot(d_quant, code[...])
         yield
         d_logits = probs * (d_probs - jnp.sum(probs * d_probs, axis=1, keepdims=True))
         d_logits = d_logits.astype(BF16)
         totals[...] += jnp.sum(d_logits.astype(F32), axis=0, keepdims=True)
         yield
-        d_latent = ((2.0 / SOFTMAX_WARMTH) * dot(d_logits, code[...]) + pulled).astype(BF16)
-        yield
-        d_resid = dot(d_latent, proj[...], NT).astype(BF16)
+        d_latent = ((2.0 / SOFTMAX_WARMTH) * dot(d_logits, code[...], NT) + pulled).astype(BF16)
+        yield
+        d_resid = dot(d_latent, proj[...]).astype(BF16)
         d_resid_out[n] = d_resid.reshape(height, wide, channels)
         g_code[...] += dot(d_quant, probs_low, TN)
         g_code[...] += (2.0 / SOFTMAX_WARMTH) * dot(latent_low, d_logits, TN)
@@ -195,21 +194,12 @@
 
     @pl.when(step == steps - 1)
     def _():
-        group = 4 if images % 4 == 0 else 1
-        sums[...] = jnp.zeros_like(sums)
         for line in range(3):
-
-            def add(g, carry, line=line):
-                total = None
-                for n in range(group):
-                    i = g * group + n
-                    window = framed[i, line * wide : line * wide + count, :]
-                    term = dot(d_pre_turned[i], window)
-                    total = term if total is None else total + term
-                sums[line] += total
-                return carry
-
-            lax.fori_loop(0, images // group, add, 0)
+            total = None
+            for n in range(images):
+                term = dot(d_pre_turned[n], framed[n, line * wide : line * wide + count, :])
+                total = term if total is None else total + term
+            sums[line] = total
         for ref in (keep, send):
             ref[...] = jnp.zeros_like(ref)
         quarter = tile // 4
@@ -227,8 +217,7 @@
                 odd = block[(q + 1) * quarter : (q + 2) * quarter]
                 keep[q // 2, slots[t]] = jnp.where(lead, even, odd)
                 send[q // 2, slots[t]] = jnp.where(lead, odd, even)
-        code_turned = code[...].astype(F32).T
-        g_words = g_code[...] - (2.0 / SOFTMAX_WARMTH) * totals[...] * code_turned
+        g_words = g_code[...] - (2.0 / SOFTMAX_WARMTH) * totals[...] * code[...].astype(F32)
         row = 0
         for grad in (g_proj[...], g_dec[...], g_words):
             for left in range(0, grad.shape[1], 128):
@@ -242,11 +231,10 @@
 
 def main_call(place, slots, alive, pull, core, feat, near, far, cot, parts, proj, dec, code, norms):
     images, height, wide, channels = feat.shape
-    latent = proj.shape[1]
-    words = code.shape[0]
+    latent, words = code.shape
     size, half, tile = parts[0].shape
     slot_count = size * len(parts) // 2
-    batch = 4 if images % 4 == 0 else 1
+    batch = 5 if images % 5 == 0 else 1
     smem = pl.BlockSpec(memory_space=pltpu.SMEM)
     strip = pl.BlockSpec((batch, height, wide, channels), lambda i: (i, 0, 0, 0))
     line = pl.BlockSpec((batch, wide, channels), lambda i: (i, 0, 0))
@@ -334,7 +322,7 @@
 
 def input_call(place, core, feat, d_resid, d_pre, near, far, parts):
     images, height, wide, channels = feat.shape
-    batch = 4 if images % 4 == 0 else 1
+    batch = 5 if images % 5 == 0 else 1
     smem = pl.BlockSpec(memory_space=pltpu.SMEM)
     strip = pl.BlockSpec((batch, height, wide, channels), lambda i: (i, 0, 0, 0))
     line = pl.BlockSpec((batch, wide, channels), lambda i: (i, 0, 0))
@@ -352,93 +340,181 @@
 
 
 BLOCK = 32
-
-
-def inverse_factors(blocks):
-    size = BLOCK
+RANK = 4
+
+
+def split3(x):
+    high = x.astype(BF16)
+    rest = x - high.astype(F32)
+    middle = rest.astype(BF16)
+    return high, middle, (rest - middle.astype(F32)).astype(BF16)
+
+
+def dot_exact(a, b, dims=NN):
+    left = jnp.concatenate([a[n] for n in (0, 0, 1, 1, 0, 2)], axis=dims[0][0])
+    right = jnp.concatenate([b[n] for n in (0, 1, 0, 1, 2, 0)], axis=dims[1][0])
+    return dot(left, right, dims)
+
+
+def inverse_factors(pairs):
+    half = 64
     lane = lax.broadcasted_iota(jnp.int32, (8, 128), 1)
     sub = lax.broadcasted_iota(jnp.int32, (8, 128), 0)
+    base = jnp.where(lane >= half, half, 0)
+    inner = lane - base
+    count = BLOCK // 8
+
+    def pick(x, k):
+        return jnp.take_along_axis(x, base + k, axis=1)
+
     mats = []
-    for block in blocks:
-        wide = jnp.concatenate([block, jnp.zeros((size, 128 - size), F32)], axis=1)
+    for one, two in pairs:
+        zero = jnp.zeros((BLOCK, half - BLOCK), F32)
+        wide = jnp.concatenate([one, zero, two, zero], axis=1)
         mats.append(
             [
-                wide[8 * v : 8 * v + 8] + jnp.where(lane == sub + (8 * v + size), 1.0, 0.0)
-                for v in range(size // 8)
+                wide[8 * v : 8 * v + 8] + jnp.where(inner == sub + (8 * v + BLOCK), 1.0, 0.0)
+                for v in range(count)
             ]
         )
-    for k in range(size):
-        v0, s0 = k // 8, k % 8
+    for start in range(0, BLOCK, RANK):
+        v0, s0 = start // 8, start % 8
         for rows in mats:
-            pivot = rows[v0][s0 : s0 + 1, :]
-            scaled = jnp.broadcast_to(pivot * (1.0 / pivot[:, k : k + 1]), (8, 128))
-            for v in range(v0, size // 8):
-                if v == v0 and s0 == 7:
-                    continue
-                col = jnp.broadcast_to(rows[v][:, k : k + 1], (8, 128))
+            pivots = [jnp.broadcast_to(rows[v0][s0 + i : s0 + i + 1], (8, 128)) for i in range(RANK)]
+            columns = [pick(rows[v0], start + j) for j in range(RANK)]
+            core = {
+                (i, j): jnp.broadcast_to(columns[j][s0 + i : s0 + i + 1], (8, 128))
+                for i in range(RANK)
+                for j in range(i, RANK)
+            }
+            lower = {}
+            scaled = []
+            for i in range(RANK):
+                root = lax.rsqrt(core[i, i])
+                for j in range(i + 1, RANK):
+                    lower[j, i] = core[i, j] * (root * root)
+                for j in range(i + 1, RANK):
+                    for k in range(j, RANK):
+                        core[j, k] = core[j, k] - lower[j, i] * core[i, k]
+                    pivots[j] = pivots[j] - lower[j, i] * pivots[i]
+                scaled.append((root, pivots[i] * root))
+            if start + RANK < BLOCK:
+                solved = [None] * RANK
+                for i in range(RANK - 1, -1, -1):
+                    solved[i] = scaled[i][1] * scaled[i][0]
+                    for j in range(i + 1, RANK):
+                        solved[i] = solved[i] - lower[j, i] * solved[j]
+            for v in range(v0, count):
+                new = rows[v]
+                if v > v0 or s0 + RANK < 8:
+                    for j in range(RANK):
+                        column = columns[j] if v == v0 else pick(rows[v], start + j)
+                        new = new - column * solved[j]
                 if v == v0:
-                    col = jnp.where(sub > s0, col, 0.0)
-                rows[v] = rows[v] - col * scaled
-    out = []
-    for rows in mats:
-        done = []
-        for v in range(size // 8):
-            diagonal = jnp.where(lane == sub + 8 * v, rows[v], 0.0)
-            diagonal = jnp.sum(diagonal, axis=1, keepdims=True)
-            done.append((rows[v] * lax.rsqrt(diagonal))[:, size : 2 * size])
-        out.append(jnp.concatenate(done, axis=0))
-    return out
-
-
-def tile_kernel(
-    turned_grad, master, first, second, left, right, basis_left, basis_right,
-    master_new, first_new, second_new, left_new, right_new, basis_left_new, basis_right_new,
-    work,
-):
+                    if s0 > 0:
+                        new = jnp.where(sub < s0, rows[v], new)
+                    for i in range(RANK):
+                        new = jnp.where(sub == s0 + i, scaled[i][1], new)
+                rows[v] = new
+    return [jnp.concatenate(rows, axis=0) for rows in mats]
+
+
+def small_update(scale, one, two, arrays, outs):
+    total = one[...].astype(F32) + two[...].astype(F32)
+    row = 0
+    for n, rate in enumerate((PROJ_RATE, DEC_RATE, CODE_RATE)):
+        rows, columns = arrays[3 * n].shape
+        pieces = []
+        for _ in range(columns // 128):
+            pieces.append(total[row : row + rows])
+            row += rows
+        grad = jnp.concatenate(pieces, axis=1)
+        new = plain_adam(grad, *(a[...] for a in arrays[3 * n : 3 * n + 3]), rate)
+        for out, value in zip(outs[3 * n : 3 * n + 3], new):
+            out[...] = value
+    outs[9][...] = jnp.sum(total[row:], axis=(0, 1), keepdims=True) * scale[0]
+
+
+def tile_kernel(*refs):
+    strip, scale = refs[:2]
+    quarters = refs[2:6]
+    master, first, second, left, right, basis_left, basis_right = refs[6:13]
+    one, two = refs[13:15]
+    small_arrays = refs[15:24]
+    (master_new, first_new, second_new, left_new, right_new, basis_left_new, basis_right_new) = refs[
+        24:31
+    ]
+    small_outs = refs[31:41]
+    work, grad_turned = refs[41:]
     count, tile = master.shape[:2]
+    for d in range(4):
+        quarter = tile // 4
+        row = pl.multiple_of((strip[0] ^ d) * quarter, quarter)
+        grad_turned[:, pl.ds(row, quarter), :] = quarters[d][...]
     for t in range(count):
-        grad_t = turned_grad[t]
-        left_new[t] = BETA_TWO * left[t] + (1.0 - BETA_TWO) * dot(grad_t, grad_t, TN, HIGHEST)
-        right_new[t] = BETA_TWO * right[t] + (1.0 - BETA_TWO) * dot(grad_t, grad_t, NT, HIGHEST)
+        grad = grad_turned[t]
+        left_new[t] = BETA_TWO * left[t] + (1.0 - BETA_TWO) * dot(grad, grad, TN)
+        right_new[t] = BETA_TWO * right[t] + (1.0 - BETA_TWO) * dot(grad, grad, NT)
         for side, (stat, basis) in enumerate(((left_new, basis_left), (right_new, basis_right))):
-            moved = dot(stat[t], basis[t], NN, HIGHEST)
-            work[2 * t + side, :, :tile] = dot(moved, moved, TN, HIGHEST)
-            work[2 * t + side, :, tile:] = moved.T
+            moved = dot_exact(split3(stat[t]), split3(basis[t]))
+            turned = moved.T
+            work[2 * t + side, :, :tile] = dot_exact(split3(turned), split3(moved))
+            work[2 * t + side, :, tile:] = turned
     for t in range(count):
-        turned = dot(basis_left[t], turned_grad[t], ((0,), (1,)), HIGHEST)
-        turned = dot(turned, basis_right[t], NN, HIGHEST)
+        one_low = basis_left[t].astype(BF16)
+        two_low = basis_right[t].astype(BF16)
+        turned = dot(one_low, grad_turned[t], ((0,), (1,)))
+        turned = dot(turned.astype(BF16), two_low)
         mom = BETA_ONE * first[t] + (1.0 - BETA_ONE) * turned
         var = BETA_TWO * second[t] + (1.0 - BETA_TWO) * turned * turned
         first_new[t] = mom
         second_new[t] = var
         ratio = mom / (1.0 - BETA_ONE**STEP) / (jnp.sqrt(var / (1.0 - BETA_TWO**STEP)) + EPSILON)
-        back = dot(dot(basis_left[t], ratio, NN, HIGHEST), basis_right[t], NT, HIGHEST)
+        back = dot(dot(one_low, ratio.astype(BF16)).astype(BF16), two_low, NT)
         master_new[t] = master[t] - TILE_RATE * (back + WEIGHT_DECAY * master[t])
+    small_update(scale, one, two, small_arrays, small_outs)
     for low in range(0, tile, BLOCK):
         high = low + BLOCK
-        factors = inverse_factors([work[n, low:high, low:high] for n in range(2 * count)])
+        factors = inverse_factors(
+            [
+                (work[2 * t, low:high, low:high], work[2 * t + 1, low:high, low:high])
+                for t in range(count)
+            ]
+        )
         for n in range(2 * count):
-            panel = dot(factors[n], work[n, low:high, :], NN, HIGHEST)
-            work[n, low:high, :] = panel
+            start = (n % 2) * 64 + BLOCK
+            factor = split3(factors[n // 2][:, start : start + BLOCK])
+            panel = dot_exact(factor, split3(work[n, low:high, :]))
+            work[n, low:high, tile:] = panel[:, tile:]
             if high < tile:
-                work[n, high:, :] = work[n, high:, :] - dot(panel[:, high:tile], panel, TN, HIGHEST)
+                panel = split3(panel)
+                work[n, high:, :] = work[n, high:, :] - dot_exact(
+                    [p[:, high:tile] for p in panel], panel, TN
+                )
     for t in range(count):
         basis_left_new[t] = work[2 * t, :, tile:].T
         basis_right_new[t] = work[2 * t + 1, :, tile:].T
 
 
-def tile_call(turned_grad, *arrays):
-    shape = jax.ShapeDtypeStruct(turned_grad.shape, F32)
+def tile_call(strip, scale, quarters, arrays, one, two, small_arrays):
+    shape = jax.ShapeDtypeStruct(arrays[0].shape, F32)
+    smem = pl.BlockSpec(memory_space=pltpu.SMEM)
     vmem = pl.BlockSpec(memory_space=pltpu.VMEM)
-    count, tile = turned_grad.shape[:2]
+    count, tile = shape.shape[:2]
+    shapes = [shape] * 7 + [jax.ShapeDtypeStruct(a.shape, F32) for a in small_arrays]
+    shapes.append(jax.ShapeDtypeStruct((1, 1), F32))
     return pl.pallas_call(
         tile_kernel,
-        in_specs=[vmem] * 8,
-        out_specs=(vmem,) * 7,
-        out_shape=(shape,) * 7,
-        scratch_shapes=[pltpu.VMEM((2 * count, tile, 2 * tile), F32)],
+        in_specs=[smem] * 2 + [vmem] * 22,
+        out_specs=[vmem] * 17,
+        out_shape=shapes,
+        scratch_shapes=[
+            pltpu.VMEM((2 * count, tile, 2 * tile), F32),
+            pltpu.VMEM((count, tile, tile), BF16),
+        ],
         compiler_params=pltpu.CompilerParams(vmem_limit_bytes=VMEM_LIMIT),
-    )(turned_grad, *arrays)
+        name="tile_adam",
+    )(strip, scale, *quarters, *arrays, one, two, *small_arrays)
 
 
 def plain_adam(gradient, master, first, second, rate):
@@ -450,40 +526,6 @@
         / (jnp.sqrt(second_new / (1.0 - BETA_TWO**STEP)) + EPSILON)
     )
     return (master - rate * (ratio + WEIGHT_DECAY * master), first_new, second_new)
-
-
-def small_kernel(scale, one, two, *refs):
-    arrays, outs = refs[:9], refs[9:]
-    total = one[...].astype(F32) + two[...].astype(F32)
-    row = 0
-    for n, (rate, turned) in enumerate(((PROJ_RATE, True), (DEC_RATE, False), (CODE_RATE, True))):
-        shape = arrays[3 * n].shape
-        rows, columns = shape[::-1] if turned else shape
-        pieces = []
-        for _ in range(columns // 128):
-            piece = total[row : row + rows]
-            pieces.append(piece.T if turned else piece)
-            row += rows
-        grad = jnp.concatenate(pieces, axis=0 if turned else 1)
-        new = plain_adam(grad, *(a[...] for a in arrays[3 * n : 3 * n + 3]), rate)
-        for out, value in zip(outs[3 * n : 3 * n + 3], new):
-            out[...] = value
-    outs[9][...] = jnp.sum(total[row:], axis=(0, 1), keepdims=True) * scale[0]
-
-
-def small_call(scale, one, two, arrays):
-    smem = pl.BlockSpec(memory_space=pltpu.SMEM)
-    vmem = pl.BlockSpec(memory_space=pltpu.VMEM)
-    shapes = [jax.ShapeDtypeStruct(a.shape, F32) for a in arrays]
-    shapes.append(jax.ShapeDtypeStruct((1, 1), F32))
-    return pl.pallas_call(
-        small_kernel,
-        in_specs=[smem] + [vmem] * 11,
-        out_specs=[vmem] * 10,
-        out_shape=shapes,
-        compiler_params=pltpu.CompilerParams(vmem_limit_bytes=VMEM_LIMIT),
-        name="small_adam",
-    )(scale, one, two, *arrays)
 
 
 def swap(x, axis, distance):
@@ -533,23 +575,35 @@
     across = strip // 2
     img = lax.axis_index("img")
     groups = lax.axis_size("img")
-    half = keep + swap(send, "strip", 1)
-    other = lax.dynamic_index_in_dim(half, 1 - across, 0, False)
-    part = lax.dynamic_index_in_dim(half, across, 0, False) + swap(other, "strip", 2)
-    left = groups
-    for radix, stride in radices(groups):
-        part = part.reshape(left // radix, radix, -1, *part.shape[-2:])
+    (radix, _), *later = radices(groups)
+    part = keep + swap(send, "strip", 1)
+    part = part.reshape(2, groups // radix, radix, -1, part.shape[-1])
+    low = img % radix
+    total = None
+    for d in range(2):
+        for e in range(radix):
+            piece = lax.dynamic_index_in_dim(part, across ^ d, 0, False)
+            piece = lax.dynamic_index_in_dim(piece, low ^ e, 1, False)
+            if d or e:
+                pairs = [
+                    (a * groups + b, (a ^ (2 * d)) * groups + (b ^ e))
+                    for a in range(4)
+                    for b in range(groups)
+                ]
+                piece = lax.ppermute(piece, ("strip", "img"), pairs)
+            piece = piece.astype(F32)
+            total = piece if total is None else total + piece
+    left = groups // radix
+    for radix, stride in later:
+        part = total.astype(BF16).reshape(left // radix, radix, *total.shape[-2:])
         low = (img // stride) % radix
         total = lax.dynamic_index_in_dim(part, low, 1, False).astype(F32)
         for d in range(1, radix):
             piece = lax.dynamic_index_in_dim(part, low ^ d, 1, False)
             total = total + swap(piece, "img", d * stride).astype(F32)
-        part = total.astype(BF16)
         left //= radix
-    total = total.reshape(tiles, *total.shape[-2:])
-    parts = jnp.stack([total] + [swap(total, "strip", d) for d in range(1, 4)])
-    ordered = [lax.dynamic_index_in_dim(parts, n ^ strip, 0, False) for n in range(4)]
-    return jnp.concatenate(ordered, axis=1)
+    total = total.astype(BF16).reshape(tiles, -1, total.shape[-1])
+    return [total] + [swap(total, "strip", d) for d in range(1, 4)]
 
 
 def reduce_small(small):
@@ -596,9 +650,9 @@
     count = jnp.sum(present).astype(F32) * (height * lax.axis_size("strip") * wide)
     latent = proj_master.shape[1]
     scale = LOSS_WEIGHT / (count * latent)
-    code_low = code_master.astype(BF16)
+    code_low = code_master.T.astype(BF16)
     code_full = code_low.astype(F32)
-    norms = jnp.sum(code_full * code_full, axis=1)[None] / SOFTMAX_WARMTH
+    norms = jnp.sum(code_full * code_full, axis=0)[None] / SOFTMAX_WARMTH
     top, bottom = features[:, 0], features[:, height - 1]
     near, far = swap_edges(jnp.where(core == 0, bottom, top), jnp.where(core == 0, top, bottom))
     (decoded, d_pre, d_resid, near_out, far_out, keep, send, small) = main_call(
@@ -612,7 +666,7 @@
         far,
         cotangent,
         parts,
-        proj_master.astype(BF16),
+        proj_master.T.astype(BF16),
         dec_master.astype(BF16),
         code_low,
         norms,
@@ -620,27 +674,28 @@
     near, far = swap_edges(near_out, far_out)
     one, two = reduce_small(small)
     input_grad = input_call(place, core.reshape(1), features, d_resid, d_pre, near, far, parts)
-    owned = reduce_tiles(keep, send, tiles)
-    tile_out = tile_call(
-        owned, tile_master, tile_mom1, tile_mom2, stat_left, stat_right, basis_left, basis_right
-    )
-    small_out = small_call(
+    quarters = reduce_tiles(keep, send, tiles)
+    out = tile_call(
+        strip.reshape(1),
         scale.reshape(1),
+        quarters,
+        [tile_master, tile_mom1, tile_mom2, stat_left, stat_right, basis_left, basis_right],
         one,
         two,
         [
-            proj_master,
-            proj_mom1,
-            proj_mom2,
+            proj_master.T,
+            proj_mom1.T,
+            proj_mom2.T,
             dec_master,
             dec_mom1,
             dec_mom2,
-            code_master,
-            code_mom1,
-            code_mom2,
+            code_master.T,
+            code_mom1.T,
+            code_mom2.T,
         ],
     )
-    return (decoded, input_grad, small_out[9].reshape(()), *tile_out, *small_out[:9])
+    small = [a.T for a in out[7:10]] + list(out[10:13]) + [a.T for a in out[13:16]]
+    return (decoded, input_grad, out[16].reshape(()), *out[:7], *small)
 
 
 def solution(mesh):

time: 162 us -> 133 us (0.82)
  Pallas kernels: 85.9 us -> 65.2 us
  local copies, waits for them, and re-layouts: 18.9 us -> 3.36 us
  starting transfers between devices: 21.3 us -> 28.2 us
    pallas_call x2 -> x1, Pallas kernels: 33.1 us -> 15.5 us  [tile_call(): pl.pallas_call(tile_kernel, in_specs=[smem] * 2 + [vmem] * 22, out_specs=...]
    unnamed x48 -> x28, local copies, waits for them, and re-layouts: 17.1 us -> 2.35 us
    ppermute x22 -> x20, waiting for transfers between devices: 22.4 us -> 13.5 us  [swap(): return lax.ppermute(x, axis, [(i, i ^ distance) for i in range(count)])]
    ppermute x0 -> x3, waiting for transfers between devices: none -> 7.75 us  [reduce_tiles(): piece = lax.ppermute(piece, ('strip', 'img'), pairs)]
    ppermute x0 -> x3, starting transfers between devices: none -> 4.89 us  [reduce_tiles(): piece = lax.ppermute(piece, ('strip', 'img'), pairs)]
    pallas_call x1, Pallas kernels: 39.6 us -> 36.9 us  [main_call(): pl.pallas_call(lambda *refs: main_kernel(batch, len(parts), *refs), grid=...]
    ppermute x22 -> x20, starting transfers between devices: 19.8 us -> 22 us  [swap(): return lax.ppermute(x, axis, [(i, i ^ distance) for i in range(count)])]
  transfers between devices with their start and end apart: 24 -> 25, of which waited for: 9 -> 8; matrix products, arithmetic and copies ran while one was open for 16% -> 9% of each run, Pallas kernels for 10% -> 10%
where the time goes in v3:
time: 133 us; the launch traced here: 132 us
  Pallas kernels  65.2 us (49%)
  starting transfers between devices  28.2 us (21%)
  waiting for transfers between devices  21.2 us (16%)
  other arithmetic  12.5 us (9%)
  local copies, waits for them, and re-layouts  3.36 us (3%)
  between operations  1.84 us (1%)
    pallas_call x1, Pallas kernels, main_call(): pl.pallas_call(lambda *refs: main_kernel(batch, len(parts), *refs), grid=...  36.9 us
    ppermute x20, starting transfers between devices, swap(): return lax.ppermute(x, axis, [(i, i ^ distance) for i in range(count)])  22 us
    pallas_call x1, Pallas kernels, tile_call(): pl.pallas_call(tile_kernel, in_specs=[smem] * 2 + [vmem] * 22, out_specs=...  15.5 us
    ppermute x20, waiting for transfers between devices, swap(): return lax.ppermute(x, axis, [(i, i ^ distance) for i in range(count)])  13.5 us
    pallas_call x1, Pallas kernels, input_call(): pl.pallas_call(lambda *refs: input_kernel(batch, len(parts), *refs), grid...  12.8 us
    ppermute x3, waiting for transfers between devices, reduce_tiles(): piece = lax.ppermute(piece, ('strip', 'img'), pairs)  7.75 us
    ppermute x3, starting transfers between devices, reduce_tiles(): piece = lax.ppermute(piece, ('strip', 'img'), pairs)  4.89 us
  transfers between devices with their start and end apart: 25, of which 8 were waited for; matrix products, arithmetic and copies ran while one was open for 9% of the time, Pallas kernels for 10%

profile of v3, /device:TPU:0, one launch (start us, length us, event | category | flops | bytes accessed | tf_op | source)
XLA Modules:
  0.0 132.4 jit_solution(9933183774451902234)
XLA Ops:
  1.6 5.1 %collective-permute-start.4 = (bf16[5,64,128]{2,1,0:T(8,128)(2,1)S(1)}, bf16[5,64,128]{2,1,0:T(8,128)(2,1)S(1)}, u32[]{:S(2)}, u32[]{:S(2)}) collective-permute-start(bf16[5,64,128]{2,1,0:T(8,128)(2,1)S(1)} %dynamic-slice_convert_fusion), channel_id=1, source_target_pairs={{0,6},{1,7},{2,4},{3,5},{4,2},{5,3},{6,0},{7,1},{8,14},{9,15},{10,... | collective-permute-start | bytes 245768 | tf_op jit(solution)/shard_map/ppermute | solution.py:533
  9.3 1.5 %multiply_reduce_fusion = (f32[512]{0:T(512)S(1)}, bf16[64,512]{1,0:T(8,128)(2,1)}) fusion(f32[512,64]{0,1:T(8,128)} %param.37), kind=kLoop, calls=%fused_computation.17 | loop fusion | flops 130560 | bytes 198656 | tf_op jit(solution)/shard_map/reduce_sum | solution.py:655
  10.8 2.8 %collective-permute-done.3 = bf16[5,64,128]{2,1,0:T(8,128)(2,1)S(1)} collective-permute-done((bf16[5,64,128]{2,1,0:T(8,128)(2,1)S(1)}, bf16[5,64,128]{2,1,0:T(8,128)(2,1)S(1)}, u32[]{:S(2)}, u32[]{:S(2)}) %collective-permute-start.3) | collective-permute-done | bytes 81952 | tf_op jit(solution)/shard_map/ppermute | solution.py:533
  13.7 1.6 %collective-permute-start.5 = (bf16[20,64,128]{2,1,0:T(8,128)(2,1)S(1)}, bf16[20,64,128]{2,1,0:T(8,128)(2,1)S(1)}, u32[]{:S(2)}, u32[]{:S(2)}) collective-permute-start(bf16[20,64,128]{2,1,0:T(8,128)(2,1)S(1)} %pad_maximum_fusion.refs_9_.refs_7_), channel_id=1, source_target_pairs={{0,1},{1,0},{2,3},{3,2},{4,5},{5,4},{6,7},{7,6},{8,9},{9,8},{10,11... | collective-permute-start | bytes 983048 | tf_op jit(solution)/shard_map/ppermute | solution.py:533
  15.2 1.2 fusion.6.refs_0_
  16.4 1.3 reduce_sum.18
  18.4 1.5 %convert_element_type.96.refs_14_ = bf16[64,256]{1,0:T(8,128)(2,1)} convert(f32[64,256]{1,0:T(8,128)} %refs_18_.1) | non-fusion elementwise | flops 16384 | bytes 98304 | tf_op jit(solution)/shard_map/convert_element_type | solution.py:670
  20.5 3.1 %collective-permute-done.5.refs_10_.refs_8_ = bf16[20,64,128]{2,1,0:T(8,128)(2,1)S(1)} collective-permute-done((bf16[20,64,128]{2,1,0:T(8,128)(2,1)S(1)}, bf16[20,64,128]{2,1,0:T(8,128)(2,1)S(1)}, u32[]{:S(2)}, u32[]{:S(2)}) %collective-permute-start.5) | collective-permute-done | bytes 327712 | tf_op jit(solution)/shard_map/ppermute | solution.py:533
  23.6 1.3 broadcast_multiply_fusion.1
  24.8 1.5 %bitcast_convert_fusion.1.refs_13_ = bf16[64,256]{1,0:T(8,128)(2,1)} fusion(f32[256,64]{0,1:T(8,128)} %param.31), kind=kLoop, calls=%fused_computation.40 | loop fusion | flops 16384 | bytes 98304 | tf_op jit(solution)/shard_map/convert_element_type | solution.py:669
  27.4 36.9 %main.1 = (bf16[20,8,32,256]{3,2,1,0:T(8,128)(2,1)}, bf16[20,8,32,256]{3,2,1,0:T(8,128)(2,1)}, bf16[20,8,32,256]{3,2,1,0:T(8,128)(2,1)}, bf16[20,32,256]{2,1,0:T...) custom-call(s32[40]{0:T(128)} %fusion.6.refs_0_, ...), custom_call_target="tpu_custom_call" | custom-call | tf_op jit(solution)/shard_map/main/pallas_call | solution.py:250
  67.8 5.1 %collective-permute-done.21 = bf16[528,128]{1,0:T(8,128)(2,1)S(1)} collective-permute-done((bf16[528,128]{1,0:T(8,128)(2,1)S(1)}, bf16[528,128]{1,0:T(8,128)(2,1)S(1)}, u32[]{:S(2)}, u32[]{:S(2)}) %collective-permute-start.21) | collective-permute-done | bytes 135200 | tf_op jit(solution)/shard_map/ppermute | solution.py:533
  72.9 1.6 %collective-permute-start.22 = (bf16[528,128]{1,0:T(8,128)(2,1)S(1)}, bf16[528,128]{1,0:T(8,128)(2,1)S(1)}, u32[]{:S(2)}, u32[]{:S(2)}) collective-permute-start(bf16[528,128]{1,0:T(8,128)(2,1)S(1)} %add_convert_fusion.2), channel_id=1, source_target_pairs={{0,1},{1,0},{2,3},{3,2},{4,5},{5,4},{6,7},{7,6},{8,9},{9,8},{10,11... | collective-permute-start | bytes 405512 | tf_op jit(solution)/shard_map/ppermute | solution.py:533
  75.2 1.3 add.134
  76.5 3.4 %collective-permute-start.13 = (bf16[4,160,128]{2,1,0:T(8,128)(2,1)S(1)}, bf16[4,160,128]{2,1,0:T(8,128)(2,1)S(1)}, u32[]{:S(2)}, u32[]{:S(2)}) collective-permute-start(bf16[4,160,128]{2,1,0:T(8,128)(2,1)S(1)} %get-tuple-element.76), channel_id=1, source_target_pairs={{0,17},{1,16},{2,19},{3,18},{4,21},{5,20},{6,23},{7,22},{8,25},{9,... | collective-permute-start | bytes 491528 | tf_op jit(solution)/shard_map/ppermute | solution.py:593
  80.0 1.4 %collective-permute-start.11 = (bf16[4,160,128]{2,1,0:T(8,128)(2,1)S(1)}, bf16[4,160,128]{2,1,0:T(8,128)(2,1)S(1)}, u32[]{:S(2)}, u32[]{:S(2)}) collective-permute-start(bf16[4,160,128]{2,1,0:T(8,128)(2,1)S(1)} %get-tuple-element.75), channel_id=1, source_target_pairs={{0,1},{1,0},{2,3},{3,2},{4,5},{5,4},{6,7},{7,6},{8,9},{9,8},{10,11... | collective-permute-start | bytes 491528 | tf_op jit(solution)/shard_map/ppermute | solution.py:593
  81.5 7.3 %collective-permute-done.13 = bf16[4,160,128]{2,1,0:T(8,128)(2,1)S(1)} collective-permute-done((bf16[4,160,128]{2,1,0:T(8,128)(2,1)S(1)}, bf16[4,160,128]{2,1,0:T(8,128)(2,1)S(1)}, u32[]{:S(2)}, u32[]{:S(2)}) %collective-permute-start.13) | collective-permute-done | bytes 163872 | tf_op jit(solution)/shard_map/ppermute | solution.py:593
  88.7 1.6 %collective-permute-start.23 = (bf16[528,128]{1,0:T(8,128)(2,1)S(1)}, bf16[528,128]{1,0:T(8,128)(2,1)S(1)}, u32[]{:S(2)}, u32[]{:S(2)}) collective-permute-start(bf16[528,128]{1,0:T(8,128)(2,1)S(1)} %add_convert_fusion.1), channel_id=1, source_target_pairs={{0,2},{1,3},{2,0},{3,1},{4,6},{5,7},{6,4},{7,5},{8,10},{9,11},{10,... | collective-permute-start | bytes 405512 | tf_op jit(solution)/shard_map/ppermute | solution.py:533
  90.9 3.4 %collective-permute-start.16 = (bf16[1,160,128]{2,1,0:T(8,128)(2,1)S(1)}, bf16[1,160,128]{2,1,0:T(8,128)(2,1)S(1)}, u32[]{:S(2)}, u32[]{:S(2)}) collective-permute-start(bf16[1,160,128]{2,1,0:T(8,128)(2,1)S(1)} %get-tuple-element.79), channel_id=1, source_target_pairs={{0,6},{1,7},{2,4},{3,5},{4,2},{5,3},{6,0},{7,1},{8,14},{9,15},{10,... | collective-permute-start | bytes 122888 | tf_op jit(solution)/shard_map/ppermute | solution.py:533
  94.3 2.2 %collective-permute-start.14 = (bf16[1,160,128]{2,1,0:T(8,128)(2,1)S(1)}, bf16[1,160,128]{2,1,0:T(8,128)(2,1)S(1)}, u32[]{:S(2)}, u32[]{:S(2)}) collective-permute-start(bf16[1,160,128]{2,1,0:T(8,128)(2,1)S(1)} %get-tuple-element.78), channel_id=1, source_target_pairs={{0,2},{1,3},{2,0},{3,1},{4,6},{5,7},{6,4},{7,5},{8,10},{9,11},{10,... | collective-permute-start | bytes 122888 | tf_op jit(solution)/shard_map/ppermute | solution.py:533
  97.0 2.5 %collective-permute-start.24 = (bf16[528,128]{1,0:T(8,128)(2,1)S(1)}, bf16[528,128]{1,0:T(8,128)(2,1)S(1)}, u32[]{:S(2)}, u32[]{:S(2)}) collective-permute-start(bf16[528,128]{1,0:T(8,128)(2,1)S(1)} %add_convert_fusion.refs_13_), channel_id=1, source_target_pairs={{0,4},{1,5},{2,6},{3,7},{4,0},{5,1},{6,2},{7,3},{8,12},{9,13},{10,... | collective-permute-start | bytes 405512 | tf_op jit(solution)/shard_map/ppermute | solution.py:533
  100.7 1.8 %collective-permute-start.19 = (bf16[5,32,128]{2,1,0:T(8,128)(2,1)S(1)}, bf16[5,32,128]{2,1,0:T(8,128)(2,1)S(1)}, u32[]{:S(2)}, u32[]{:S(2)}) collective-permute-start(bf16[5,32,128]{2,1,0:T(8,128)(2,1)S(1)} %bitcast.53), channel_id=1, source_target_pairs={{0,24},{8,16},{16,8},{24,0},{1,25},{9,17},{17,9},{25,1},{2,26},{10... | collective-permute-start | bytes 122888 | tf_op jit(solution)/shard_map/ppermute | solution.py:533
  103.2 12.8 %input_grad.1 = bf16[20,8,32,256]{3,2,1,0:T(8,128)(2,1)} custom-call(s32[40]{0:T(128)} %fusion.6.refs_0_, s32[1]{0:T(128)} %bitcast.refs_4_.refs_1_, bf16[20,8,32,256]{3,2,1,0:T(8,128)(2,1)} %refs_2_.1, bf16[20,8,32,256]{3,2,1,0:T(8,128)(2,1)} %get-tuple-element.45.refs_3_, bf16[20,8,32,256]{3,2,1,0:T(8,128)(2,1)} %get-tuple-element.46.refs_4_, ...), custom_call_target="tpu_custom_call" | custom-call | tf_op jit(solution)/shard_map/input_grad/pallas_call | solution.py:329
  116.7 15.5 %tile_adam.1 = (f32[5,128,128]{2,1,0:T(8,128)}, f32[5,128,128]{2,1,0:T(8,128)}, f32[5,128,128]{2,1,0:T(8,128)}, f32[5,128,128]{2,1,0:T(8,128)}, f32[5,128,128]{2...) custom-call(s32[1]{0:T(128)} %bitcast.6.refs_0_, ...), custom_call_target="tpu_custom_call" | custom-call | tf_op jit(solution)/shard_map/tile_adam/pallas_call | solution.py:506
  (76 shorter events, 13.1 us)
Async XLA Ops:
  1.6 9.2 %collective-permute-start.4 = (bf16[5,64,128]{2,1,0:T(8,128)(2,1)S(1)}, bf16[5,64,128]{2,1,0:T(8,128)(2,1)S(1)}, u32[]{:S(2)}, u32[]{:S(2)}) collective-permute-start(bf16[5,64,128]{2,1,0:T(8,128)(2,1)S(1)} %dynamic-slice_convert_fusion), channel_id=1, source_target_pairs={{0,6},{1,7},{2,4},{3,5},{4,2},{5,3},{6,0},{7,1},{8,14},{9,15},{10,... | collective-permute-start | bytes 245768 | tf_op jit(solution)/shard_map/ppermute | solution.py:533
  6.7 6.9 %collective-permute-start.3 = (bf16[5,64,128]{2,1,0:T(8,128)(2,1)S(1)}, bf16[5,64,128]{2,1,0:T(8,128)(2,1)S(1)}, u32[]{:S(2)}, u32[]{:S(2)}) collective-permute-start(bf16[5,64,128]{2,1,0:T(8,128)(2,1)S(1)} %dynamic-slice_convert_fusion), channel_id=1, source_target_pairs={{0,4},{1,5},{2,6},{3,7},{4,0},{5,1},{6,2},{7,3},{8,12},{9,13},{10,... | collective-permute-start | bytes 245768 | tf_op jit(solution)/shard_map/ppermute | solution.py:533
  6.7 6.9 %collective-permute-start.2 = (bf16[5,64,128]{2,1,0:T(8,128)(2,1)S(1)}, bf16[5,64,128]{2,1,0:T(8,128)(2,1)S(1)}, u32[]{:S(2)}, u32[]{:S(2)}) collective-permute-start(bf16[5,64,128]{2,1,0:T(8,128)(2,1)S(1)} %dynamic-slice_convert_fusion), channel_id=1, source_target_pairs={{0,2},{1,3},{2,0},{3,1},{4,6},{5,7},{6,4},{7,5},{8,10},{9,11},{10,... | collective-permute-start | bytes 245768 | tf_op jit(solution)/shard_map/ppermute | solution.py:533
  8.5 17.8 %collective-permute-start = (bf16[20,32,256]{2,1,0:T(8,128)(2,1)S(1)}, bf16[20,32,256]{2,1,0:T(8,128)(2,1)S(1)}, u32[]{:S(2)}, u32[]{:S(2)}) collective-permute-start(bf16[20,32,256]{2,1,0:T(8,128)(2,1)S(1)} %get-tuple-element.74), channel_id=1, source_target_pairs={{0,8},{8,0},{16,24},{24,16},{1,9},{9,1},{17,25},{25,17},{2,10},{10... | collective-permute-start | bytes 983048 | tf_op jit(solution)/shard_map/ppermute | solution.py:533
  8.6 17.7 %collective-permute-start.1 = (bf16[20,32,256]{2,1,0:T(8,128)(2,1)S(1)}, bf16[20,32,256]{2,1,0:T(8,128)(2,1)S(1)}, u32[]{:S(2)}, u32[]{:S(2)}) collective-permute-start(bf16[20,32,256]{2,1,0:T(8,128)(2,1)S(1)} %get-tuple-element.73), channel_id=1, source_target_pairs={{8,16},{16,8},{9,17},{17,9},{10,18},{18,10},{11,19},{19,11},{12,20... | collective-permute-start | bytes 983048 | tf_op jit(solution)/shard_map/ppermute | solution.py:548
  13.7 9.9 %collective-permute-start.5 = (bf16[20,64,128]{2,1,0:T(8,128)(2,1)S(1)}, bf16[20,64,128]{2,1,0:T(8,128)(2,1)S(1)}, u32[]{:S(2)}, u32[]{:S(2)}) collective-permute-start(bf16[20,64,128]{2,1,0:T(8,128)(2,1)S(1)} %pad_maximum_fusion.refs_9_.refs_7_), channel_id=1, source_target_pairs={{0,1},{1,0},{2,3},{3,2},{4,5},{5,4},{6,7},{7,6},{8,9},{9,8},{10,11... | collective-permute-start | bytes 983048 | tf_op jit(solution)/shard_map/ppermute | solution.py:533
  20.5 5.8 %collective-permute-start.6 = (bf16[20,64,128]{2,1,0:T(8,128)(2,1)S(1)}, bf16[20,64,128]{2,1,0:T(8,128)(2,1)S(1)}, u32[]{:S(2)}, u32[]{:S(2)}) collective-permute-start(bf16[20,64,128]{2,1,0:T(8,128)(2,1)S(1)} %pad_maximum_fusion.refs_9_.refs_7_), channel_id=1, source_target_pairs={{0,8},{8,0},{16,24},{24,16},{1,9},{9,1},{17,25},{25,17},{2,10},{10... | collective-permute-start | bytes 983048 | tf_op jit(solution)/shard_map/ppermute | solution.py:533
  23.6 2.8 %collective-permute-start.7 = (bf16[20,64,128]{2,1,0:T(8,128)(2,1)S(1)}, bf16[20,64,128]{2,1,0:T(8,128)(2,1)S(1)}, u32[]{:S(2)}, u32[]{:S(2)}) collective-permute-start(bf16[20,64,128]{2,1,0:T(8,128)(2,1)S(1)} %collective-permute-done.5.refs_10_.refs_8_), channel_id=1, source_target_pairs={{0,8},{8,0},{16,24},{24,16},{1,9},{9,1},{17,25},{25,17},{2,10},{10... | collective-permute-start | bytes 983048 | tf_op jit(solution)/shard_map/ppermute | solution.py:533
  64.8 10.4 %collective-permute-start.10 = (bf16[2,40,32,128]{3,2,1,0:T(8,128)(2,1)}, bf16[2,40,32,128]{3,2,1,0:T(8,128)(2,1)S(1)}, u32[]{:S(2)}, u32[]{:S(2)}) collective-permute-start(bf16[2,40,32,128]{3,2,1,0:T(8,128)(2,1)} %get-tuple-element.50), channel_id=1, source_target_pairs={{0,8},{8,0},{16,24},{24,16},{1,9},{9,1},{17,25},{25,17},{2,10},{10... | collective-permute-start | bytes 1966088 | tf_op jit(solution)/shard_map/ppermute | solution.py:533
  66.9 5.9 %collective-permute-start.21 = (bf16[528,128]{1,0:T(8,128)(2,1)S(1)}, bf16[528,128]{1,0:T(8,128)(2,1)S(1)}, u32[]{:S(2)}, u32[]{:S(2)}) collective-permute-start(bf16[528,128]{1,0:T(8,128)(2,1)S(1)} %add_convert_fusion.3), channel_id=1, source_target_pairs={{0,16},{8,24},{16,0},{24,8},{1,17},{9,25},{17,1},{25,9},{2,18},{10... | collective-permute-start | bytes 405512 | tf_op jit(solution)/shard_map/ppermute | solution.py:533
  72.9 7.1 %collective-permute-start.22 = (bf16[528,128]{1,0:T(8,128)(2,1)S(1)}, bf16[528,128]{1,0:T(8,128)(2,1)S(1)}, u32[]{:S(2)}, u32[]{:S(2)}) collective-permute-start(bf16[528,128]{1,0:T(8,128)(2,1)S(1)} %add_convert_fusion.2), channel_id=1, source_target_pairs={{0,1},{1,0},{2,3},{3,2},{4,5},{5,4},{6,7},{7,6},{8,9},{9,8},{10,11... | collective-permute-start | bytes 405512 | tf_op jit(solution)/shard_map/ppermute | solution.py:533
  74.5 26.1 %collective-permute-start.8 = (bf16[20,32,256]{2,1,0:T(8,128)(2,1)}, bf16[20,32,256]{2,1,0:T(8,128)(2,1)S(1)}, u32[]{:S(2)}, u32[]{:S(2)}) collective-permute-start(bf16[20,32,256]{2,1,0:T(8,128)(2,1)} %get-tuple-element.47), channel_id=1, source_target_pairs={{0,8},{8,0},{16,24},{24,16},{1,9},{9,1},{17,25},{25,17},{2,10},{10... | collective-permute-start | bytes 983048 | tf_op jit(solution)/shard_map/ppermute | solution.py:533
  74.5 27.9 %collective-permute-start.9 = (bf16[20,32,256]{2,1,0:T(8,128)(2,1)}, bf16[20,32,256]{2,1,0:T(8,128)(2,1)S(1)}, u32[]{:S(2)}, u32[]{:S(2)}) collective-permute-start(bf16[20,32,256]{2,1,0:T(8,128)(2,1)} %get-tuple-element.48), channel_id=1, source_target_pairs={{8,16},{16,8},{9,17},{17,9},{10,18},{18,10},{11,19},{19,11},{12,20... | collective-permute-start | bytes 983048 | tf_op jit(solution)/shard_map/ppermute | solution.py:548
  76.5 12.2 %collective-permute-start.13 = (bf16[4,160,128]{2,1,0:T(8,128)(2,1)S(1)}, bf16[4,160,128]{2,1,0:T(8,128)(2,1)S(1)}, u32[]{:S(2)}, u32[]{:S(2)}) collective-permute-start(bf16[4,160,128]{2,1,0:T(8,128)(2,1)S(1)} %get-tuple-element.76), channel_id=1, source_target_pairs={{0,17},{1,16},{2,19},{3,18},{4,21},{5,20},{6,23},{7,22},{8,25},{9,... | collective-permute-start | bytes 491528 | tf_op jit(solution)/shard_map/ppermute | solution.py:593
  79.9 10.9 %collective-permute-start.12 = (bf16[4,160,128]{2,1,0:T(8,128)(2,1)S(1)}, bf16[4,160,128]{2,1,0:T(8,128)(2,1)S(1)}, u32[]{:S(2)}, u32[]{:S(2)}) collective-permute-start(bf16[4,160,128]{2,1,0:T(8,128)(2,1)S(1)} %get-tuple-element.77), channel_id=1, source_target_pairs={{0,16},{1,17},{2,18},{3,19},{4,20},{5,21},{6,22},{7,23},{8,24},{9,... | collective-permute-start | bytes 491528 | tf_op jit(solution)/shard_map/ppermute | solution.py:593
  80.0 10.8 %collective-permute-start.11 = (bf16[4,160,128]{2,1,0:T(8,128)(2,1)S(1)}, bf16[4,160,128]{2,1,0:T(8,128)(2,1)S(1)}, u32[]{:S(2)}, u32[]{:S(2)}) collective-permute-start(bf16[4,160,128]{2,1,0:T(8,128)(2,1)S(1)} %get-tuple-element.75), channel_id=1, source_target_pairs={{0,1},{1,0},{2,3},{3,2},{4,5},{5,4},{6,7},{7,6},{8,9},{9,8},{10,11... | collective-permute-start | bytes 491528 | tf_op jit(solution)/shard_map/ppermute | solution.py:593
  88.7 5.6 %collective-permute-start.23 = (bf16[528,128]{1,0:T(8,128)(2,1)S(1)}, bf16[528,128]{1,0:T(8,128)(2,1)S(1)}, u32[]{:S(2)}, u32[]{:S(2)}) collective-permute-start(bf16[528,128]{1,0:T(8,128)(2,1)S(1)} %add_convert_fusion.1), channel_id=1, source_target_pairs={{0,2},{1,3},{2,0},{3,1},{4,6},{5,7},{6,4},{7,5},{8,10},{9,11},{10,... | collective-permute-start | bytes 405512 | tf_op jit(solution)/shard_map/ppermute | solution.py:533
  90.9 6.0 %collective-permute-start.16 = (bf16[1,160,128]{2,1,0:T(8,128)(2,1)S(1)}, bf16[1,160,128]{2,1,0:T(8,128)(2,1)S(1)}, u32[]{:S(2)}, u32[]{:S(2)}) collective-permute-start(bf16[1,160,128]{2,1,0:T(8,128)(2,1)S(1)} %get-tuple-element.79), channel_id=1, source_target_pairs={{0,6},{1,7},{2,4},{3,5},{4,2},{5,3},{6,0},{7,1},{8,14},{9,15},{10,... | collective-permute-start | bytes 122888 | tf_op jit(solution)/shard_map/ppermute | solution.py:533
  94.3 6.1 %collective-permute-start.15 = (bf16[1,160,128]{2,1,0:T(8,128)(2,1)S(1)}, bf16[1,160,128]{2,1,0:T(8,128)(2,1)S(1)}, u32[]{:S(2)}, u32[]{:S(2)}) collective-permute-start(bf16[1,160,128]{2,1,0:T(8,128)(2,1)S(1)} %get-tuple-element.80), channel_id=1, source_target_pairs={{0,4},{1,5},{2,6},{3,7},{4,0},{5,1},{6,2},{7,3},{8,12},{9,13},{10,... | collective-permute-start | bytes 122888 | tf_op jit(solution)/shard_map/ppermute | solution.py:533
  94.3 6.1 %collective-permute-start.14 = (bf16[1,160,128]{2,1,0:T(8,128)(2,1)S(1)}, bf16[1,160,128]{2,1,0:T(8,128)(2,1)S(1)}, u32[]{:S(2)}, u32[]{:S(2)}) collective-permute-start(bf16[1,160,128]{2,1,0:T(8,128)(2,1)S(1)} %get-tuple-element.78), channel_id=1, source_target_pairs={{0,2},{1,3},{2,0},{3,1},{4,6},{5,7},{6,4},{7,5},{8,10},{9,11},{10,... | collective-permute-start | bytes 122888 | tf_op jit(solution)/shard_map/ppermute | solution.py:533
  97.0 19.0 %collective-permute-start.24 = (bf16[528,128]{1,0:T(8,128)(2,1)S(1)}, bf16[528,128]{1,0:T(8,128)(2,1)S(1)}, u32[]{:S(2)}, u32[]{:S(2)}) collective-permute-start(bf16[528,128]{1,0:T(8,128)(2,1)S(1)} %add_convert_fusion.refs_13_), channel_id=1, source_target_pairs={{0,4},{1,5},{2,6},{3,7},{4,0},{5,1},{6,2},{7,3},{8,12},{9,13},{10,... | collective-permute-start | bytes 405512 | tf_op jit(solution)/shard_map/ppermute | solution.py:533
  100.5 15.5 %collective-permute-start.17 = (bf16[5,32,128]{2,1,0:T(8,128)(2,1)S(1)}, bf16[5,32,128]{2,1,0:T(8,128)(2,1)S(1)}, u32[]{:S(2)}, u32[]{:S(2)}) collective-permute-start(bf16[5,32,128]{2,1,0:T(8,128)(2,1)S(1)} %bitcast.51), channel_id=1, source_target_pairs={{0,8},{8,0},{16,24},{24,16},{1,9},{9,1},{17,25},{25,17},{2,10},{10... | collective-permute-start | bytes 122888 | tf_op jit(solution)/shard_map/ppermute | solution.py:533
  100.6 15.4 %collective-permute-start.18 = (bf16[5,32,128]{2,1,0:T(8,128)(2,1)S(1)}, bf16[5,32,128]{2,1,0:T(8,128)(2,1)S(1)}, u32[]{:S(2)}, u32[]{:S(2)}) collective-permute-start(bf16[5,32,128]{2,1,0:T(8,128)(2,1)S(1)} %bitcast.52), channel_id=1, source_target_pairs={{0,16},{8,24},{16,0},{24,8},{1,17},{9,25},{17,1},{25,9},{2,18},{10... | collective-permute-start | bytes 122888 | tf_op jit(solution)/shard_map/ppermute | solution.py:533
  100.7 15.4 %collective-permute-start.19 = (bf16[5,32,128]{2,1,0:T(8,128)(2,1)S(1)}, bf16[5,32,128]{2,1,0:T(8,128)(2,1)S(1)}, u32[]{:S(2)}, u32[]{:S(2)}) collective-permute-start(bf16[5,32,128]{2,1,0:T(8,128)(2,1)S(1)} %bitcast.53), channel_id=1, source_target_pairs={{0,24},{8,16},{16,8},{24,0},{1,25},{9,17},{17,9},{25,1},{2,26},{10... | collective-permute-start | bytes 122888 | tf_op jit(solution)/shard_map/ppermute | solution.py:533
  (15 other events, 60.8 us)

commit v4 on v3

--- a/solution.py
+++ b/solution.py
@@ -24,7 +24,9 @@
 TN = ((0,), (0,))
 GELU_A = 0.7978845608028654
 GELU_B = 0.044715
-VMEM_LIMIT = 56 * 1024 * 1024
+LOSS_ROWS = 16
+MAIN_VMEM = 56 * 1024 * 1024
+FINISH_VMEM = 56 * 1024 * 1024
 
 
 def dot(a, b, dims=NN):
@@ -55,18 +57,23 @@
     return before, after
 
 
-def place_weights(place, parts, core, put):
+def place_weights(places, ids, parts, put):
     half = parts[0].shape[1]
     count = len(parts) // 2
     size = parts[0].shape[0]
     for t in range(40):
-        which = place[t] // size
-        index = place[t] % size
+        which = lax.div(places[t], size)
+        index = lax.rem(places[t], size)
         for side in range(2):
             block = parts[side * count][index]
             for n in range(1, count):
                 block = jnp.where(which == n, parts[side * count + n][index], block)
-            put(t, block, pl.multiple_of((core ^ side) * half, half))
+            put(t, block, pl.multiple_of((lax.rem(ids[0], 2) ^ side) * half, half))
+
+
+def loss_scale(present, positions, latent):
+    count = jnp.sum(present[...].astype(F32)) * positions
+    return LOSS_WEIGHT / (count * latent)
 
 
 def shift_lines(line, first, last):
@@ -77,16 +84,17 @@
 
 
 def main_kernel(batch, part_count, *refs):
-    place, slots, alive_all, pull_all, core = refs[:5]
-    feat, near, far, cot = refs[5:9]
+    ids, places, slots, present = refs[:4]
+    present_row, feat, near, far, cot = refs[4:9]
     parts = refs[9 : 9 + part_count]
-    proj, dec, code, norms = refs[9 + part_count : 13 + part_count]
-    (decoded, d_pre_out, d_resid_out, near_out, far_out, keep, send, small) = refs[
-        13 + part_count : 21 + part_count
+    proj_full, dec_full, code_full = refs[9 + part_count : 12 + part_count]
+    (decoded, d_pre_out, d_resid_out, near_out, far_out, weights, keep, send) = refs[
+        12 + part_count : 20 + part_count
     ]
-    (weights, mixer, framed, d_pre_turned, sums, g_mixer, g_proj, g_dec, g_code, totals, loss) = refs[
-        21 + part_count :
+    (mixer, framed, d_pre_turned, sums, g_mixer, g_proj, g_dec, g_code, totals, loss) = refs[
+        20 + part_count : 30 + part_count
     ]
+    proj, dec, code, norms, scale = refs[30 + part_count :]
     step = pl.program_id(0)
     steps = pl.num_programs(0)
     height, wide, channels = feat.shape[1:]
@@ -94,7 +102,7 @@
     tile = parts[0].shape[2]
     half = tile // 2
     images = framed.shape[0]
-    lead = core[0] == 0
+    lead = lax.rem(ids[0], 2) == 0
 
     @pl.when(step == 0)
     def _():
@@ -107,7 +115,13 @@
             else:
                 mixer[pl.ds(i * tile + row, half), j * tile : (j + 1) * tile] = block
 
-        place_weights(place, parts, core[0], put)
+        place_weights(places, ids, parts, put)
+        proj[...] = proj_full[...].astype(BF16)
+        dec[...] = dec_full[...].astype(BF16)
+        code[...] = code_full[...].astype(BF16)
+        words = code[...].astype(F32)
+        norms[...] = jnp.sum(words * words, axis=0, keepdims=True) * (1.0 / SOFTMAX_WARMTH)
+        scale[0] = 2.0 * loss_scale(present_row, 4 * count, proj.shape[0])
         for ref in (g_mixer, g_proj, g_dec, g_code, totals, loss):
             ref[...] = jnp.zeros_like(ref)
 
@@ -117,8 +131,8 @@
 
     def chain(n):
         image = step * batch + n
-        alive = alive_all[image]
-        pull = pull_all[image]
+        alive = present[ids[1] * images + image].astype(F32)
+        pull = alive * scale[0]
         for r in range(height + 2):
             if r == 0:
                 line = jnp.where(lead, far[n].astype(F32), near[n].astype(F32))
@@ -215,21 +229,30 @@
             for q in range(0, 4, 2):
                 even = block[q * quarter : (q + 1) * quarter]
                 odd = block[(q + 1) * quarter : (q + 2) * quarter]
-                keep[q // 2, slots[t]] = jnp.where(lead, even, odd)
-                send[q // 2, slots[t]] = jnp.where(lead, odd, even)
+                row = pl.ds(pl.multiple_of(slots[t] * quarter, quarter), quarter)
+                keep[q // 2, row] = jnp.where(lead, even, odd)
+                send[q // 2, row] = jnp.where(lead, odd, even)
         g_words = g_code[...] - (2.0 / SOFTMAX_WARMTH) * totals[...] * code[...].astype(F32)
-        row = 0
+        blocks = []
         for grad in (g_proj[...], g_dec[...], g_words):
             for left in range(0, grad.shape[1], 128):
-                small[row : row + grad.shape[0]] = grad[:, left : left + 128].astype(BF16)
-                row += grad.shape[0]
-        small[row:] = jnp.zeros((small.shape[0] - row, 128), BF16)
-        small[row : row + 16, 0 : loss.shape[1]] = jnp.broadcast_to(
-            loss[...] * (1.0 / 16.0), (16, loss.shape[1])
-        ).astype(BF16)
-
-
-def main_call(place, slots, alive, pull, core, feat, near, far, cot, parts, proj, dec, code, norms):
+                blocks.append(grad[:, left : left + 128].astype(BF16))
+        size = blocks[0].shape[0]
+        each = len(blocks) // 4
+        start = keep.shape[1] - each * size - LOSS_ROWS
+        for x in range(2):
+            for n in range(each):
+                even, odd = blocks[2 * x * each + n], blocks[(2 * x + 1) * each + n]
+                row = slice(start + n * size, start + (n + 1) * size)
+                keep[x, row] = jnp.where(lead, even, odd)
+                send[x, row] = jnp.where(lead, odd, even)
+        row = start + each * size
+        value = jnp.broadcast_to(loss[...] * (1.0 / LOSS_ROWS), (LOSS_ROWS, loss.shape[1]))
+        keep[0, row:, 0 : loss.shape[1]] = jnp.where(lead, value, 0.0).astype(BF16)
+        send[0, row:, 0 : loss.shape[1]] = jnp.where(lead, 0.0, value).astype(BF16)
+
+
+def main_call(ids, places, slots, present, feat, near, far, cot, parts, proj, dec, code):
     images, height, wide, channels = feat.shape
     latent, words = code.shape
     size, half, tile = parts[0].shape
@@ -244,19 +267,19 @@
 
     big = jax.ShapeDtypeStruct(feat.shape, BF16)
     edge = jax.ShapeDtypeStruct(near.shape, BF16)
-    part = jax.ShapeDtypeStruct((2, slot_count, tile // 4, tile), BF16)
-    rows = (2 * latent * channels + latent * words) // 128 + 16
-    shapes = (big, big, big, edge, edge, part, part, jax.ShapeDtypeStruct((rows, 128), BF16))
+    rows = (2 * latent * channels + latent * words) // (4 * 128) + LOSS_ROWS
+    part = jax.ShapeDtypeStruct((2, slot_count * tile // 4 + rows, tile), BF16)
+    weights = jax.ShapeDtypeStruct((3, 3 * channels, channels), BF16)
+    shapes = (big, big, big, edge, edge, weights, part, part)
     return pl.pallas_call(
         lambda *refs: main_kernel(batch, len(parts), *refs),
         grid=(images // batch,),
-        in_specs=[smem] * 5
-        + [strip, line, line, strip]
-        + [whole(a.shape) for a in (*parts, proj, dec, code, norms)],
+        in_specs=[smem] * 4
+        + [whole((1, present.shape[0])), strip, line, line, strip]
+        + [whole(a.shape) for a in (*parts, proj, dec, code)],
         out_specs=[strip] * 3 + [line] * 2 + [whole(s.shape) for s in shapes[5:]],
         out_shape=shapes,
         scratch_shapes=[
-            pltpu.VMEM((3, 3 * channels, channels), BF16),
             pltpu.VMEM((channels, channels), BF16),
             pltpu.VMEM((images, (height + 2) * wide, 3 * channels), BF16),
             pltpu.VMEM((images, channels, height * wide), BF16),
@@ -267,76 +290,15 @@
             pltpu.VMEM((latent, words), F32),
             pltpu.VMEM((1, words), F32),
             pltpu.VMEM((1, latent), F32),
+            pltpu.VMEM(proj.shape, BF16),
+            pltpu.VMEM(dec.shape, BF16),
+            pltpu.VMEM(code.shape, BF16),
+            pltpu.VMEM((1, words), F32),
+            pltpu.SMEM((1,), F32),
         ],
-        compiler_params=pltpu.CompilerParams(vmem_limit_bytes=VMEM_LIMIT),
+        compiler_params=pltpu.CompilerParams(vmem_limit_bytes=MAIN_VMEM),
         name="main",
-    )(place, slots, alive, pull, core, feat, near, far, cot, *parts, proj, dec, code, norms)
-
-
-def input_kernel(batch, part_count, *refs):
-    place, core, feat, d_resid, d_pre, near, far = refs[:7]
-    parts = refs[7 : 7 + part_count]
-    out, weights = refs[7 + part_count :]
-    height, wide, channels = feat.shape[1:]
-    count = height * wide
-    tile = parts[0].shape[2]
-    half = tile // 2
-    lead = core[0] == 0
-
-    @pl.when(pl.program_id(0) == 0)
-    def _():
-        def put(t, block, row):
-            if t < 36:
-                i, j = (t // 2) % 2, t % 2
-                p = t // 4
-                start = (2 - p % 3) * channels + i * tile
-                weights[2 - p // 3, pl.ds(start + row, half), j * tile : (j + 1) * tile] = block
-
-        place_weights(place, parts, core[0], put)
-
-    column = lax.broadcasted_iota(jnp.int32, (wide, channels), 0)
-    first = column == 0
-    last = column == wide - 1
-    for n in range(batch):
-        lines = []
-        for r in range(height + 2):
-            if r == 0:
-                line = jnp.where(lead, far[n], near[n])
-            elif r == height + 1:
-                line = jnp.where(lead, near[n], far[n])
-            else:
-                line = d_pre[n, r - 1]
-            before, after = shift_lines(line.astype(F32), first, last)
-            lines.append((before, line, after))
-        sides = [jnp.concatenate([l[s] for l in lines], axis=0) for s in range(3)]
-        d_act = None
-        for line in range(3):
-            for side in range(3):
-                window = sides[side][line * wide : line * wide + count]
-                term = dot(window, weights[line, side * channels : (side + 1) * channels, :], NT)
-                d_act = term if d_act is None else d_act + term
-        _, slope = gelu_both(feat[n].reshape(count, channels).astype(F32))
-        total = d_resid[n].reshape(count, channels).astype(F32) + slope * d_act
-        out[n] = total.astype(BF16).reshape(height, wide, channels)
-
-
-def input_call(place, core, feat, d_resid, d_pre, near, far, parts):
-    images, height, wide, channels = feat.shape
-    batch = 5 if images % 5 == 0 else 1
-    smem = pl.BlockSpec(memory_space=pltpu.SMEM)
-    strip = pl.BlockSpec((batch, height, wide, channels), lambda i: (i, 0, 0, 0))
-    line = pl.BlockSpec((batch, wide, channels), lambda i: (i, 0, 0))
-    return pl.pallas_call(
-        lambda *refs: input_kernel(batch, len(parts), *refs),
-        grid=(images // batch,),
-        in_specs=[smem, smem, strip, strip, strip, line, line]
-        + [pl.BlockSpec(p.shape, lambda i: (0, 0, 0)) for p in parts],
-        out_specs=strip,
-        out_shape=jax.ShapeDtypeStruct(feat.shape, BF16),
-        scratch_shapes=[pltpu.VMEM((3, 3 * channels, channels), BF16)],
-        compiler_params=pltpu.CompilerParams(vmem_limit_bytes=VMEM_LIMIT),
-        name="input_grad",
-    )(place, core, feat, d_resid, d_pre, near, far, *parts)
+    )(ids, places, slots, present, present[None], feat, near, far, cot, *parts, proj, dec, code)
 
 
 BLOCK = 32
@@ -356,7 +318,7 @@
     return dot(left, right, dims)
 
 
-def inverse_factors(pairs):
+def inverse_factors(pairs, beside):
     half = 64
     lane = lax.broadcasted_iota(jnp.int32, (8, 128), 1)
     sub = lax.broadcasted_iota(jnp.int32, (8, 128), 0)
@@ -378,6 +340,7 @@
             ]
         )
     for start in range(0, BLOCK, RANK):
+        beside()
         v0, s0 = start // 8, start % 8
         for rows in mats:
             pivots = [jnp.broadcast_to(rows[v0][s0 + i : s0 + i + 1], (8, 128)) for i in range(RANK)]
@@ -419,8 +382,8 @@
     return [jnp.concatenate(rows, axis=0) for rows in mats]
 
 
-def small_update(scale, one, two, arrays, outs):
-    total = one[...].astype(F32) + two[...].astype(F32)
+def small_update(present, shape, sums, arrays, outs):
+    total = jnp.concatenate([sums[q, : sums.shape[1] - LOSS_ROWS] for q in range(4)], axis=0).astype(F32)
     row = 0
     for n, rate in enumerate((PROJ_RATE, DEC_RATE, CODE_RATE)):
         rows, columns = arrays[3 * n].shape
@@ -432,35 +395,50 @@
         new = plain_adam(grad, *(a[...] for a in arrays[3 * n : 3 * n + 3]), rate)
         for out, value in zip(outs[3 * n : 3 * n + 3], new):
             out[...] = value
-    outs[9][...] = jnp.sum(total[row:], axis=(0, 1), keepdims=True) * scale[0]
-
-
-def tile_kernel(*refs):
-    strip, scale = refs[:2]
-    quarters = refs[2:6]
-    master, first, second, left, right, basis_left, basis_right = refs[6:13]
-    one, two = refs[13:15]
-    small_arrays = refs[15:24]
-    (master_new, first_new, second_new, left_new, right_new, basis_left_new, basis_right_new) = refs[
-        24:31
-    ]
-    small_outs = refs[31:41]
-    work, grad_turned = refs[41:]
-    count, tile = master.shape[:2]
-    for d in range(4):
-        quarter = tile // 4
-        row = pl.multiple_of((strip[0] ^ d) * quarter, quarter)
-        grad_turned[:, pl.ds(row, quarter), :] = quarters[d][...]
-    for t in range(count):
-        grad = grad_turned[t]
-        left_new[t] = BETA_TWO * left[t] + (1.0 - BETA_TWO) * dot(grad, grad, TN)
-        right_new[t] = BETA_TWO * right[t] + (1.0 - BETA_TWO) * dot(grad, grad, NT)
-        for side, (stat, basis) in enumerate(((left_new, basis_left), (right_new, basis_right))):
-            moved = dot_exact(split3(stat[t]), split3(basis[t]))
-            turned = moved.T
-            work[2 * t + side, :, :tile] = dot_exact(split3(turned), split3(moved))
-            work[2 * t + side, :, tile:] = turned
-    for t in range(count):
+    loss = sums[0, sums.shape[1] - LOSS_ROWS :].astype(F32)
+    scale = loss_scale(present, 4 * shape[1] * shape[2], arrays[0].shape[0])
+    outs[9][...] = jnp.sum(loss, axis=(0, 1), keepdims=True) * scale
+
+
+def input_units(weights, feat, d_resid, d_pre, near, far, lead, out, done):
+    images, height, wide, channels = feat.shape
+    column = lax.broadcasted_iota(jnp.int32, (wide, channels), 0)
+    first = column == 0
+    last = column == wide - 1
+    count = height * wide
+    for base in range(0, images, 2):
+        group = range(base, base + 2)
+        sides = []
+        for n in group:
+            lines = []
+            for r in range(height + 2):
+                if r == 0:
+                    line = jnp.where(lead, far[n], near[n])
+                elif r == height + 1:
+                    line = jnp.where(lead, near[n], far[n])
+                else:
+                    line = d_pre[n, r - 1]
+                before, after = shift_lines(line.astype(F32), first, last)
+                lines.append((before, line, after))
+            sides.append([jnp.concatenate([l[s] for l in lines], axis=0) for s in range(3)])
+        acts = [None for n in group]
+        for a in range(3):
+            for k in range(len(acts)):
+                window = jnp.concatenate([sides[k][b][a * wide : a * wide + count] for b in range(3)], axis=1)
+                weight = jnp.concatenate([weights[2 - a, (2 - b) * channels : (3 - b) * channels, :] for b in range(3)], axis=1)
+                term = dot(window, weight, NT)
+                acts[k] = term if acts[k] is None else acts[k] + term
+        for k, n in enumerate(group):
+            _, slope = gelu_both(feat[n].reshape(count, channels).astype(F32))
+            total = d_resid[n].reshape(count, channels).astype(F32) + slope * acts[k]
+            out[n] = total.astype(BF16).reshape(height, wide, channels)
+            done(n)
+        yield
+
+
+def adam_units(tiles, grad_turned, first_new, second_new, master_new, small):
+    master, first, second, basis_left, basis_right = tiles
+    for t in range(master.shape[0]):
         one_low = basis_left[t].astype(BF16)
         two_low = basis_right[t].astype(BF16)
         turned = dot(one_low, grad_turned[t], ((0,), (1,)))
@@ -472,14 +450,93 @@
         ratio = mom / (1.0 - BETA_ONE**STEP) / (jnp.sqrt(var / (1.0 - BETA_TWO**STEP)) + EPSILON)
         back = dot(dot(one_low, ratio.astype(BF16)).astype(BF16), two_low, NT)
         master_new[t] = master[t] - TILE_RATE * (back + WEIGHT_DECAY * master[t])
-    small_update(scale, one, two, small_arrays, small_outs)
+        yield
+    small()
+    yield
+
+
+CHUNKS = 4
+
+
+def finish_kernel(*refs):
+    ids, present = refs[:2]
+    quarters = refs[2:6]
+    master, first, second, left, right, basis_left, basis_right = refs[6:13]
+    small_arrays = refs[13:22]
+    loads = refs[22:28]
+    (master_new, first_new, second_new, left_new, right_new, basis_left_new, basis_right_new) = refs[
+        28:35
+    ]
+    small_outs = refs[35:45]
+    input_grad = refs[45]
+    work, grad_turned, small_sums = refs[46:49]
+    held = refs[49:55]
+    out, load_sems, store_sems = refs[55:]
+    count, tile = master.shape[:2]
+    images = out.shape[0]
+    copies = [
+        pltpu.make_async_copy(src, dst, load_sems.at[n]) for n, (src, dst) in enumerate(zip(loads, held))
+    ]
+    for copy in copies:
+        copy.start()
+    for d in range(4):
+        quarter = tile // 4
+        row = pl.multiple_of((ids[0] ^ d) * quarter, quarter)
+        rows = count * quarter
+        grad_turned[:, pl.ds(row, quarter), :] = quarters[d][:rows].reshape(count, quarter, tile)
+        small_sums[ids[0] ^ d] = quarters[d][rows:]
+    for t in range(count):
+        grad = grad_turned[t]
+        left_new[t] = BETA_TWO * left[t] + (1.0 - BETA_TWO) * dot(grad, grad, TN)
+        right_new[t] = BETA_TWO * right[t] + (1.0 - BETA_TWO) * dot(grad, grad, NT)
+        for side, (stat, basis) in enumerate(((left_new, basis_left), (right_new, basis_right))):
+            moved = dot_exact(split3(stat[t]), split3(basis[t]))
+            turned = moved.T
+            work[2 * t + side, :, :tile] = dot_exact(split3(turned), split3(moved))
+            work[2 * t + side, :, tile:] = turned
+    for copy in copies:
+        copy.wait()
+    group = images // CHUNKS if images % CHUNKS == 0 else images
+    stores = []
+
+    def done(n):
+        if n % group == group - 1:
+            part = pl.ds(n + 1 - group, group)
+            sem = store_sems.at[len(stores)]
+            stores.append(pltpu.make_async_copy(out.at[part], input_grad.at[part], sem))
+            stores[-1].start()
+
+    units = [
+        adam_units(
+            (master, first, second, basis_left, basis_right),
+            grad_turned,
+            first_new,
+            second_new,
+            master_new,
+            lambda: small_update(present, out.shape, small_sums, small_arrays, small_outs),
+        ),
+        input_units(*held, lax.rem(ids[0], 2) == 0, out, done),
+    ]
+    total = count + 1 + images // 2
+    slots = tile // RANK
+    used = [0, 0]
+
+    def beside():
+        used[0] += 1
+        while used[1] < total * used[0] // slots:
+            used[1] += 1
+            if next(units[0], True) is not None:
+                units.pop(0)
+                next(units[0])
+
     for low in range(0, tile, BLOCK):
         high = low + BLOCK
         factors = inverse_factors(
             [
                 (work[2 * t, low:high, low:high], work[2 * t + 1, low:high, low:high])
                 for t in range(count)
-            ]
+            ],
+            beside,
         )
         for n in range(2 * count):
             start = (n % 2) * 64 + BLOCK
@@ -494,27 +551,36 @@
     for t in range(count):
         basis_left_new[t] = work[2 * t, :, tile:].T
         basis_right_new[t] = work[2 * t + 1, :, tile:].T
-
-
-def tile_call(strip, scale, quarters, arrays, one, two, small_arrays):
+    for store in stores:
+        store.wait()
+
+
+def finish_call(ids, present, quarters, arrays, small_arrays, loads):
     shape = jax.ShapeDtypeStruct(arrays[0].shape, F32)
     smem = pl.BlockSpec(memory_space=pltpu.SMEM)
     vmem = pl.BlockSpec(memory_space=pltpu.VMEM)
+    hbm = pl.BlockSpec(memory_space=pl.ANY)
     count, tile = shape.shape[:2]
     shapes = [shape] * 7 + [jax.ShapeDtypeStruct(a.shape, F32) for a in small_arrays]
     shapes.append(jax.ShapeDtypeStruct((1, 1), F32))
+    shapes.append(jax.ShapeDtypeStruct(loads[1].shape, BF16))
     return pl.pallas_call(
-        tile_kernel,
-        in_specs=[smem] * 2 + [vmem] * 22,
-        out_specs=[vmem] * 17,
+        finish_kernel,
+        in_specs=[smem] + [vmem] * 21 + [hbm] * len(loads),
+        out_specs=[vmem] * 17 + [hbm],
         out_shape=shapes,
         scratch_shapes=[
             pltpu.VMEM((2 * count, tile, 2 * tile), F32),
             pltpu.VMEM((count, tile, tile), BF16),
+            pltpu.VMEM((4, quarters[0].shape[0] - count * tile // 4, tile), BF16),
+            *(pltpu.VMEM(a.shape, a.dtype) for a in loads),
+            pltpu.VMEM(loads[1].shape, BF16),
+            pltpu.SemaphoreType.DMA((len(loads),)),
+            pltpu.SemaphoreType.DMA((CHUNKS,)),
         ],
-        compiler_params=pltpu.CompilerParams(vmem_limit_bytes=VMEM_LIMIT),
-        name="tile_adam",
-    )(strip, scale, *quarters, *arrays, one, two, *small_arrays)
+        compiler_params=pltpu.CompilerParams(vmem_limit_bytes=FINISH_VMEM),
+        name="finish",
+    )(ids, present[None], *quarters, *arrays, *small_arrays, *loads)
 
 
 def plain_adam(gradient, master, first, second, rate):
@@ -548,19 +614,23 @@
     return swap(near, "strip", 1), lax.ppermute(far, "strip", [(1, 2), (2, 1)])
 
 
-def gather_tiles(mine):
+def gather_tiles(mine, meanwhile):
     core = lax.axis_index("strip") % 2
     half = mine.shape[1] // 2
     part = lax.dynamic_slice_in_dim(mine, core * half, half, axis=1)
-    steps = radices(lax.axis_size("img"))[::-1]
+    *steps, (last, _) = radices(lax.axis_size("img"))[::-1]
     for number, (radix, stride) in enumerate(steps):
         parts = [part] + [swap(part, "img", d * stride) for d in range(1, radix)]
         if number < len(steps) - 1:
             part = jnp.concatenate(parts, axis=0)
-    return parts + [swap(p, "strip", 1) for p in parts]
-
-
-def tile_place(owners, tiles):
+    count = len(parts) // 2
+    pairs = [jnp.concatenate(parts[n * count : (n + 1) * count], axis=0) for n in range(2)]
+    pairs, meanwhile = lax.optimization_barrier((pairs, meanwhile))
+    arrays = [swap(pair, "img", d) if d else pair for d in range(last) for pair in pairs]
+    return arrays + [swap(a, "strip", 1) for a in arrays], meanwhile
+
+
+def tile_places(owners, tiles):
     distance = (owners // tiles) ^ lax.axis_index("img")
     place = jnp.zeros_like(owners)
     size = 1
@@ -570,20 +640,31 @@
     return place * tiles + owners % tiles
 
 
-def reduce_tiles(keep, send, tiles):
+def tree_sum(terms):
+    terms = [t.astype(F32) for t in terms]
+    while len(terms) > 1:
+        terms = [terms[n] + terms[n + 1] for n in range(0, len(terms), 2)]
+    return terms[0]
+
+
+def reduce_all(keep, send, tiles, quarter):
     strip = lax.axis_index("strip")
     across = strip // 2
     img = lax.axis_index("img")
     groups = lax.axis_size("img")
     (radix, _), *later = radices(groups)
+    low = img % radix
+    size = tiles * quarter
+    columns = keep.shape[-1]
     part = keep + swap(send, "strip", 1)
-    part = part.reshape(2, groups // radix, radix, -1, part.shape[-1])
-    low = img % radix
-    total = None
+    left = groups // radix
+    terms = []
     for d in range(2):
         for e in range(radix):
-            piece = lax.dynamic_index_in_dim(part, across ^ d, 0, False)
-            piece = lax.dynamic_index_in_dim(piece, low ^ e, 1, False)
+            both = lax.dynamic_index_in_dim(part, across ^ d, 0, False)
+            piece = both[: groups * size].reshape(left, radix, size, columns)
+            piece = lax.dynamic_index_in_dim(piece, low ^ e, 1, False).reshape(left * size, columns)
+            piece = jnp.concatenate([piece, both[groups * size :]], axis=0)
             if d or e:
                 pairs = [
                     (a * groups + b, (a ^ (2 * d)) * groups + (b ^ e))
@@ -591,30 +672,20 @@
                     for b in range(groups)
                 ]
                 piece = lax.ppermute(piece, ("strip", "img"), pairs)
-            piece = piece.astype(F32)
-            total = piece if total is None else total + piece
-    left = groups // radix
+            terms.append(piece)
+    total = tree_sum(terms).astype(BF16)
     for radix, stride in later:
-        part = total.astype(BF16).reshape(left // radix, radix, *total.shape[-2:])
         low = (img // stride) % radix
-        total = lax.dynamic_index_in_dim(part, low, 1, False).astype(F32)
-        for d in range(1, radix):
-            piece = lax.dynamic_index_in_dim(part, low ^ d, 1, False)
-            total = total + swap(piece, "img", d * stride).astype(F32)
+        terms = []
+        for d in range(radix):
+            piece = total[: left * size].reshape(left // radix, radix, size, columns)
+            piece = lax.dynamic_index_in_dim(piece, low ^ d, 1, False)
+            piece = piece.reshape(left // radix * size, columns)
+            piece = jnp.concatenate([piece, total[left * size :]], axis=0)
+            terms.append(swap(piece, "img", d * stride) if d else piece)
+        total = tree_sum(terms).astype(BF16)
         left //= radix
-    total = total.astype(BF16).reshape(tiles, -1, total.shape[-1])
     return [total] + [swap(total, "strip", d) for d in range(1, 4)]
-
-
-def reduce_small(small):
-    steps = [("strip", 1), ("strip", 2)]
-    for radix, stride in radices(lax.axis_size("img")):
-        steps += [("img", stride << n) for n in range(radix.bit_length() - 1)]
-    for number, (axis, distance) in enumerate(steps):
-        other = swap(small, axis, distance)
-        if number == len(steps) - 1:
-            return small, other
-        small = (small.astype(F32) + other.astype(F32)).astype(BF16)
 
 
 def body(
@@ -644,44 +715,32 @@
     img = lax.axis_index("img")
     strip = lax.axis_index("strip")
     core = strip % 2
-    parts = gather_tiles(tile_master.astype(BF16))
-    place = tile_place(owners, tiles)
-    alive = lax.dynamic_slice_in_dim(present, img * images, images).astype(F32)
-    count = jnp.sum(present).astype(F32) * (height * lax.axis_size("strip") * wide)
-    latent = proj_master.shape[1]
-    scale = LOSS_WEIGHT / (count * latent)
-    code_low = code_master.T.astype(BF16)
-    code_full = code_low.astype(F32)
-    norms = jnp.sum(code_full * code_full, axis=0)[None] / SOFTMAX_WARMTH
+    ids = jnp.stack([strip, img]).astype(jnp.int32)
+    ready = (ids, tile_places(owners, tiles))
+    parts, (ids, places) = gather_tiles(tile_master.astype(BF16), ready)
     top, bottom = features[:, 0], features[:, height - 1]
     near, far = swap_edges(jnp.where(core == 0, bottom, top), jnp.where(core == 0, top, bottom))
-    (decoded, d_pre, d_resid, near_out, far_out, keep, send, small) = main_call(
-        place,
+    (decoded, d_pre, d_resid, near_out, far_out, weights, keep, send) = main_call(
+        ids,
+        places,
         owners,
-        alive,
-        2.0 * scale * alive,
-        core.reshape(1),
+        present,
         features,
         near,
         far,
         cotangent,
         parts,
-        proj_master.T.astype(BF16),
-        dec_master.astype(BF16),
-        code_low,
-        norms,
+        proj_master.T,
+        dec_master,
+        code_master.T,
     )
     near, far = swap_edges(near_out, far_out)
-    one, two = reduce_small(small)
-    input_grad = input_call(place, core.reshape(1), features, d_resid, d_pre, near, far, parts)
-    quarters = reduce_tiles(keep, send, tiles)
-    out = tile_call(
-        strip.reshape(1),
-        scale.reshape(1),
+    quarters = reduce_all(keep, send, tiles, tile_master.shape[1] // 4)
+    out = finish_call(
+        ids,
+        present,
         quarters,
         [tile_master, tile_mom1, tile_mom2, stat_left, stat_right, basis_left, basis_right],
-        one,
-        two,
         [
             proj_master.T,
             proj_mom1.T,
@@ -693,9 +752,10 @@
             code_mom1.T,
             code_mom2.T,
         ],
+        [weights, features, d_resid, d_pre, near, far],
     )
     small = [a.T for a in out[7:10]] + list(out[10:13]) + [a.T for a in out[13:16]]
-    return (decoded, input_grad, out[16].reshape(()), *out[:7], *small)
+    return (decoded, out[17], out[16].reshape(()), *out[:7], *small)
 
 
 def solution(mesh):

time: 133 us -> 120 us (0.902)
  waiting for transfers between devices: 21.2 us -> 32.8 us
  starting transfers between devices: 28.2 us -> 19.9 us
  other arithmetic: 12.5 us -> 4.45 us
  Pallas kernels: 65.2 us -> 59.2 us
    ppermute x20 -> x18, waiting for transfers between devices: 13.5 us -> 23.8 us  [swap(): return lax.ppermute(x, axis, [(i, i ^ distance) for i in range(count)])]
    ppermute x20 -> x18, starting transfers between devices: 22 us -> 14.9 us  [swap(): return lax.ppermute(x, axis, [(i, i ^ distance) for i in range(count)])]
    pallas_call x2 -> x1, Pallas kernels: 28.3 us -> 21.4 us  [finish_call(): pl.pallas_call(finish_kernel, in_specs=[smem] + [vmem] * 21 + [hbm] * len...]
    convert_element_type x8 -> x2, other arithmetic: 4.11 us -> 0.15 us  [reduce_all(): total = tree_sum(terms).astype(BF16)]
    reduce_sum x2 -> x0, other arithmetic: 2.86 us -> none  [the longest x1 1.55 us: body(): norms = jnp.sum(code_full * code_full, axis=0)[None] / SOFTMAX_WARMTH]
  transfers between devices with their start and end apart: 25 -> 23, of which waited for: 8 -> 12; matrix products, arithmetic and copies ran while one was open for 9% -> 3% of each run, Pallas kernels for 10% -> 0%
where the time goes in v4:
time: 120 us
  Pallas kernels  59.2 us (49%)
  waiting for transfers between devices  32.8 us (27%)
  starting transfers between devices  19.9 us (17%)
  other arithmetic  4.45 us (4%)
  local copies, waits for them, and re-layouts  2.44 us (2%)
  between operations  1.21 us (1%)
    pallas_call x1, Pallas kernels, main_call(): pl.pallas_call(lambda *refs: main_kernel(batch, len(parts), *refs), grid=...  37.9 us
    ppermute x18, waiting for transfers between devices, swap(): return lax.ppermute(x, axis, [(i, i ^ distance) for i in range(count)])  23.8 us
    pallas_call x1, Pallas kernels, finish_call(): pl.pallas_call(finish_kernel, in_specs=[smem] + [vmem] * 21 + [hbm] * len...  21.4 us
    ppermute x18, starting transfers between devices, swap(): return lax.ppermute(x, axis, [(i, i ^ distance) for i in range(count)])  14.9 us
    ppermute x3, waiting for transfers between devices, reduce_all(): piece = lax.ppermute(piece, ('strip', 'img'), pairs)  9.03 us
    ppermute x3, starting transfers between devices, reduce_all(): piece = lax.ppermute(piece, ('strip', 'img'), pairs)  3.62 us
  transfers between devices with their start and end apart: 23, of which 12 were waited for; matrix products, arithmetic and copies ran while one was open for 3% of the time, Pallas kernels for 0%

profile of v4, /device:TPU:0, one launch (start us, length us, event | category | flops | bytes accessed | tf_op | source)
XLA Modules:
  0.0 120.0 jit_solution(3956629198191645765)
XLA Ops:
  1.6 4.1 %collective-permute-start.1 = (bf16[5,64,128]{2,1,0:T(8,128)(2,1)S(1)}, bf16[5,64,128]{2,1,0:T(8,128)(2,1)S(1)}, u32[]{:S(2)}, u32[]{:S(2)}) collective-permute-start(bf16[5,64,128]{2,1,0:T(8,128)(2,1)S(1)} %dynamic-slice_convert_fusion), channel_id=1, source_target_pairs={{0,4},{1,5},{2,6},{3,7},{4,0},{5,1},{6,2},{7,3},{8,12},{9,13},{10,... | collective-permute-start | bytes 245768 | tf_op jit(solution)/shard_map/ppermute | solution.py:599
  5.7 1.6 %collective-permute-start = (bf16[5,64,128]{2,1,0:T(8,128)(2,1)S(1)}, bf16[5,64,128]{2,1,0:T(8,128)(2,1)S(1)}, u32[]{:S(2)}, u32[]{:S(2)}) collective-permute-start(bf16[5,64,128]{2,1,0:T(8,128)(2,1)S(1)} %dynamic-slice_convert_fusion), channel_id=1, source_target_pairs={{0,2},{1,3},{2,0},{3,1},{4,6},{5,7},{6,4},{7,5},{8,10},{9,11},{10,... | collective-permute-start | bytes 245768 | tf_op jit(solution)/shard_map/ppermute | solution.py:599
  7.3 1.1 fusion.1
  9.1 1.2 fusion.3.refs_1_
  10.9 2.6 %collective-permute-done.2 = bf16[5,64,128]{2,1,0:T(8,128)(2,1)S(1)} collective-permute-done((bf16[5,64,128]{2,1,0:T(8,128)(2,1)S(1)}, bf16[5,64,128]{2,1,0:T(8,128)(2,1)S(1)}, u32[]{:S(2)}, u32[]{:S(2)}) %collective-permute-start.2) | collective-permute-done | bytes 81952 | tf_op jit(solution)/shard_map/ppermute | solution.py:599
  14.2 1.6 %collective-permute-start.5 = (bf16[10,64,128]{2,1,0:T(8,128)(2,1)S(1)}, bf16[10,64,128]{2,1,0:T(8,128)(2,1)S(1)}, u32[]{:S(2)}, u32[]{:S(2)}) collective-permute-start(bf16[10,64,128]{2,1,0:T(8,128)(2,1)S(1)} %pad_maximum_fusion.4.refs_9_), channel_id=1, source_target_pairs={{0,1},{1,0},{2,3},{3,2},{4,5},{5,4},{6,7},{7,6},{8,9},{9,8},{10,11... | collective-permute-start | bytes 491528 | tf_op jit(solution)/shard_map/ppermute | solution.py:599
  16.2 5.0 %collective-permute-done.5.refs_11_ = bf16[10,64,128]{2,1,0:T(8,128)(2,1)S(1)} collective-permute-done((bf16[10,64,128]{2,1,0:T(8,128)(2,1)S(1)}, bf16[10,64,128]{2,1,0:T(8,128)(2,1)S(1)}, u32[]{:S(2)}, u32[]{:S(2)}) %collective-permute-start.5) | collective-permute-done | bytes 163872 | tf_op jit(solution)/shard_map/ppermute | solution.py:599
  21.2 3.1 %collective-permute-done.6.refs_12_ = bf16[10,64,128]{2,1,0:T(8,128)(2,1)S(1)} collective-permute-done((bf16[10,64,128]{2,1,0:T(8,128)(2,1)S(1)}, bf16[10,64,128]{2,1,0:T(8,128)(2,1)S(1)}, u32[]{:S(2)}, u32[]{:S(2)}) %collective-permute-start.6) | collective-permute-done | bytes 163872 | tf_op jit(solution)/shard_map/ppermute | solution.py:599
  24.3 1.3 %collective-permute-done.10.refs_16_ = bf16[10,64,128]{2,1,0:T(8,128)(2,1)S(1)} collective-permute-done((bf16[10,64,128]{2,1,0:T(8,128)(2,1)S(1)}, bf16[10,64,128]{2,1,0:T(8,128)(2,1)S(1)}, u32[]{:S(2)}, u32[]{:S(2)}) %collective-permute-start.10) | collective-permute-done | bytes 163872 | tf_op jit(solution)/shard_map/ppermute | solution.py:599
  26.3 37.9 %main.1 = (bf16[20,8,32,256]{3,2,1,0:T(8,128)(2,1)}, bf16[20,8,32,256]{3,2,1,0:T(8,128)(2,1)}, bf16[20,8,32,256]{3,2,1,0:T(8,128)(2,1)}, bf16[20,32,256]{2,1,0:T...) custom-call(s32[2]{0:T(128)} %pad_add_fusion.refs_0_, ...), custom_call_target="tpu_custom_call" | custom-call | tf_op jit(solution)/shard_map/main/pallas_call | solution.py:274
  64.4 2.3 %collective-permute-done.11 = bf16[2,1424,128]{2,1,0:T(8,128)(2,1)S(1)} collective-permute-done((bf16[2,1424,128]{2,1,0:T(8,128)(2,1)}, bf16[2,1424,128]{2,1,0:T(8,128)(2,1)S(1)}, u32[]{:S(2)}, u32[]{:S(2)}) %collective-permute-start.11) | collective-permute-done | bytes 729120 | tf_op jit(solution)/shard_map/ppermute | solution.py:599
  66.7 1.3 %add.98 = bf16[2,1424,128]{2,1,0:T(8,128)(2,1)S(1)} add(bf16[2,1424,128]{2,1,0:T(8,128)(2,1)} %get-tuple-element.54, bf16[2,1424,128]{2,1,0:T(8,128)(2,1)S(1)} %collective-permute-done.11) | non-fusion elementwise | flops 364544 | bytes 2187264 | tf_op jit(solution)/shard_map/add | solution.py:659
  68.2 1.6 %collective-permute-start.12 = (bf16[784,128]{1,0:T(8,128)(2,1)S(1)}, bf16[784,128]{1,0:T(8,128)(2,1)S(1)}, u32[]{:S(2)}, u32[]{:S(2)}) collective-permute-start(bf16[784,128]{1,0:T(8,128)(2,1)S(1)} %pad_maximum_fusion), channel_id=1, source_target_pairs={{0,1},{1,0},{2,3},{3,2},{4,5},{5,4},{6,7},{7,6},{8,9},{9,8},{10,11... | collective-permute-start | bytes 602120 | tf_op jit(solution)/shard_map/ppermute | solution.py:674
  69.8 1.2 %collective-permute-start.13 = (bf16[784,128]{1,0:T(8,128)(2,1)S(1)}, bf16[784,128]{1,0:T(8,128)(2,1)S(1)}, u32[]{:S(2)}, u32[]{:S(2)}) collective-permute-start(bf16[784,128]{1,0:T(8,128)(2,1)S(1)} %get-tuple-element.96), channel_id=1, source_target_pairs={{0,16},{1,17},{2,18},{3,19},{4,20},{5,21},{6,22},{7,23},{8,24},{9,... | collective-permute-start | bytes 602120 | tf_op jit(solution)/shard_map/ppermute | solution.py:674
  71.9 3.4 %collective-permute-done.12 = bf16[784,128]{1,0:T(8,128)(2,1)S(1)} collective-permute-done((bf16[784,128]{1,0:T(8,128)(2,1)S(1)}, bf16[784,128]{1,0:T(8,128)(2,1)S(1)}, u32[]{:S(2)}, u32[]{:S(2)}) %collective-permute-start.12) | collective-permute-done | bytes 200736 | tf_op jit(solution)/shard_map/ppermute | solution.py:674
  75.3 2.4 %collective-permute-done.13 = bf16[784,128]{1,0:T(8,128)(2,1)S(1)} collective-permute-done((bf16[784,128]{1,0:T(8,128)(2,1)S(1)}, bf16[784,128]{1,0:T(8,128)(2,1)S(1)}, u32[]{:S(2)}, u32[]{:S(2)}) %collective-permute-start.13) | collective-permute-done | bytes 200736 | tf_op jit(solution)/shard_map/ppermute | solution.py:674
  77.7 3.1 %collective-permute-done.14 = bf16[784,128]{1,0:T(8,128)(2,1)S(1)} collective-permute-done((bf16[784,128]{1,0:T(8,128)(2,1)S(1)}, bf16[784,128]{1,0:T(8,128)(2,1)S(1)}, u32[]{:S(2)}, u32[]{:S(2)}) %collective-permute-start.14) | collective-permute-done | bytes 200736 | tf_op jit(solution)/shard_map/ppermute | solution.py:674
  81.8 3.5 %collective-permute-start.16 = (bf16[304,128]{1,0:T(8,128)(2,1)S(1)}, bf16[304,128]{1,0:T(8,128)(2,1)S(1)}, u32[]{:S(2)}, u32[]{:S(2)}) collective-permute-start(bf16[304,128]{1,0:T(8,128)(2,1)S(1)} %get-tuple-element.94), channel_id=1, source_target_pairs={{0,4},{1,5},{2,6},{3,7},{4,0},{5,1},{6,2},{7,3},{8,12},{9,13},{10,... | collective-permute-start | bytes 233480 | tf_op jit(solution)/shard_map/ppermute | solution.py:599
  86.3 3.6 %collective-permute-done.16 = bf16[304,128]{1,0:T(8,128)(2,1)S(1)} collective-permute-done((bf16[304,128]{1,0:T(8,128)(2,1)S(1)}, bf16[304,128]{1,0:T(8,128)(2,1)S(1)}, u32[]{:S(2)}, u32[]{:S(2)}) %collective-permute-start.16) | collective-permute-done | bytes 77856 | tf_op jit(solution)/shard_map/ppermute | solution.py:599
  89.9 1.7 %collective-permute-done.17 = bf16[304,128]{1,0:T(8,128)(2,1)S(1)} collective-permute-done((bf16[304,128]{1,0:T(8,128)(2,1)S(1)}, bf16[304,128]{1,0:T(8,128)(2,1)S(1)}, u32[]{:S(2)}, u32[]{:S(2)}) %collective-permute-start.17) | collective-permute-done | bytes 77856 | tf_op jit(solution)/shard_map/ppermute | solution.py:599
  92.1 1.4 %collective-permute-start.18 = (bf16[304,128]{1,0:T(8,128)(2,1)S(1)}, bf16[304,128]{1,0:T(8,128)(2,1)S(1)}, u32[]{:S(2)}, u32[]{:S(2)}) collective-permute-start(bf16[304,128]{1,0:T(8,128)(2,1)S(1)} %add_convert_fusion.1.refs_2_), channel_id=1, source_target_pairs={{0,8},{8,0},{16,24},{24,16},{1,9},{9,1},{17,25},{25,17},{2,10},{10... | collective-permute-start | bytes 233480 | tf_op jit(solution)/shard_map/ppermute | solution.py:599
  93.6 2.8 %collective-permute-done.20.refs_5_ = bf16[304,128]{1,0:T(8,128)(2,1)S(1)} collective-permute-done((bf16[304,128]{1,0:T(8,128)(2,1)S(1)}, bf16[304,128]{1,0:T(8,128)(2,1)S(1)}, u32[]{:S(2)}, u32[]{:S(2)}) %collective-permute-start.20) | collective-permute-done | bytes 77856 | tf_op jit(solution)/shard_map/ppermute | solution.py:599
  96.4 1.4 %collective-permute-done.19.refs_4_ = bf16[304,128]{1,0:T(8,128)(2,1)S(1)} collective-permute-done((bf16[304,128]{1,0:T(8,128)(2,1)S(1)}, bf16[304,128]{1,0:T(8,128)(2,1)S(1)}, u32[]{:S(2)}, u32[]{:S(2)}) %collective-permute-start.19) | collective-permute-done | bytes 77856 | tf_op jit(solution)/shard_map/ppermute | solution.py:599
  98.5 21.4 %finish.1 = (f32[5,128,128]{2,1,0:T(8,128)}, f32[5,128,128]{2,1,0:T(8,128)}, f32[5,128,128]{2,1,0:T(8,128)}, f32[5,128,128]{2,1,0:T(8,128)}, f32[5,128,128]{2,1,...) custom-call(s32[2]{0:T(128)} %pad_add_fusion.refs_0_, ...), custom_call_target="tpu_custom_call" | custom-call | tf_op jit(solution)/shard_map/finish/pallas_call | solution.py:567
  (78 shorter events, 8.2 us)
Async XLA Ops:
  1.6 9.3 %collective-permute-start.1 = (bf16[5,64,128]{2,1,0:T(8,128)(2,1)S(1)}, bf16[5,64,128]{2,1,0:T(8,128)(2,1)S(1)}, u32[]{:S(2)}, u32[]{:S(2)}) collective-permute-start(bf16[5,64,128]{2,1,0:T(8,128)(2,1)S(1)} %dynamic-slice_convert_fusion), channel_id=1, source_target_pairs={{0,4},{1,5},{2,6},{3,7},{4,0},{5,1},{6,2},{7,3},{8,12},{9,13},{10,... | collective-permute-start | bytes 245768 | tf_op jit(solution)/shard_map/ppermute | solution.py:599
  5.7 5.2 %collective-permute-start = (bf16[5,64,128]{2,1,0:T(8,128)(2,1)S(1)}, bf16[5,64,128]{2,1,0:T(8,128)(2,1)S(1)}, u32[]{:S(2)}, u32[]{:S(2)}) collective-permute-start(bf16[5,64,128]{2,1,0:T(8,128)(2,1)S(1)} %dynamic-slice_convert_fusion), channel_id=1, source_target_pairs={{0,2},{1,3},{2,0},{3,1},{4,6},{5,7},{6,4},{7,5},{8,10},{9,11},{10,... | collective-permute-start | bytes 245768 | tf_op jit(solution)/shard_map/ppermute | solution.py:599
  7.3 6.2 %collective-permute-start.2 = (bf16[5,64,128]{2,1,0:T(8,128)(2,1)S(1)}, bf16[5,64,128]{2,1,0:T(8,128)(2,1)S(1)}, u32[]{:S(2)}, u32[]{:S(2)}) collective-permute-start(bf16[5,64,128]{2,1,0:T(8,128)(2,1)S(1)} %dynamic-slice_convert_fusion), channel_id=1, source_target_pairs={{0,6},{1,7},{2,4},{3,5},{4,2},{5,3},{6,0},{7,1},{8,14},{9,15},{10,... | collective-permute-start | bytes 245768 | tf_op jit(solution)/shard_map/ppermute | solution.py:599
  8.4 15.8 %collective-permute-start.4 = (bf16[20,32,256]{2,1,0:T(8,128)(2,1)S(1)}, bf16[20,32,256]{2,1,0:T(8,128)(2,1)S(1)}, u32[]{:S(2)}, u32[]{:S(2)}) collective-permute-start(bf16[20,32,256]{2,1,0:T(8,128)(2,1)S(1)} %get-tuple-element.79), channel_id=1, source_target_pairs={{8,16},{16,8},{9,17},{17,9},{10,18},{18,10},{11,19},{19,11},{12,20... | collective-permute-start | bytes 983048 | tf_op jit(solution)/shard_map/ppermute | solution.py:614
  13.6 2.6 %collective-permute-start.7 = (bf16[10,64,128]{2,1,0:T(8,128)(2,1)S(1)}, bf16[10,64,128]{2,1,0:T(8,128)(2,1)S(1)}, u32[]{:S(2)}, u32[]{:S(2)}) collective-permute-start(bf16[10,64,128]{2,1,0:T(8,128)(2,1)S(1)} %pad_maximum_fusion.4.refs_9_), channel_id=1, source_target_pairs={{0,8},{8,0},{16,24},{24,16},{1,9},{9,1},{17,25},{25,17},{2,10},{10... | collective-permute-start | bytes 491528 | tf_op jit(solution)/shard_map/ppermute | solution.py:599
  14.1 10.2 %collective-permute-start.3 = (bf16[20,32,256]{2,1,0:T(8,128)(2,1)S(1)}, bf16[20,32,256]{2,1,0:T(8,128)(2,1)S(1)}, u32[]{:S(2)}, u32[]{:S(2)}) collective-permute-start(bf16[20,32,256]{2,1,0:T(8,128)(2,1)S(1)} %get-tuple-element.80), channel_id=1, source_target_pairs={{0,8},{8,0},{16,24},{24,16},{1,9},{9,1},{17,25},{25,17},{2,10},{10... | collective-permute-start | bytes 983048 | tf_op jit(solution)/shard_map/ppermute | solution.py:599
  14.2 7.0 %collective-permute-start.5 = (bf16[10,64,128]{2,1,0:T(8,128)(2,1)S(1)}, bf16[10,64,128]{2,1,0:T(8,128)(2,1)S(1)}, u32[]{:S(2)}, u32[]{:S(2)}) collective-permute-start(bf16[10,64,128]{2,1,0:T(8,128)(2,1)S(1)} %pad_maximum_fusion.4.refs_9_), channel_id=1, source_target_pairs={{0,1},{1,0},{2,3},{3,2},{4,5},{5,4},{6,7},{7,6},{8,9},{9,8},{10,11... | collective-permute-start | bytes 491528 | tf_op jit(solution)/shard_map/ppermute | solution.py:599
  15.8 8.5 %collective-permute-start.6 = (bf16[10,64,128]{2,1,0:T(8,128)(2,1)S(1)}, bf16[10,64,128]{2,1,0:T(8,128)(2,1)S(1)}, u32[]{:S(2)}, u32[]{:S(2)}) collective-permute-start(bf16[10,64,128]{2,1,0:T(8,128)(2,1)S(1)} %pad_maximum_fusion.5.refs_10_), channel_id=1, source_target_pairs={{0,1},{1,0},{2,3},{3,2},{4,5},{5,4},{6,7},{7,6},{8,9},{9,8},{10,11... | collective-permute-start | bytes 491528 | tf_op jit(solution)/shard_map/ppermute | solution.py:599
  16.2 8.0 %collective-permute-start.8 = (bf16[10,64,128]{2,1,0:T(8,128)(2,1)S(1)}, bf16[10,64,128]{2,1,0:T(8,128)(2,1)S(1)}, u32[]{:S(2)}, u32[]{:S(2)}) collective-permute-start(bf16[10,64,128]{2,1,0:T(8,128)(2,1)S(1)} %pad_maximum_fusion.5.refs_10_), channel_id=1, source_target_pairs={{0,8},{8,0},{16,24},{24,16},{1,9},{9,1},{17,25},{25,17},{2,10},{10... | collective-permute-start | bytes 491528 | tf_op jit(solution)/shard_map/ppermute | solution.py:599
  21.2 3.1 %collective-permute-start.9 = (bf16[10,64,128]{2,1,0:T(8,128)(2,1)S(1)}, bf16[10,64,128]{2,1,0:T(8,128)(2,1)S(1)}, u32[]{:S(2)}, u32[]{:S(2)}) collective-permute-start(bf16[10,64,128]{2,1,0:T(8,128)(2,1)S(1)} %collective-permute-done.5.refs_11_), channel_id=1, source_target_pairs={{0,8},{8,0},{16,24},{24,16},{1,9},{9,1},{17,25},{25,17},{2,10},{10... | collective-permute-start | bytes 491528 | tf_op jit(solution)/shard_map/ppermute | solution.py:599
  24.2 1.4 %collective-permute-start.10 = (bf16[10,64,128]{2,1,0:T(8,128)(2,1)S(1)}, bf16[10,64,128]{2,1,0:T(8,128)(2,1)S(1)}, u32[]{:S(2)}, u32[]{:S(2)}) collective-permute-start(bf16[10,64,128]{2,1,0:T(8,128)(2,1)S(1)} %collective-permute-done.6.refs_12_), channel_id=1, source_target_pairs={{0,8},{8,0},{16,24},{24,16},{1,9},{9,1},{17,25},{25,17},{2,10},{10... | collective-permute-start | bytes 491528 | tf_op jit(solution)/shard_map/ppermute | solution.py:599
  64.2 2.5 %collective-permute-start.11 = (bf16[2,1424,128]{2,1,0:T(8,128)(2,1)}, bf16[2,1424,128]{2,1,0:T(8,128)(2,1)S(1)}, u32[]{:S(2)}, u32[]{:S(2)}) collective-permute-start(bf16[2,1424,128]{2,1,0:T(8,128)(2,1)} %get-tuple-element.55), channel_id=1, source_target_pairs={{0,8},{8,0},{16,24},{24,16},{1,9},{9,1},{17,25},{25,17},{2,10},{10... | collective-permute-start | bytes 2187272 | tf_op jit(solution)/shard_map/ppermute | solution.py:599
  68.1 17.5 %copy-start.17 = (bf16[20,32,256]{2,1,0:T(8,128)(2,1)S(1)}, bf16[20,32,256]{2,1,0:T(8,128)(2,1)}, u32[]{:S(2)}) copy-start(bf16[20,32,256]{2,1,0:T(8,128)(2,1)} %get-tuple-element.59) | copy-start | bytes 983044
  68.2 7.1 %collective-permute-start.12 = (bf16[784,128]{1,0:T(8,128)(2,1)S(1)}, bf16[784,128]{1,0:T(8,128)(2,1)S(1)}, u32[]{:S(2)}, u32[]{:S(2)}) collective-permute-start(bf16[784,128]{1,0:T(8,128)(2,1)S(1)} %pad_maximum_fusion), channel_id=1, source_target_pairs={{0,1},{1,0},{2,3},{3,2},{4,5},{5,4},{6,7},{7,6},{8,9},{9,8},{10,11... | collective-permute-start | bytes 602120 | tf_op jit(solution)/shard_map/ppermute | solution.py:674
  69.8 7.9 %collective-permute-start.13 = (bf16[784,128]{1,0:T(8,128)(2,1)S(1)}, bf16[784,128]{1,0:T(8,128)(2,1)S(1)}, u32[]{:S(2)}, u32[]{:S(2)}) collective-permute-start(bf16[784,128]{1,0:T(8,128)(2,1)S(1)} %get-tuple-element.96), channel_id=1, source_target_pairs={{0,16},{1,17},{2,18},{3,19},{4,20},{5,21},{6,22},{7,23},{8,24},{9,... | collective-permute-start | bytes 602120 | tf_op jit(solution)/shard_map/ppermute | solution.py:674
  71.0 9.9 %collective-permute-start.14 = (bf16[784,128]{1,0:T(8,128)(2,1)S(1)}, bf16[784,128]{1,0:T(8,128)(2,1)S(1)}, u32[]{:S(2)}, u32[]{:S(2)}) collective-permute-start(bf16[784,128]{1,0:T(8,128)(2,1)S(1)} %get-tuple-element.97), channel_id=1, source_target_pairs={{0,17},{1,16},{2,19},{3,18},{4,21},{5,20},{6,23},{7,22},{8,25},{9,... | collective-permute-start | bytes 602120 | tf_op jit(solution)/shard_map/ppermute | solution.py:674
  81.1 5.2 %collective-permute-start.15 = (bf16[304,128]{1,0:T(8,128)(2,1)S(1)}, bf16[304,128]{1,0:T(8,128)(2,1)S(1)}, u32[]{:S(2)}, u32[]{:S(2)}) collective-permute-start(bf16[304,128]{1,0:T(8,128)(2,1)S(1)} %get-tuple-element.93), channel_id=1, source_target_pairs={{0,2},{1,3},{2,0},{3,1},{4,6},{5,7},{6,4},{7,5},{8,10},{9,11},{10,... | collective-permute-start | bytes 233480 | tf_op jit(solution)/shard_map/ppermute | solution.py:599
  81.8 8.1 %collective-permute-start.16 = (bf16[304,128]{1,0:T(8,128)(2,1)S(1)}, bf16[304,128]{1,0:T(8,128)(2,1)S(1)}, u32[]{:S(2)}, u32[]{:S(2)}) collective-permute-start(bf16[304,128]{1,0:T(8,128)(2,1)S(1)} %get-tuple-element.94), channel_id=1, source_target_pairs={{0,4},{1,5},{2,6},{3,7},{4,0},{5,1},{6,2},{7,3},{8,12},{9,13},{10,... | collective-permute-start | bytes 233480 | tf_op jit(solution)/shard_map/ppermute | solution.py:599
  85.3 6.2 %collective-permute-start.17 = (bf16[304,128]{1,0:T(8,128)(2,1)S(1)}, bf16[304,128]{1,0:T(8,128)(2,1)S(1)}, u32[]{:S(2)}, u32[]{:S(2)}) collective-permute-start(bf16[304,128]{1,0:T(8,128)(2,1)S(1)} %get-tuple-element.95), channel_id=1, source_target_pairs={{0,6},{1,7},{2,4},{3,5},{4,2},{5,3},{6,0},{7,1},{8,14},{9,15},{10,... | collective-permute-start | bytes 233480 | tf_op jit(solution)/shard_map/ppermute | solution.py:599
  85.5 8.0 %collective-permute-start.21 = (bf16[20,32,256]{2,1,0:T(8,128)(2,1)S(1)}, bf16[20,32,256]{2,1,0:T(8,128)(2,1)S(1)}, u32[]{:S(2)}, u32[]{:S(2)}) collective-permute-start(bf16[20,32,256]{2,1,0:T(8,128)(2,1)S(1)} %copy-done.17), channel_id=1, source_target_pairs={{0,8},{8,0},{16,24},{24,16},{1,9},{9,1},{17,25},{25,17},{2,10},{10... | collective-permute-start | bytes 983048 | tf_op jit(solution)/shard_map/ppermute | solution.py:599
  85.6 8.0 %collective-permute-start.22 = (bf16[20,32,256]{2,1,0:T(8,128)(2,1)S(1)}, bf16[20,32,256]{2,1,0:T(8,128)(2,1)S(1)}, u32[]{:S(2)}, u32[]{:S(2)}) collective-permute-start(bf16[20,32,256]{2,1,0:T(8,128)(2,1)S(1)} %copy-done.16), channel_id=1, source_target_pairs={{8,16},{16,8},{9,17},{17,9},{10,18},{18,10},{11,19},{19,11},{12,20... | collective-permute-start | bytes 983048 | tf_op jit(solution)/shard_map/ppermute | solution.py:614
  91.6 4.8 %collective-permute-start.20 = (bf16[304,128]{1,0:T(8,128)(2,1)S(1)}, bf16[304,128]{1,0:T(8,128)(2,1)S(1)}, u32[]{:S(2)}, u32[]{:S(2)}) collective-permute-start(bf16[304,128]{1,0:T(8,128)(2,1)S(1)} %add_convert_fusion.1.refs_2_), channel_id=1, source_target_pairs={{0,24},{8,16},{16,8},{24,0},{1,25},{9,17},{17,9},{25,1},{2,26},{10... | collective-permute-start | bytes 233480 | tf_op jit(solution)/shard_map/ppermute | solution.py:599
  91.7 6.1 %collective-permute-start.19 = (bf16[304,128]{1,0:T(8,128)(2,1)S(1)}, bf16[304,128]{1,0:T(8,128)(2,1)S(1)}, u32[]{:S(2)}, u32[]{:S(2)}) collective-permute-start(bf16[304,128]{1,0:T(8,128)(2,1)S(1)} %add_convert_fusion.1.refs_2_), channel_id=1, source_target_pairs={{0,16},{8,24},{16,0},{24,8},{1,17},{9,25},{17,1},{25,9},{2,18},{10... | collective-permute-start | bytes 233480 | tf_op jit(solution)/shard_map/ppermute | solution.py:599
  92.1 5.7 %collective-permute-start.18 = (bf16[304,128]{1,0:T(8,128)(2,1)S(1)}, bf16[304,128]{1,0:T(8,128)(2,1)S(1)}, u32[]{:S(2)}, u32[]{:S(2)}) collective-permute-start(bf16[304,128]{1,0:T(8,128)(2,1)S(1)} %add_convert_fusion.1.refs_2_), channel_id=1, source_target_pairs={{0,8},{8,0},{16,24},{24,16},{1,9},{9,1},{17,25},{25,17},{2,10},{10... | collective-permute-start | bytes 233480 | tf_op jit(solution)/shard_map/ppermute | solution.py:599
  (17 other events, 83.5 us)

commit v5 on v4

--- a/solution.py
+++ b/solution.py
@@ -88,13 +88,13 @@
     present_row, feat, near, far, cot = refs[4:9]
     parts = refs[9 : 9 + part_count]
     proj_full, dec_full, code_full = refs[9 + part_count : 12 + part_count]
-    (decoded, d_pre_out, d_resid_out, near_out, far_out, weights, keep, send) = refs[
+    (decoded, d_pre_out, d_resid_out, near_out, far_out, weights_back, keep, send) = refs[
         12 + part_count : 20 + part_count
     ]
-    (mixer, framed, d_pre_turned, sums, g_mixer, g_proj, g_dec, g_code, totals, loss) = refs[
-        20 + part_count : 30 + part_count
+    (weights, mixer, framed, d_pre_turned, sums, g_mixer, g_proj, g_dec, g_code, totals, loss) = refs[
+        20 + part_count : 31 + part_count
     ]
-    proj, dec, code, norms, scale = refs[30 + part_count :]
+    proj, dec, code, norms, scale = refs[31 + part_count :]
     step = pl.program_id(0)
     steps = pl.num_programs(0)
     height, wide, channels = feat.shape[1:]
@@ -208,6 +208,10 @@
 
     @pl.when(step == steps - 1)
     def _():
+        for a in range(3):
+            for b in range(3):
+                block = weights[2 - a, (2 - b) * channels : (3 - b) * channels, :]
+                weights_back[a, b * channels : (b + 1) * channels, :] = block.T
         for line in range(3):
             total = None
             for n in range(images):
@@ -280,6 +284,7 @@
         out_specs=[strip] * 3 + [line] * 2 + [whole(s.shape) for s in shapes[5:]],
         out_shape=shapes,
         scratch_shapes=[
+            pltpu.VMEM((3, 3 * channels, channels), BF16),
             pltpu.VMEM((channels, channels), BF16),
             pltpu.VMEM((images, (height + 2) * wide, 3 * channels), BF16),
             pltpu.VMEM((images, channels, height * wide), BF16),
@@ -400,39 +405,73 @@
     outs[9][...] = jnp.sum(loss, axis=(0, 1), keepdims=True) * scale
 
 
-def input_units(weights, feat, d_resid, d_pre, near, far, lead, out, done):
-    images, height, wide, channels = feat.shape
+def taps(line, first, last):
+    before, after = shift_lines(line.astype(F32), first, last)
+    return jnp.concatenate([before, line, after], axis=1)
+
+
+def inner_kernel(batch, weights, feat, d_resid, d_pre, out):
+    height, wide, channels = feat.shape[1:]
     column = lax.broadcasted_iota(jnp.int32, (wide, channels), 0)
     first = column == 0
     last = column == wide - 1
-    count = height * wide
-    for base in range(0, images, 2):
-        group = range(base, base + 2)
-        sides = []
-        for n in group:
-            lines = []
-            for r in range(height + 2):
-                if r == 0:
-                    line = jnp.where(lead, far[n], near[n])
-                elif r == height + 1:
-                    line = jnp.where(lead, near[n], far[n])
-                else:
-                    line = d_pre[n, r - 1]
-                before, after = shift_lines(line.astype(F32), first, last)
-                lines.append((before, line, after))
-            sides.append([jnp.concatenate([l[s] for l in lines], axis=0) for s in range(3)])
-        acts = [None for n in group]
+    lines = height - 2
+    rows = lines * wide
+    sides = []
+    for n in range(batch):
+        seen = [taps(d_pre[n, r], first, last) for r in range(height)]
+        sides.append(jnp.concatenate(seen, axis=0))
+    acts = [None] * batch
+    for a in range(3):
+        for n in range(batch):
+            term = dot(sides[n][a * wide : a * wide + rows], weights[a])
+            acts[n] = term if acts[n] is None else acts[n] + term
+    for n in range(batch):
+        for r in range(lines):
+            _, slope = gelu_both(feat[n, 1 + r].astype(F32))
+            act = acts[n][r * wide : (r + 1) * wide]
+            out[n, 1 + r] = (d_resid[n, 1 + r].astype(F32) + slope * act).astype(BF16)
+        for r in (0, height - 1):
+            out[n, r] = jnp.zeros((wide, channels), BF16)
+
+
+def inner_call(weights, feat, d_resid, d_pre):
+    images, height, wide, channels = feat.shape
+    batch = 5 if images % 5 == 0 else 1
+    strip = pl.BlockSpec((batch, height, wide, channels), lambda i: (i, 0, 0, 0))
+    return pl.pallas_call(
+        lambda *refs: inner_kernel(batch, *refs),
+        grid=(images // batch,),
+        in_specs=[pl.BlockSpec(weights.shape, lambda i: (0, 0, 0)), strip, strip, strip],
+        out_specs=strip,
+        out_shape=jax.ShapeDtypeStruct(feat.shape, BF16),
+        compiler_params=pltpu.CompilerParams(vmem_limit_bytes=FINISH_VMEM),
+        name="inner_lines",
+    )(weights, feat, d_resid, d_pre)
+
+
+def edge_units(group, weights, feats, d_resids, d_pres, near, far, lead, outs):
+    images, _, wide, channels = d_pres[0].shape
+    column = lax.broadcasted_iota(jnp.int32, (wide, channels), 0)
+    first = column == 0
+    last = column == wide - 1
+    for base in range(0, images, group):
+        members = [(n, end) for n in range(base, base + group) for end in range(2)]
+        seen = []
+        for n, end in members:
+            if end == 0:
+                lines = [jnp.where(lead, far[n], near[n]), d_pres[0][n, 0], d_pres[0][n, 1]]
+            else:
+                lines = [d_pres[1][n, 0], d_pres[1][n, 1], jnp.where(lead, near[n], far[n])]
+            seen.append([taps(line, first, last) for line in lines])
+        act = None
         for a in range(3):
-            for k in range(len(acts)):
-                window = jnp.concatenate([sides[k][b][a * wide : a * wide + count] for b in range(3)], axis=1)
-                weight = jnp.concatenate([weights[2 - a, (2 - b) * channels : (3 - b) * channels, :] for b in range(3)], axis=1)
-                term = dot(window, weight, NT)
-                acts[k] = term if acts[k] is None else acts[k] + term
-        for k, n in enumerate(group):
-            _, slope = gelu_both(feat[n].reshape(count, channels).astype(F32))
-            total = d_resid[n].reshape(count, channels).astype(F32) + slope * acts[k]
-            out[n] = total.astype(BF16).reshape(height, wide, channels)
-            done(n)
+            term = dot(jnp.concatenate([s[a] for s in seen], axis=0), weights[a])
+            act = term if act is None else act + term
+        for k, (n, end) in enumerate(members):
+            _, slope = gelu_both(feats[end][n].astype(F32))
+            total = d_resids[end][n].astype(F32) + slope * act[k * wide : (k + 1) * wide]
+            outs[end][n] = total.astype(BF16)
         yield
 
 
@@ -455,7 +494,7 @@
     yield
 
 
-CHUNKS = 4
+EDGE_GROUP = 4
 
 
 def finish_kernel(*refs):
@@ -463,19 +502,24 @@
     quarters = refs[2:6]
     master, first, second, left, right, basis_left, basis_right = refs[6:13]
     small_arrays = refs[13:22]
-    loads = refs[22:28]
+    weights_far, feat, d_resid, d_pre, near_far, far_far = refs[22:28]
     (master_new, first_new, second_new, left_new, right_new, basis_left_new, basis_right_new) = refs[
-        28:35
+        29:36
     ]
-    small_outs = refs[35:45]
-    input_grad = refs[45]
-    work, grad_turned, small_sums = refs[46:49]
-    held = refs[49:55]
-    out, load_sems, store_sems = refs[55:]
+    small_outs = refs[36:46]
+    input_grad = refs[46]
+    work, grad_turned, small_sums = refs[47:50]
+    weights, feats, d_resids, d_pres, near, far, outs, load_sems, store_sems = refs[50:]
     count, tile = master.shape[:2]
-    images = out.shape[0]
+    images, height = feat.shape[:2]
+    ends = (0, height - 1)
+    loads = [(weights_far, weights), (near_far, near), (far_far, far)]
+    for end in range(2):
+        loads.append((feat.at[:, ends[end]], feats.at[end]))
+        loads.append((d_resid.at[:, ends[end]], d_resids.at[end]))
+        loads.append((d_pre.at[:, pl.ds(end * (height - 2), 2)], d_pres.at[end]))
     copies = [
-        pltpu.make_async_copy(src, dst, load_sems.at[n]) for n, (src, dst) in enumerate(zip(loads, held))
+        pltpu.make_async_copy(src, dst, load_sems.at[n]) for n, (src, dst) in enumerate(loads)
     ]
     for copy in copies:
         copy.start()
@@ -496,16 +540,7 @@
             work[2 * t + side, :, tile:] = turned
     for copy in copies:
         copy.wait()
-    group = images // CHUNKS if images % CHUNKS == 0 else images
-    stores = []
-
-    def done(n):
-        if n % group == group - 1:
-            part = pl.ds(n + 1 - group, group)
-            sem = store_sems.at[len(stores)]
-            stores.append(pltpu.make_async_copy(out.at[part], input_grad.at[part], sem))
-            stores[-1].start()
-
+    group = EDGE_GROUP if images % EDGE_GROUP == 0 else 1
     units = [
         adam_units(
             (master, first, second, basis_left, basis_right),
@@ -513,11 +548,21 @@
             first_new,
             second_new,
             master_new,
-            lambda: small_update(present, out.shape, small_sums, small_arrays, small_outs),
+            lambda: small_update(present, feat.shape, small_sums, small_arrays, small_outs),
         ),
-        input_units(*held, lax.rem(ids[0], 2) == 0, out, done),
+        edge_units(
+            group,
+            weights,
+            [feats.at[end] for end in range(2)],
+            [d_resids.at[end] for end in range(2)],
+            [d_pres.at[end] for end in range(2)],
+            near,
+            far,
+            lax.rem(ids[0], 2) == 0,
+            [outs.at[end] for end in range(2)],
+        ),
     ]
-    total = count + 1 + images // 2
+    total = count + 1 + images // group
     slots = tile // RANK
     used = [0, 0]
 
@@ -551,6 +596,12 @@
     for t in range(count):
         basis_left_new[t] = work[2 * t, :, tile:].T
         basis_right_new[t] = work[2 * t + 1, :, tile:].T
+    stores = [
+        pltpu.make_async_copy(outs.at[end], input_grad.at[:, ends[end]], store_sems.at[end])
+        for end in range(2)
+    ]
+    for store in stores:
+        store.start()
     for store in stores:
         store.wait()
 
@@ -563,7 +614,10 @@
     count, tile = shape.shape[:2]
     shapes = [shape] * 7 + [jax.ShapeDtypeStruct(a.shape, F32) for a in small_arrays]
     shapes.append(jax.ShapeDtypeStruct((1, 1), F32))
-    shapes.append(jax.ShapeDtypeStruct(loads[1].shape, BF16))
+    weights, feat, _, _, near, far, partial = loads
+    images, height, wide, channels = feat.shape
+    shapes.append(jax.ShapeDtypeStruct(feat.shape, BF16))
+    ends = (2, images, wide, channels)
     return pl.pallas_call(
         finish_kernel,
         in_specs=[smem] + [vmem] * 21 + [hbm] * len(loads),
@@ -573,11 +627,17 @@
             pltpu.VMEM((2 * count, tile, 2 * tile), F32),
             pltpu.VMEM((count, tile, tile), BF16),
             pltpu.VMEM((4, quarters[0].shape[0] - count * tile // 4, tile), BF16),
-            *(pltpu.VMEM(a.shape, a.dtype) for a in loads),
-            pltpu.VMEM(loads[1].shape, BF16),
-            pltpu.SemaphoreType.DMA((len(loads),)),
-            pltpu.SemaphoreType.DMA((CHUNKS,)),
+            pltpu.VMEM(weights.shape, BF16),
+            pltpu.VMEM(ends, BF16),
+            pltpu.VMEM(ends, BF16),
+            pltpu.VMEM((2, images, 2, wide, channels), BF16),
+            pltpu.VMEM(near.shape, BF16),
+            pltpu.VMEM(far.shape, BF16),
+            pltpu.VMEM(ends, BF16),
+            pltpu.SemaphoreType.DMA((9,)),
+            pltpu.SemaphoreType.DMA((2,)),
         ],
+        input_output_aliases={22 + len(loads) - 1: 17},
         compiler_params=pltpu.CompilerParams(vmem_limit_bytes=FINISH_VMEM),
         name="finish",
     )(ids, present[None], *quarters, *arrays, *small_arrays, *loads)
@@ -647,7 +707,7 @@
     return terms[0]
 
 
-def reduce_all(keep, send, tiles, quarter):
+def reduce_all(keep, send, tiles, quarter, inner, inputs):
     strip = lax.axis_index("strip")
     across = strip // 2
     img = lax.axis_index("img")
@@ -659,6 +719,7 @@
     part = keep + swap(send, "strip", 1)
     left = groups // radix
     terms = []
+    part, inputs = lax.optimization_barrier((part, inputs))
     for d in range(2):
         for e in range(radix):
             both = lax.dynamic_index_in_dim(part, across ^ d, 0, False)
@@ -673,6 +734,7 @@
                 ]
                 piece = lax.ppermute(piece, ("strip", "img"), pairs)
             terms.append(piece)
+    terms, result = lax.optimization_barrier((terms, inner(*inputs)))
     total = tree_sum(terms).astype(BF16)
     for radix, stride in later:
         low = (img // stride) % radix
@@ -685,7 +747,7 @@
             terms.append(swap(piece, "img", d * stride) if d else piece)
         total = tree_sum(terms).astype(BF16)
         left //= radix
-    return [total] + [swap(total, "strip", d) for d in range(1, 4)]
+    return [total] + [swap(total, "strip", d) for d in range(1, 4)], result
 
 
 def body(
@@ -735,7 +797,14 @@
         code_master.T,
     )
     near, far = swap_edges(near_out, far_out)
-    quarters = reduce_all(keep, send, tiles, tile_master.shape[1] // 4)
+    quarters, partial = reduce_all(
+        keep,
+        send,
+        tiles,
+        tile_master.shape[1] // 4,
+        inner_call,
+        (weights, features, d_resid, d_pre),
+    )
     out = finish_call(
         ids,
         present,
@@ -752,7 +821,7 @@
             code_mom1.T,
             code_mom2.T,
         ],
-        [weights, features, d_resid, d_pre, near, far],
+        [weights, features, d_resid, d_pre, near, far, partial],
     )
     small = [a.T for a in out[7:10]] + list(out[10:13]) + [a.T for a in out[13:16]]
     return (decoded, out[17], out[16].reshape(()), *out[:7], *small)

time: 120 us -> 117 us (0.975)
  waiting for transfers between devices: 32.8 us -> 23.7 us
  Pallas kernels: 59.2 us -> 65.1 us
    pallas_call x0 -> x1, Pallas kernels: none -> 9.82 us  [inner_call(): pl.pallas_call(lambda *refs: inner_kernel(batch, *refs), grid=(images //...]
    ppermute x3, waiting for transfers between devices: 9.03 us -> 0.01 us  [reduce_all(): piece = lax.ppermute(piece, ('strip', 'img'), pairs)]
    pallas_call x1, Pallas kernels: 21.4 us -> 17.4 us  [finish_call(): pl.pallas_call(finish_kernel, in_specs=[smem] + [vmem] * 21 + [hbm] * len...]
  transfers between devices with their start and end apart: 23 -> 23, of which waited for: 12 -> 9; matrix products, arithmetic and copies ran while one was open for 3% -> 3% of each run, Pallas kernels for 0% -> 8%
where the time goes in v5:
time: 117 us
  Pallas kernels  65.1 us (56%)
  waiting for transfers between devices  23.7 us (20%)
  starting transfers between devices  20 us (17%)
  other arithmetic  4.53 us (4%)
  local copies, waits for them, and re-layouts  2.39 us (2%)
  between operations  1.2 us (1%)
    pallas_call x1, Pallas kernels, main_call(): pl.pallas_call(lambda *refs: main_kernel(batch, len(parts), *refs), grid=...  37.9 us
    ppermute x18, waiting for transfers between devices, swap(): return lax.ppermute(x, axis, [(i, i ^ distance) for i in range(count)])  23.6 us
    pallas_call x1, Pallas kernels, finish_call(): pl.pallas_call(finish_kernel, in_specs=[smem] + [vmem] * 21 + [hbm] * len...  17.4 us
    ppermute x18, starting transfers between devices, swap(): return lax.ppermute(x, axis, [(i, i ^ distance) for i in range(count)])  15 us
    pallas_call x1, Pallas kernels, inner_call(): pl.pallas_call(lambda *refs: inner_kernel(batch, *refs), grid=(images //...  9.82 us
    ppermute x3, starting transfers between devices, reduce_all(): piece = lax.ppermute(piece, ('strip', 'img'), pairs)  3.62 us
  transfers between devices with their start and end apart: 23, of which 9 were waited for; matrix products, arithmetic and copies ran while one was open for 3% of the time, Pallas kernels for 8%

profile of v5, /device:TPU:0, one launch (start us, length us, event | category | flops | bytes accessed | tf_op | source)
XLA Modules:
  0.0 116.8 jit_solution(6296364504551804957)
XLA Ops:
  0.7 0.9 dynamic-slice_convert_fusion
  1.6 4.1 %collective-permute-start.1 = (bf16[5,64,128]{2,1,0:T(8,128)(2,1)S(1)}, bf16[5,64,128]{2,1,0:T(8,128)(2,1)S(1)}, u32[]{:S(2)}, u32[]{:S(2)}) collective-permute-start(bf16[5,64,128]{2,1,0:T(8,128)(2,1)S(1)} %dynamic-slice_convert_fusion), channel_id=1, source_target_pairs={{0,4},{1,5},{2,6},{3,7},{4,0},{5,1},{6,2},{7,3},{8,12},{9,13},{10,... | collective-permute-start | bytes 245768 | tf_op jit(solution)/shard_map/ppermute | solution.py:659
  5.7 1.6 %collective-permute-start = (bf16[5,64,128]{2,1,0:T(8,128)(2,1)S(1)}, bf16[5,64,128]{2,1,0:T(8,128)(2,1)S(1)}, u32[]{:S(2)}, u32[]{:S(2)}) collective-permute-start(bf16[5,64,128]{2,1,0:T(8,128)(2,1)S(1)} %dynamic-slice_convert_fusion), channel_id=1, source_target_pairs={{0,2},{1,3},{2,0},{3,1},{4,6},{5,7},{6,4},{7,5},{8,10},{9,11},{10,... | collective-permute-start | bytes 245768 | tf_op jit(solution)/shard_map/ppermute | solution.py:659
  7.3 1.1 fusion.1
  9.1 1.2 %fusion.3.refs_1_ = s32[40]{0:T(128)} fusion(s32[40]{0:T(128)} %refs_2_.1, s32[]{:T(128)} %axis_index.17), kind=kLoop, calls=%fused_computation.40 | loop fusion | flops 1880 | bytes 324 | tf_op jit(solution)/shard_map/add | solution.py:700
  11.0 2.5 %collective-permute-done.2 = bf16[5,64,128]{2,1,0:T(8,128)(2,1)S(1)} collective-permute-done((bf16[5,64,128]{2,1,0:T(8,128)(2,1)S(1)}, bf16[5,64,128]{2,1,0:T(8,128)(2,1)S(1)}, u32[]{:S(2)}, u32[]{:S(2)}) %collective-permute-start.2) | collective-permute-done | bytes 81952 | tf_op jit(solution)/shard_map/ppermute | solution.py:659
  14.3 1.5 %collective-permute-start.5 = (bf16[10,64,128]{2,1,0:T(8,128)(2,1)S(1)}, bf16[10,64,128]{2,1,0:T(8,128)(2,1)S(1)}, u32[]{:S(2)}, u32[]{:S(2)}) collective-permute-start(bf16[10,64,128]{2,1,0:T(8,128)(2,1)S(1)} %pad_maximum_fusion.4.refs_9_), channel_id=1, source_target_pairs={{0,1},{1,0},{2,3},{3,2},{4,5},{5,4},{6,7},{7,6},{8,9},{9,8},{10,11... | collective-permute-start | bytes 491528 | tf_op jit(solution)/shard_map/ppermute | solution.py:659
  16.3 5.0 %collective-permute-done.5.refs_11_ = bf16[10,64,128]{2,1,0:T(8,128)(2,1)S(1)} collective-permute-done((bf16[10,64,128]{2,1,0:T(8,128)(2,1)S(1)}, bf16[10,64,128]{2,1,0:T(8,128)(2,1)S(1)}, u32[]{:S(2)}, u32[]{:S(2)}) %collective-permute-start.5) | collective-permute-done | bytes 163872 | tf_op jit(solution)/shard_map/ppermute | solution.py:659
  21.3 3.1 %collective-permute-done.6.refs_12_ = bf16[10,64,128]{2,1,0:T(8,128)(2,1)S(1)} collective-permute-done((bf16[10,64,128]{2,1,0:T(8,128)(2,1)S(1)}, bf16[10,64,128]{2,1,0:T(8,128)(2,1)S(1)}, u32[]{:S(2)}, u32[]{:S(2)}) %collective-permute-start.6) | collective-permute-done | bytes 163872 | tf_op jit(solution)/shard_map/ppermute | solution.py:659
  24.4 1.3 %collective-permute-done.10.refs_16_ = bf16[10,64,128]{2,1,0:T(8,128)(2,1)S(1)} collective-permute-done((bf16[10,64,128]{2,1,0:T(8,128)(2,1)S(1)}, bf16[10,64,128]{2,1,0:T(8,128)(2,1)S(1)}, u32[]{:S(2)}, u32[]{:S(2)}) %collective-permute-start.10) | collective-permute-done | bytes 163872 | tf_op jit(solution)/shard_map/ppermute | solution.py:659
  26.4 37.9 %main.1 = (bf16[20,8,32,256]{3,2,1,0:T(8,128)(2,1)}, bf16[20,8,32,256]{3,2,1,0:T(8,128)(2,1)}, bf16[20,8,32,256]{3,2,1,0:T(8,128)(2,1)}, bf16[20,32,256]{2,1,0:T...) custom-call(s32[2]{0:T(128)} %pad_add_fusion.refs_0_, ...), custom_call_target="tpu_custom_call" | custom-call | tf_op jit(solution)/shard_map/main/pallas_call | solution.py:278
  64.5 2.3 %collective-permute-done.11 = bf16[2,1424,128]{2,1,0:T(8,128)(2,1)S(1)} collective-permute-done((bf16[2,1424,128]{2,1,0:T(8,128)(2,1)}, bf16[2,1424,128]{2,1,0:T(8,128)(2,1)S(1)}, u32[]{:S(2)}, u32[]{:S(2)}) %collective-permute-start.11) | collective-permute-done | bytes 729120 | tf_op jit(solution)/shard_map/ppermute | solution.py:659
  66.8 1.3 %add.98 = bf16[2,1424,128]{2,1,0:T(8,128)(2,1)S(1)} add(bf16[2,1424,128]{2,1,0:T(8,128)(2,1)} %get-tuple-element.64, bf16[2,1424,128]{2,1,0:T(8,128)(2,1)S(1)} %collective-permute-done.11) | non-fusion elementwise | flops 364544 | bytes 2187264 | tf_op jit(solution)/shard_map/add | solution.py:719
  68.3 1.6 %collective-permute-start.12 = (bf16[784,128]{1,0:T(8,128)(2,1)S(1)}, bf16[784,128]{1,0:T(8,128)(2,1)S(1)}, u32[]{:S(2)}, u32[]{:S(2)}) collective-permute-start(bf16[784,128]{1,0:T(8,128)(2,1)S(1)} %get-tuple-element.118), channel_id=1, source_target_pairs={{0,1},{1,0},{2,3},{3,2},{4,5},{5,4},{6,7},{7,6},{8,9},{9,8},{10,11... | collective-permute-start | bytes 602120 | tf_op jit(solution)/shard_map/ppermute | solution.py:735
  69.9 1.1 collective-permute-start.14
  71.0 0.9 collective-permute-start.13
  71.9 9.8 %inner_lines.1.refs_28_ = bf16[20,8,32,256]{3,2,1,0:T(8,128)(2,1)} custom-call(bf16[3,768,256]{2,1,0:T(8,128)(2,1)} %get-tuple-element.70.refs_0_.refs_22_, bf16[20,8,32,256]{3,2,1,0:T(8,128)(2,1)} %refs_23_.1, bf16[20,8,32,256]{3,2,1,0:T(8,128)(2,1)} %get-tuple-element.72.refs_2_.refs_24_, bf16[20,8,32,256]{3,2,1,0:T(8,128)(2,1)} %get-tuple-element.73.refs_3_.refs_25_), custom_call_target="tpu_custom_call" | custom-call | tf_op jit(solution)/shard_map/inner_lines/pallas_call | solution.py:442
  82.8 3.5 %collective-permute-start.16 = (bf16[304,128]{1,0:T(8,128)(2,1)S(1)}, bf16[304,128]{1,0:T(8,128)(2,1)S(1)}, u32[]{:S(2)}, u32[]{:S(2)}) collective-permute-start(bf16[304,128]{1,0:T(8,128)(2,1)S(1)} %get-tuple-element.114), channel_id=1, source_target_pairs={{0,4},{1,5},{2,6},{3,7},{4,0},{5,1},{6,2},{7,3},{8,12},{9,13},{10,... | collective-permute-start | bytes 233480 | tf_op jit(solution)/shard_map/ppermute | solution.py:659
  87.2 4.0 %collective-permute-done.16 = bf16[304,128]{1,0:T(8,128)(2,1)S(1)} collective-permute-done((bf16[304,128]{1,0:T(8,128)(2,1)S(1)}, bf16[304,128]{1,0:T(8,128)(2,1)S(1)}, u32[]{:S(2)}, u32[]{:S(2)}) %collective-permute-start.16) | collective-permute-done | bytes 77856 | tf_op jit(solution)/shard_map/ppermute | solution.py:659
  91.1 1.4 %collective-permute-done.17 = bf16[304,128]{1,0:T(8,128)(2,1)S(1)} collective-permute-done((bf16[304,128]{1,0:T(8,128)(2,1)S(1)}, bf16[304,128]{1,0:T(8,128)(2,1)S(1)}, u32[]{:S(2)}, u32[]{:S(2)}) %collective-permute-start.17) | collective-permute-done | bytes 77856 | tf_op jit(solution)/shard_map/ppermute | solution.py:659
  93.0 1.5 %collective-permute-start.18 = (bf16[304,128]{1,0:T(8,128)(2,1)S(1)}, bf16[304,128]{1,0:T(8,128)(2,1)S(1)}, u32[]{:S(2)}, u32[]{:S(2)}) collective-permute-start(bf16[304,128]{1,0:T(8,128)(2,1)S(1)} %add_convert_fusion.1.refs_2_), channel_id=1, source_target_pairs={{0,8},{8,0},{16,24},{24,16},{1,9},{9,1},{17,25},{25,17},{2,10},{10... | collective-permute-start | bytes 233480 | tf_op jit(solution)/shard_map/ppermute | solution.py:659
  94.5 2.8 %collective-permute-done.20.refs_5_ = bf16[304,128]{1,0:T(8,128)(2,1)S(1)} collective-permute-done((bf16[304,128]{1,0:T(8,128)(2,1)S(1)}, bf16[304,128]{1,0:T(8,128)(2,1)S(1)}, u32[]{:S(2)}, u32[]{:S(2)}) %collective-permute-start.20) | collective-permute-done | bytes 77856 | tf_op jit(solution)/shard_map/ppermute | solution.py:659
  97.4 1.3 %collective-permute-done.19.refs_4_ = bf16[304,128]{1,0:T(8,128)(2,1)S(1)} collective-permute-done((bf16[304,128]{1,0:T(8,128)(2,1)S(1)}, bf16[304,128]{1,0:T(8,128)(2,1)S(1)}, u32[]{:S(2)}, u32[]{:S(2)}) %collective-permute-start.19) | collective-permute-done | bytes 77856 | tf_op jit(solution)/shard_map/ppermute | solution.py:659
  99.3 17.4 %finish.1 = (f32[5,128,128]{2,1,0:T(8,128)}, f32[5,128,128]{2,1,0:T(8,128)}, f32[5,128,128]{2,1,0:T(8,128)}, f32[5,128,128]{2,1,0:T(8,128)}, f32[5,128,128]{2,1,...) custom-call(s32[2]{0:T(128)} %pad_add_fusion.refs_0_, ...), custom_call_target="tpu_custom_call", output_to_operand_aliasing={{17}: (28, {})} | custom-call | tf_op jit(solution)/shard_map/finish/pallas_call | solution.py:621
  (79 shorter events, 6.6 us)
Async XLA Ops:
  1.6 9.4 %collective-permute-start.1 = (bf16[5,64,128]{2,1,0:T(8,128)(2,1)S(1)}, bf16[5,64,128]{2,1,0:T(8,128)(2,1)S(1)}, u32[]{:S(2)}, u32[]{:S(2)}) collective-permute-start(bf16[5,64,128]{2,1,0:T(8,128)(2,1)S(1)} %dynamic-slice_convert_fusion), channel_id=1, source_target_pairs={{0,4},{1,5},{2,6},{3,7},{4,0},{5,1},{6,2},{7,3},{8,12},{9,13},{10,... | collective-permute-start | bytes 245768 | tf_op jit(solution)/shard_map/ppermute | solution.py:659
  5.7 5.2 %collective-permute-start = (bf16[5,64,128]{2,1,0:T(8,128)(2,1)S(1)}, bf16[5,64,128]{2,1,0:T(8,128)(2,1)S(1)}, u32[]{:S(2)}, u32[]{:S(2)}) collective-permute-start(bf16[5,64,128]{2,1,0:T(8,128)(2,1)S(1)} %dynamic-slice_convert_fusion), channel_id=1, source_target_pairs={{0,2},{1,3},{2,0},{3,1},{4,6},{5,7},{6,4},{7,5},{8,10},{9,11},{10,... | collective-permute-start | bytes 245768 | tf_op jit(solution)/shard_map/ppermute | solution.py:659
  7.3 6.2 %collective-permute-start.2 = (bf16[5,64,128]{2,1,0:T(8,128)(2,1)S(1)}, bf16[5,64,128]{2,1,0:T(8,128)(2,1)S(1)}, u32[]{:S(2)}, u32[]{:S(2)}) collective-permute-start(bf16[5,64,128]{2,1,0:T(8,128)(2,1)S(1)} %dynamic-slice_convert_fusion), channel_id=1, source_target_pairs={{0,6},{1,7},{2,4},{3,5},{4,2},{5,3},{6,0},{7,1},{8,14},{9,15},{10,... | collective-permute-start | bytes 245768 | tf_op jit(solution)/shard_map/ppermute | solution.py:659
  8.4 15.9 %collective-permute-start.4 = (bf16[20,32,256]{2,1,0:T(8,128)(2,1)S(1)}, bf16[20,32,256]{2,1,0:T(8,128)(2,1)S(1)}, u32[]{:S(2)}, u32[]{:S(2)}) collective-permute-start(bf16[20,32,256]{2,1,0:T(8,128)(2,1)S(1)} %get-tuple-element.99), channel_id=1, source_target_pairs={{8,16},{16,8},{9,17},{17,9},{10,18},{18,10},{11,19},{19,11},{12,20... | collective-permute-start | bytes 983048 | tf_op jit(solution)/shard_map/ppermute | solution.py:674
  11.0 14.7 %copy-start = (bf16[10,64,128]{2,1,0:T(8,128)(2,1)}, bf16[10,64,128]{2,1,0:T(8,128)(2,1)S(1)}, u32[]{:S(2)}) copy-start(bf16[10,64,128]{2,1,0:T(8,128)(2,1)S(1)} %pad_maximum_fusion.4.refs_9_) | copy-start | bytes 491524
  13.6 2.7 %collective-permute-start.7 = (bf16[10,64,128]{2,1,0:T(8,128)(2,1)S(1)}, bf16[10,64,128]{2,1,0:T(8,128)(2,1)S(1)}, u32[]{:S(2)}, u32[]{:S(2)}) collective-permute-start(bf16[10,64,128]{2,1,0:T(8,128)(2,1)S(1)} %pad_maximum_fusion.4.refs_9_), channel_id=1, source_target_pairs={{0,8},{8,0},{16,24},{24,16},{1,9},{9,1},{17,25},{25,17},{2,10},{10... | collective-permute-start | bytes 491528 | tf_op jit(solution)/shard_map/ppermute | solution.py:659
  14.2 10.2 %collective-permute-start.3 = (bf16[20,32,256]{2,1,0:T(8,128)(2,1)S(1)}, bf16[20,32,256]{2,1,0:T(8,128)(2,1)S(1)}, u32[]{:S(2)}, u32[]{:S(2)}) collective-permute-start(bf16[20,32,256]{2,1,0:T(8,128)(2,1)S(1)} %get-tuple-element.100), channel_id=1, source_target_pairs={{0,8},{8,0},{16,24},{24,16},{1,9},{9,1},{17,25},{25,17},{2,10},{10... | collective-permute-start | bytes 983048 | tf_op jit(solution)/shard_map/ppermute | solution.py:659
  14.3 7.0 %collective-permute-start.5 = (bf16[10,64,128]{2,1,0:T(8,128)(2,1)S(1)}, bf16[10,64,128]{2,1,0:T(8,128)(2,1)S(1)}, u32[]{:S(2)}, u32[]{:S(2)}) collective-permute-start(bf16[10,64,128]{2,1,0:T(8,128)(2,1)S(1)} %pad_maximum_fusion.4.refs_9_), channel_id=1, source_target_pairs={{0,1},{1,0},{2,3},{3,2},{4,5},{5,4},{6,7},{7,6},{8,9},{9,8},{10,11... | collective-permute-start | bytes 491528 | tf_op jit(solution)/shard_map/ppermute | solution.py:659
  15.8 8.5 %collective-permute-start.6 = (bf16[10,64,128]{2,1,0:T(8,128)(2,1)S(1)}, bf16[10,64,128]{2,1,0:T(8,128)(2,1)S(1)}, u32[]{:S(2)}, u32[]{:S(2)}) collective-permute-start(bf16[10,64,128]{2,1,0:T(8,128)(2,1)S(1)} %pad_maximum_fusion.5.refs_10_), channel_id=1, source_target_pairs={{0,1},{1,0},{2,3},{3,2},{4,5},{5,4},{6,7},{7,6},{8,9},{9,8},{10,11... | collective-permute-start | bytes 491528 | tf_op jit(solution)/shard_map/ppermute | solution.py:659
  16.3 8.0 %collective-permute-start.8 = (bf16[10,64,128]{2,1,0:T(8,128)(2,1)S(1)}, bf16[10,64,128]{2,1,0:T(8,128)(2,1)S(1)}, u32[]{:S(2)}, u32[]{:S(2)}) collective-permute-start(bf16[10,64,128]{2,1,0:T(8,128)(2,1)S(1)} %pad_maximum_fusion.5.refs_10_), channel_id=1, source_target_pairs={{0,8},{8,0},{16,24},{24,16},{1,9},{9,1},{17,25},{25,17},{2,10},{10... | collective-permute-start | bytes 491528 | tf_op jit(solution)/shard_map/ppermute | solution.py:659
  21.3 3.1 %collective-permute-start.9 = (bf16[10,64,128]{2,1,0:T(8,128)(2,1)S(1)}, bf16[10,64,128]{2,1,0:T(8,128)(2,1)S(1)}, u32[]{:S(2)}, u32[]{:S(2)}) collective-permute-start(bf16[10,64,128]{2,1,0:T(8,128)(2,1)S(1)} %collective-permute-done.5.refs_11_), channel_id=1, source_target_pairs={{0,8},{8,0},{16,24},{24,16},{1,9},{9,1},{17,25},{25,17},{2,10},{10... | collective-permute-start | bytes 491528 | tf_op jit(solution)/shard_map/ppermute | solution.py:659
  24.3 1.4 %collective-permute-start.10 = (bf16[10,64,128]{2,1,0:T(8,128)(2,1)S(1)}, bf16[10,64,128]{2,1,0:T(8,128)(2,1)S(1)}, u32[]{:S(2)}, u32[]{:S(2)}) collective-permute-start(bf16[10,64,128]{2,1,0:T(8,128)(2,1)S(1)} %collective-permute-done.6.refs_12_), channel_id=1, source_target_pairs={{0,8},{8,0},{16,24},{24,16},{1,9},{9,1},{17,25},{25,17},{2,10},{10... | collective-permute-start | bytes 491528 | tf_op jit(solution)/shard_map/ppermute | solution.py:659
  64.3 2.5 %collective-permute-start.11 = (bf16[2,1424,128]{2,1,0:T(8,128)(2,1)}, bf16[2,1424,128]{2,1,0:T(8,128)(2,1)S(1)}, u32[]{:S(2)}, u32[]{:S(2)}) collective-permute-start(bf16[2,1424,128]{2,1,0:T(8,128)(2,1)} %get-tuple-element.65), channel_id=1, source_target_pairs={{0,8},{8,0},{16,24},{24,16},{1,9},{9,1},{17,25},{25,17},{2,10},{10... | collective-permute-start | bytes 2187272 | tf_op jit(solution)/shard_map/ppermute | solution.py:659
  68.3 13.5 %collective-permute-start.12 = (bf16[784,128]{1,0:T(8,128)(2,1)S(1)}, bf16[784,128]{1,0:T(8,128)(2,1)S(1)}, u32[]{:S(2)}, u32[]{:S(2)}) collective-permute-start(bf16[784,128]{1,0:T(8,128)(2,1)S(1)} %get-tuple-element.118), channel_id=1, source_target_pairs={{0,1},{1,0},{2,3},{3,2},{4,5},{5,4},{6,7},{7,6},{8,9},{9,8},{10,11... | collective-permute-start | bytes 602120 | tf_op jit(solution)/shard_map/ppermute | solution.py:735
  69.9 11.9 %collective-permute-start.14 = (bf16[784,128]{1,0:T(8,128)(2,1)S(1)}, bf16[784,128]{1,0:T(8,128)(2,1)S(1)}, u32[]{:S(2)}, u32[]{:S(2)}) collective-permute-start(bf16[784,128]{1,0:T(8,128)(2,1)S(1)} %get-tuple-element.116), channel_id=1, source_target_pairs={{0,17},{1,16},{2,19},{3,18},{4,21},{5,20},{6,23},{7,22},{8,25},{9,... | collective-permute-start | bytes 602120 | tf_op jit(solution)/shard_map/ppermute | solution.py:735
  71.0 10.7 %collective-permute-start.13 = (bf16[784,128]{1,0:T(8,128)(2,1)S(1)}, bf16[784,128]{1,0:T(8,128)(2,1)S(1)}, u32[]{:S(2)}, u32[]{:S(2)}) collective-permute-start(bf16[784,128]{1,0:T(8,128)(2,1)S(1)} %get-tuple-element.117), channel_id=1, source_target_pairs={{0,16},{1,17},{2,18},{3,19},{4,20},{5,21},{6,22},{7,23},{8,24},{9,... | collective-permute-start | bytes 602120 | tf_op jit(solution)/shard_map/ppermute | solution.py:735
  82.0 5.2 %collective-permute-start.15 = (bf16[304,128]{1,0:T(8,128)(2,1)S(1)}, bf16[304,128]{1,0:T(8,128)(2,1)S(1)}, u32[]{:S(2)}, u32[]{:S(2)}) collective-permute-start(bf16[304,128]{1,0:T(8,128)(2,1)S(1)} %get-tuple-element.113), channel_id=1, source_target_pairs={{0,2},{1,3},{2,0},{3,1},{4,6},{5,7},{6,4},{7,5},{8,10},{9,11},{10,... | collective-permute-start | bytes 233480 | tf_op jit(solution)/shard_map/ppermute | solution.py:659
  82.8 8.4 %collective-permute-start.16 = (bf16[304,128]{1,0:T(8,128)(2,1)S(1)}, bf16[304,128]{1,0:T(8,128)(2,1)S(1)}, u32[]{:S(2)}, u32[]{:S(2)}) collective-permute-start(bf16[304,128]{1,0:T(8,128)(2,1)S(1)} %get-tuple-element.114), channel_id=1, source_target_pairs={{0,4},{1,5},{2,6},{3,7},{4,0},{5,1},{6,2},{7,3},{8,12},{9,13},{10,... | collective-permute-start | bytes 233480 | tf_op jit(solution)/shard_map/ppermute | solution.py:659
  86.2 6.3 %collective-permute-start.17 = (bf16[304,128]{1,0:T(8,128)(2,1)S(1)}, bf16[304,128]{1,0:T(8,128)(2,1)S(1)}, u32[]{:S(2)}, u32[]{:S(2)}) collective-permute-start(bf16[304,128]{1,0:T(8,128)(2,1)S(1)} %get-tuple-element.115), channel_id=1, source_target_pairs={{0,6},{1,7},{2,4},{3,5},{4,2},{5,3},{6,0},{7,1},{8,14},{9,15},{10,... | collective-permute-start | bytes 233480 | tf_op jit(solution)/shard_map/ppermute | solution.py:659
  86.4 8.1 %collective-permute-start.21 = (bf16[20,32,256]{2,1,0:T(8,128)(2,1)S(1)}, bf16[20,32,256]{2,1,0:T(8,128)(2,1)S(1)}, u32[]{:S(2)}, u32[]{:S(2)}) collective-permute-start(bf16[20,32,256]{2,1,0:T(8,128)(2,1)S(1)} %copy-done.17), channel_id=1, source_target_pairs={{0,8},{8,0},{16,24},{24,16},{1,9},{9,1},{17,25},{25,17},{2,10},{10... | collective-permute-start | bytes 983048 | tf_op jit(solution)/shard_map/ppermute | solution.py:659
  86.5 8.1 %collective-permute-start.22 = (bf16[20,32,256]{2,1,0:T(8,128)(2,1)S(1)}, bf16[20,32,256]{2,1,0:T(8,128)(2,1)S(1)}, u32[]{:S(2)}, u32[]{:S(2)}) collective-permute-start(bf16[20,32,256]{2,1,0:T(8,128)(2,1)S(1)} %copy-done.16), channel_id=1, source_target_pairs={{8,16},{16,8},{9,17},{17,9},{10,18},{18,10},{11,19},{19,11},{12,20... | collective-permute-start | bytes 983048 | tf_op jit(solution)/shard_map/ppermute | solution.py:674
  92.6 4.8 %collective-permute-start.20 = (bf16[304,128]{1,0:T(8,128)(2,1)S(1)}, bf16[304,128]{1,0:T(8,128)(2,1)S(1)}, u32[]{:S(2)}, u32[]{:S(2)}) collective-permute-start(bf16[304,128]{1,0:T(8,128)(2,1)S(1)} %add_convert_fusion.1.refs_2_), channel_id=1, source_target_pairs={{0,24},{8,16},{16,8},{24,0},{1,25},{9,17},{17,9},{25,1},{2,26},{10... | collective-permute-start | bytes 233480 | tf_op jit(solution)/shard_map/ppermute | solution.py:659
  92.7 6.0 %collective-permute-start.19 = (bf16[304,128]{1,0:T(8,128)(2,1)S(1)}, bf16[304,128]{1,0:T(8,128)(2,1)S(1)}, u32[]{:S(2)}, u32[]{:S(2)}) collective-permute-start(bf16[304,128]{1,0:T(8,128)(2,1)S(1)} %add_convert_fusion.1.refs_2_), channel_id=1, source_target_pairs={{0,16},{8,24},{16,0},{24,8},{1,17},{9,25},{17,1},{25,9},{2,18},{10... | collective-permute-start | bytes 233480 | tf_op jit(solution)/shard_map/ppermute | solution.py:659
  93.0 5.7 %collective-permute-start.18 = (bf16[304,128]{1,0:T(8,128)(2,1)S(1)}, bf16[304,128]{1,0:T(8,128)(2,1)S(1)}, u32[]{:S(2)}, u32[]{:S(2)}) collective-permute-start(bf16[304,128]{1,0:T(8,128)(2,1)S(1)} %add_convert_fusion.1.refs_2_), channel_id=1, source_target_pairs={{0,8},{8,0},{16,24},{24,16},{1,9},{9,1},{17,25},{25,17},{2,10},{10... | collective-permute-start | bytes 233480 | tf_op jit(solution)/shard_map/ppermute | solution.py:659
  (17 other events, 79.9 us)

commit v6 on v5

--- a/solution.py
+++ b/solution.py
@@ -88,13 +88,14 @@
     present_row, feat, near, far, cot = refs[4:9]
     parts = refs[9 : 9 + part_count]
     proj_full, dec_full, code_full = refs[9 + part_count : 12 + part_count]
-    (decoded, d_pre_out, d_resid_out, near_out, far_out, weights_back, keep, send) = refs[
+    (decoded_far, d_pre_far, d_resid_far, near_out, far_out, weights_far, keep, send) = refs[
         12 + part_count : 20 + part_count
     ]
-    (weights, mixer, framed, d_pre_turned, sums, g_mixer, g_proj, g_dec, g_code, totals, loss) = refs[
-        20 + part_count : 31 + part_count
+    (weights, mixer, framed, d_pre_turned, g_mixer, g_proj, g_dec, g_code, totals, loss) = refs[
+        20 + part_count : 30 + part_count
     ]
-    proj, dec, code, norms, scale = refs[31 + part_count :]
+    proj, dec, code, norms, scale = refs[30 + part_count : 35 + part_count]
+    decoded, d_pre_out, d_resid_out, weights_back, big_sems, weight_sem = refs[35 + part_count :]
     step = pl.program_id(0)
     steps = pl.num_programs(0)
     height, wide, channels = feat.shape[1:]
@@ -122,8 +123,16 @@
         words = code[...].astype(F32)
         norms[...] = jnp.sum(words * words, axis=0, keepdims=True) * (1.0 / SOFTMAX_WARMTH)
         scale[0] = 2.0 * loss_scale(present_row, 4 * count, proj.shape[0])
-        for ref in (g_mixer, g_proj, g_dec, g_code, totals, loss):
+        for ref in (keep, send, g_mixer, g_proj, g_dec, g_code, totals, loss):
             ref[...] = jnp.zeros_like(ref)
+
+    @pl.when(step == 0)
+    def _():
+        for a in range(3):
+            for b in range(3):
+                block = weights[2 - a, (2 - b) * channels : (3 - b) * channels, :]
+                weights_back[a, b * channels : (b + 1) * channels, :] = block.T
+        pltpu.make_async_copy(weights_back, weights_far, weight_sem).start()
 
     column = lax.broadcasted_iota(jnp.int32, (wide, channels), 0)
     first = column == 0
@@ -170,7 +179,7 @@
         quant_low = quant.astype(BF16)
         yield
         out = (dot(quant_low, dec[...]) * alive).astype(BF16)
-        decoded[n] = out.reshape(height, wide, channels)
+        decoded[image] = out.reshape(height, wide, channels)
         diff = latent - quant
         loss[...] += alive * jnp.sum(diff * diff, axis=0, keepdims=True)
         back_out = (cot[n].reshape(count, channels).astype(F32) * alive).astype(BF16)
@@ -182,19 +191,22 @@
         yield
         d_logits = probs * (d_probs - jnp.sum(probs * d_probs, axis=1, keepdims=True))
         d_logits = d_logits.astype(BF16)
-        totals[...] += jnp.sum(d_logits.astype(F32), axis=0, keepdims=True)
         yield
         d_latent = ((2.0 / SOFTMAX_WARMTH) * dot(d_logits, code[...], NT) + pulled).astype(BF16)
         yield
         d_resid = dot(d_latent, proj[...]).astype(BF16)
-        d_resid_out[n] = d_resid.reshape(height, wide, channels)
+        d_resid_out[image] = d_resid.reshape(height, wide, channels)
         g_code[...] += dot(d_quant, probs_low, TN)
-        g_code[...] += (2.0 / SOFTMAX_WARMTH) * dot(latent_low, d_logits, TN)
+        ones = jnp.ones((count, 16), BF16)
+        both = dot(jnp.concatenate([latent_low, ones], axis=1), d_logits, TN)
+        size = latent.shape[1]
+        g_code[...] += (2.0 / SOFTMAX_WARMTH) * both[:size]
+        totals[...] += both[size : size + 1]
         yield
         d_pre = (slope * dot(d_resid, mixer[...], NT)).astype(BF16)
         g_proj[...] += dot(d_latent, resid, TN)
         yield
-        d_pre_out[n] = d_pre.reshape(height, wide, channels)
+        d_pre_out[image] = d_pre.reshape(height, wide, channels)
         top, bottom = d_pre[:wide], d_pre[count - wide :]
         near_out[n] = jnp.where(lead, bottom, top)
         far_out[n] = jnp.where(lead, top, bottom)
@@ -205,30 +217,20 @@
     live = [chain(n) for n in range(batch)]
     while live:
         live = [c for c in live if next(c, True) is None]
+    bigs = ((decoded, decoded_far), (d_pre_out, d_pre_far), (d_resid_out, d_resid_far))
+
+    def store(n, number):
+        part = pl.ds(number * batch, batch)
+        return pltpu.make_async_copy(bigs[n][0].at[part], bigs[n][1].at[part], big_sems.at[n, number])
+
+    for n in range(3):
+        store(n, step).start()
 
     @pl.when(step == steps - 1)
     def _():
-        for a in range(3):
-            for b in range(3):
-                block = weights[2 - a, (2 - b) * channels : (3 - b) * channels, :]
-                weights_back[a, b * channels : (b + 1) * channels, :] = block.T
-        for line in range(3):
-            total = None
-            for n in range(images):
-                term = dot(d_pre_turned[n], framed[n, line * wide : line * wide + count, :])
-                total = term if total is None else total + term
-            sums[line] = total
-        for ref in (keep, send):
-            ref[...] = jnp.zeros_like(ref)
         quarter = tile // 4
-        for t in range(40):
-            i, j = (t // 2) % 2, t % 2
-            if t < 36:
-                p = t // 4
-                left = (p % 3) * channels + i * tile
-                block = sums[p // 3, j * tile : (j + 1) * tile, left : left + tile]
-            else:
-                block = g_mixer[j * tile : (j + 1) * tile, i * tile : (i + 1) * tile]
+
+        def put(t, block):
             block = block.astype(BF16)
             for q in range(0, 4, 2):
                 even = block[q * quarter : (q + 1) * quarter]
@@ -236,6 +238,19 @@
                 row = pl.ds(pl.multiple_of(slots[t] * quarter, quarter), quarter)
                 keep[q // 2, row] = jnp.where(lead, even, odd)
                 send[q // 2, row] = jnp.where(lead, odd, even)
+
+        for t in range(36, 40):
+            i, j = (t // 2) % 2, t % 2
+            put(t, g_mixer[j * tile : (j + 1) * tile, i * tile : (i + 1) * tile])
+        for line in range(3):
+            total = None
+            for n in range(images):
+                term = dot(d_pre_turned[n], framed[n, line * wide : line * wide + count, :])
+                total = term if total is None else total + term
+            for t in range(12 * line, 12 * line + 12):
+                i, j = (t // 2) % 2, t % 2
+                left = (t // 4 % 3) * channels + i * tile
+                put(t, total[j * tile : (j + 1) * tile, left : left + tile])
         g_words = g_code[...] - (2.0 / SOFTMAX_WARMTH) * totals[...] * code[...].astype(F32)
         blocks = []
         for grad in (g_proj[...], g_dec[...], g_words):
@@ -254,6 +269,10 @@
         value = jnp.broadcast_to(loss[...] * (1.0 / LOSS_ROWS), (LOSS_ROWS, loss.shape[1]))
         keep[0, row:, 0 : loss.shape[1]] = jnp.where(lead, value, 0.0).astype(BF16)
         send[0, row:, 0 : loss.shape[1]] = jnp.where(lead, 0.0, value).astype(BF16)
+        for number in range(images // batch):
+            for n in range(3):
+                store(n, number).wait()
+        pltpu.make_async_copy(weights_back, weights_far, weight_sem).wait()
 
 
 def main_call(ids, places, slots, present, feat, near, far, cot, parts, proj, dec, code):
@@ -265,6 +284,7 @@
     smem = pl.BlockSpec(memory_space=pltpu.SMEM)
     strip = pl.BlockSpec((batch, height, wide, channels), lambda i: (i, 0, 0, 0))
     line = pl.BlockSpec((batch, wide, channels), lambda i: (i, 0, 0))
+    hbm = pl.BlockSpec(memory_space=pl.ANY)
 
     def whole(shape):
         return pl.BlockSpec(shape, lambda i: (0,) * len(shape))
@@ -281,14 +301,13 @@
         in_specs=[smem] * 4
         + [whole((1, present.shape[0])), strip, line, line, strip]
         + [whole(a.shape) for a in (*parts, proj, dec, code)],
-        out_specs=[strip] * 3 + [line] * 2 + [whole(s.shape) for s in shapes[5:]],
+        out_specs=[hbm] * 3 + [line] * 2 + [hbm] + [whole(s.shape) for s in shapes[6:]],
         out_shape=shapes,
         scratch_shapes=[
             pltpu.VMEM((3, 3 * channels, channels), BF16),
             pltpu.VMEM((channels, channels), BF16),
             pltpu.VMEM((images, (height + 2) * wide, 3 * channels), BF16),
             pltpu.VMEM((images, channels, height * wide), BF16),
-            pltpu.VMEM((3, channels, 3 * channels), F32),
             pltpu.VMEM((channels, channels), F32),
             pltpu.VMEM((latent, channels), F32),
             pltpu.VMEM((latent, channels), F32),
@@ -300,6 +319,12 @@
             pltpu.VMEM(code.shape, BF16),
             pltpu.VMEM((1, words), F32),
             pltpu.SMEM((1,), F32),
+            pltpu.VMEM(feat.shape, BF16),
+            pltpu.VMEM(feat.shape, BF16),
+            pltpu.VMEM(feat.shape, BF16),
+            pltpu.VMEM(weights.shape, BF16),
+            pltpu.SemaphoreType.DMA((3, images // batch)),
+            pltpu.SemaphoreType.DMA,
         ],
         compiler_params=pltpu.CompilerParams(vmem_limit_bytes=MAIN_VMEM),
         name="main",

time: 117 us -> 116 us (level)
  Pallas kernels: 65.1 us -> 63.4 us
    pallas_call x1, Pallas kernels: 37.9 us -> 36.3 us  [main_call(): pl.pallas_call(lambda *refs: main_kernel(batch, len(parts), *refs), grid=...]
  transfers between devices with their start and end apart: 23 -> 23, of which waited for: 9 -> 9; matrix products, arithmetic and copies ran while one was open for 3% -> 3% of each run, Pallas kernels for 8% -> 9%
where the time goes in v6:
time: 116 us; the launch traced here: 115 us
  Pallas kernels  63.4 us (55%)
  waiting for transfers between devices  23.6 us (20%)
  starting transfers between devices  20 us (17%)
  other arithmetic  4.53 us (4%)
  local copies, waits for them, and re-layouts  2.39 us (2%)
  between operations  1.2 us (1%)
    pallas_call x1, Pallas kernels, main_call(): pl.pallas_call(lambda *refs: main_kernel(batch, len(parts), *refs), grid=...  36.3 us
    ppermute x18, waiting for transfers between devices, swap(): return lax.ppermute(x, axis, [(i, i ^ distance) for i in range(count)])  23.6 us
    pallas_call x1, Pallas kernels, finish_call(): pl.pallas_call(finish_kernel, in_specs=[smem] + [vmem] * 21 + [hbm] * len...  17.4 us
    ppermute x18, starting transfers between devices, swap(): return lax.ppermute(x, axis, [(i, i ^ distance) for i in range(count)])  15 us
    pallas_call x1, Pallas kernels, inner_call(): pl.pallas_call(lambda *refs: inner_kernel(batch, *refs), grid=(images //...  9.83 us
    ppermute x3, starting transfers between devices, reduce_all(): piece = lax.ppermute(piece, ('strip', 'img'), pairs)  3.62 us
  transfers between devices with their start and end apart: 23, of which 9 were waited for; matrix products, arithmetic and copies ran while one was open for 3% of the time, Pallas kernels for 9%

profile of v6, /device:TPU:0, one launch (start us, length us, event | category | flops | bytes accessed | tf_op | source)
XLA Modules:
  0.0 115.2 jit_solution(6297482499777648818)
XLA Ops:
  0.7 0.9 dynamic-slice_convert_fusion
  1.6 4.1 %collective-permute-start.1 = (bf16[5,64,128]{2,1,0:T(8,128)(2,1)S(1)}, bf16[5,64,128]{2,1,0:T(8,128)(2,1)S(1)}, u32[]{:S(2)}, u32[]{:S(2)}) collective-permute-start(bf16[5,64,128]{2,1,0:T(8,128)(2,1)S(1)} %dynamic-slice_convert_fusion), channel_id=1, source_target_pairs={{0,4},{1,5},{2,6},{3,7},{4,0},{5,1},{6,2},{7,3},{8,12},{9,13},{10,... | collective-permute-start | bytes 245768 | tf_op jit(solution)/shard_map/ppermute | solution.py:684
  5.7 1.6 %collective-permute-start = (bf16[5,64,128]{2,1,0:T(8,128)(2,1)S(1)}, bf16[5,64,128]{2,1,0:T(8,128)(2,1)S(1)}, u32[]{:S(2)}, u32[]{:S(2)}) collective-permute-start(bf16[5,64,128]{2,1,0:T(8,128)(2,1)S(1)} %dynamic-slice_convert_fusion), channel_id=1, source_target_pairs={{0,2},{1,3},{2,0},{3,1},{4,6},{5,7},{6,4},{7,5},{8,10},{9,11},{10,... | collective-permute-start | bytes 245768 | tf_op jit(solution)/shard_map/ppermute | solution.py:684
  7.3 1.1 fusion.1
  9.1 1.2 %fusion.3.refs_1_ = s32[40]{0:T(128)} fusion(s32[40]{0:T(128)} %refs_2_.1, s32[]{:T(128)} %axis_index.17), kind=kLoop, calls=%fused_computation.40 | loop fusion | flops 1880 | bytes 324 | tf_op jit(solution)/shard_map/add | solution.py:725
  11.0 2.5 %collective-permute-done.2 = bf16[5,64,128]{2,1,0:T(8,128)(2,1)S(1)} collective-permute-done((bf16[5,64,128]{2,1,0:T(8,128)(2,1)S(1)}, bf16[5,64,128]{2,1,0:T(8,128)(2,1)S(1)}, u32[]{:S(2)}, u32[]{:S(2)}) %collective-permute-start.2) | collective-permute-done | bytes 81952 | tf_op jit(solution)/shard_map/ppermute | solution.py:684
  14.3 1.5 %collective-permute-start.5 = (bf16[10,64,128]{2,1,0:T(8,128)(2,1)S(1)}, bf16[10,64,128]{2,1,0:T(8,128)(2,1)S(1)}, u32[]{:S(2)}, u32[]{:S(2)}) collective-permute-start(bf16[10,64,128]{2,1,0:T(8,128)(2,1)S(1)} %pad_maximum_fusion.4.refs_9_), channel_id=1, source_target_pairs={{0,1},{1,0},{2,3},{3,2},{4,5},{5,4},{6,7},{7,6},{8,9},{9,8},{10,11... | collective-permute-start | bytes 491528 | tf_op jit(solution)/shard_map/ppermute | solution.py:684
  16.3 5.0 %collective-permute-done.5.refs_11_ = bf16[10,64,128]{2,1,0:T(8,128)(2,1)S(1)} collective-permute-done((bf16[10,64,128]{2,1,0:T(8,128)(2,1)S(1)}, bf16[10,64,128]{2,1,0:T(8,128)(2,1)S(1)}, u32[]{:S(2)}, u32[]{:S(2)}) %collective-permute-start.5) | collective-permute-done | bytes 163872 | tf_op jit(solution)/shard_map/ppermute | solution.py:684
  21.3 3.1 %collective-permute-done.6.refs_12_ = bf16[10,64,128]{2,1,0:T(8,128)(2,1)S(1)} collective-permute-done((bf16[10,64,128]{2,1,0:T(8,128)(2,1)S(1)}, bf16[10,64,128]{2,1,0:T(8,128)(2,1)S(1)}, u32[]{:S(2)}, u32[]{:S(2)}) %collective-permute-start.6) | collective-permute-done | bytes 163872 | tf_op jit(solution)/shard_map/ppermute | solution.py:684
  24.4 1.3 %collective-permute-done.10.refs_16_ = bf16[10,64,128]{2,1,0:T(8,128)(2,1)S(1)} collective-permute-done((bf16[10,64,128]{2,1,0:T(8,128)(2,1)S(1)}, bf16[10,64,128]{2,1,0:T(8,128)(2,1)S(1)}, u32[]{:S(2)}, u32[]{:S(2)}) %collective-permute-start.10) | collective-permute-done | bytes 163872 | tf_op jit(solution)/shard_map/ppermute | solution.py:684
  26.4 36.3 %main.1 = (bf16[20,8,32,256]{3,2,1,0:T(8,128)(2,1)}, bf16[20,8,32,256]{3,2,1,0:T(8,128)(2,1)}, bf16[20,8,32,256]{3,2,1,0:T(8,128)(2,1)}, bf16[20,32,256]{2,1,0:T...) custom-call(s32[2]{0:T(128)} %pad_add_fusion.refs_0_, ...), custom_call_target="tpu_custom_call" | custom-call | tf_op jit(solution)/shard_map/main/pallas_call | solution.py:298
  62.9 2.3 %collective-permute-done.11 = bf16[2,1424,128]{2,1,0:T(8,128)(2,1)S(1)} collective-permute-done((bf16[2,1424,128]{2,1,0:T(8,128)(2,1)}, bf16[2,1424,128]{2,1,0:T(8,128)(2,1)S(1)}, u32[]{:S(2)}, u32[]{:S(2)}) %collective-permute-start.11) | collective-permute-done | bytes 729120 | tf_op jit(solution)/shard_map/ppermute | solution.py:684
  65.1 1.3 %add.98 = bf16[2,1424,128]{2,1,0:T(8,128)(2,1)S(1)} add(bf16[2,1424,128]{2,1,0:T(8,128)(2,1)} %get-tuple-element.64, bf16[2,1424,128]{2,1,0:T(8,128)(2,1)S(1)} %collective-permute-done.11) | non-fusion elementwise | flops 364544 | bytes 2187264 | tf_op jit(solution)/shard_map/add | solution.py:744
  66.6 1.6 %collective-permute-start.12 = (bf16[784,128]{1,0:T(8,128)(2,1)S(1)}, bf16[784,128]{1,0:T(8,128)(2,1)S(1)}, u32[]{:S(2)}, u32[]{:S(2)}) collective-permute-start(bf16[784,128]{1,0:T(8,128)(2,1)S(1)} %get-tuple-element.118), channel_id=1, source_target_pairs={{0,1},{1,0},{2,3},{3,2},{4,5},{5,4},{6,7},{7,6},{8,9},{9,8},{10,11... | collective-permute-start | bytes 602120 | tf_op jit(solution)/shard_map/ppermute | solution.py:760
  68.2 1.1 collective-permute-start.14
  69.4 0.9 collective-permute-start.13
  70.3 9.8 %inner_lines.1.refs_28_ = bf16[20,8,32,256]{3,2,1,0:T(8,128)(2,1)} custom-call(bf16[3,768,256]{2,1,0:T(8,128)(2,1)} %get-tuple-element.70.refs_0_.refs_22_, bf16[20,8,32,256]{3,2,1,0:T(8,128)(2,1)} %refs_23_.1, bf16[20,8,32,256]{3,2,1,0:T(8,128)(2,1)} %get-tuple-element.72.refs_2_.refs_24_, bf16[20,8,32,256]{3,2,1,0:T(8,128)(2,1)} %get-tuple-element.73.refs_3_.refs_25_), custom_call_target="tpu_custom_call" | custom-call | tf_op jit(solution)/shard_map/inner_lines/pallas_call | solution.py:467
  81.1 3.5 %collective-permute-start.16 = (bf16[304,128]{1,0:T(8,128)(2,1)S(1)}, bf16[304,128]{1,0:T(8,128)(2,1)S(1)}, u32[]{:S(2)}, u32[]{:S(2)}) collective-permute-start(bf16[304,128]{1,0:T(8,128)(2,1)S(1)} %get-tuple-element.114), channel_id=1, source_target_pairs={{0,4},{1,5},{2,6},{3,7},{4,0},{5,1},{6,2},{7,3},{8,12},{9,13},{10,... | collective-permute-start | bytes 233480 | tf_op jit(solution)/shard_map/ppermute | solution.py:684
  85.5 4.0 %collective-permute-done.16 = bf16[304,128]{1,0:T(8,128)(2,1)S(1)} collective-permute-done((bf16[304,128]{1,0:T(8,128)(2,1)S(1)}, bf16[304,128]{1,0:T(8,128)(2,1)S(1)}, u32[]{:S(2)}, u32[]{:S(2)}) %collective-permute-start.16) | collective-permute-done | bytes 77856 | tf_op jit(solution)/shard_map/ppermute | solution.py:684
  89.4 1.4 %collective-permute-done.17 = bf16[304,128]{1,0:T(8,128)(2,1)S(1)} collective-permute-done((bf16[304,128]{1,0:T(8,128)(2,1)S(1)}, bf16[304,128]{1,0:T(8,128)(2,1)S(1)}, u32[]{:S(2)}, u32[]{:S(2)}) %collective-permute-start.17) | collective-permute-done | bytes 77856 | tf_op jit(solution)/shard_map/ppermute | solution.py:684
  91.3 1.5 %collective-permute-start.18 = (bf16[304,128]{1,0:T(8,128)(2,1)S(1)}, bf16[304,128]{1,0:T(8,128)(2,1)S(1)}, u32[]{:S(2)}, u32[]{:S(2)}) collective-permute-start(bf16[304,128]{1,0:T(8,128)(2,1)S(1)} %add_convert_fusion.1.refs_2_), channel_id=1, source_target_pairs={{0,8},{8,0},{16,24},{24,16},{1,9},{9,1},{17,25},{25,17},{2,10},{10... | collective-permute-start | bytes 233480 | tf_op jit(solution)/shard_map/ppermute | solution.py:684
  92.9 2.8 %collective-permute-done.20.refs_5_ = bf16[304,128]{1,0:T(8,128)(2,1)S(1)} collective-permute-done((bf16[304,128]{1,0:T(8,128)(2,1)S(1)}, bf16[304,128]{1,0:T(8,128)(2,1)S(1)}, u32[]{:S(2)}, u32[]{:S(2)}) %collective-permute-start.20) | collective-permute-done | bytes 77856 | tf_op jit(solution)/shard_map/ppermute | solution.py:684
  95.7 1.3 %collective-permute-done.19.refs_4_ = bf16[304,128]{1,0:T(8,128)(2,1)S(1)} collective-permute-done((bf16[304,128]{1,0:T(8,128)(2,1)S(1)}, bf16[304,128]{1,0:T(8,128)(2,1)S(1)}, u32[]{:S(2)}, u32[]{:S(2)}) %collective-permute-start.19) | collective-permute-done | bytes 77856 | tf_op jit(solution)/shard_map/ppermute | solution.py:684
  97.6 17.4 %finish.1 = (f32[5,128,128]{2,1,0:T(8,128)}, f32[5,128,128]{2,1,0:T(8,128)}, f32[5,128,128]{2,1,0:T(8,128)}, f32[5,128,128]{2,1,0:T(8,128)}, f32[5,128,128]{2,1,...) custom-call(s32[2]{0:T(128)} %pad_add_fusion.refs_0_, ...), custom_call_target="tpu_custom_call", output_to_operand_aliasing={{17}: (28, {})} | custom-call | tf_op jit(solution)/shard_map/finish/pallas_call | solution.py:646
  (79 shorter events, 6.6 us)
Async XLA Ops:
  1.6 9.4 %collective-permute-start.1 = (bf16[5,64,128]{2,1,0:T(8,128)(2,1)S(1)}, bf16[5,64,128]{2,1,0:T(8,128)(2,1)S(1)}, u32[]{:S(2)}, u32[]{:S(2)}) collective-permute-start(bf16[5,64,128]{2,1,0:T(8,128)(2,1)S(1)} %dynamic-slice_convert_fusion), channel_id=1, source_target_pairs={{0,4},{1,5},{2,6},{3,7},{4,0},{5,1},{6,2},{7,3},{8,12},{9,13},{10,... | collective-permute-start | bytes 245768 | tf_op jit(solution)/shard_map/ppermute | solution.py:684
  5.7 5.2 %collective-permute-start = (bf16[5,64,128]{2,1,0:T(8,128)(2,1)S(1)}, bf16[5,64,128]{2,1,0:T(8,128)(2,1)S(1)}, u32[]{:S(2)}, u32[]{:S(2)}) collective-permute-start(bf16[5,64,128]{2,1,0:T(8,128)(2,1)S(1)} %dynamic-slice_convert_fusion), channel_id=1, source_target_pairs={{0,2},{1,3},{2,0},{3,1},{4,6},{5,7},{6,4},{7,5},{8,10},{9,11},{10,... | collective-permute-start | bytes 245768 | tf_op jit(solution)/shard_map/ppermute | solution.py:684
  7.3 6.2 %collective-permute-start.2 = (bf16[5,64,128]{2,1,0:T(8,128)(2,1)S(1)}, bf16[5,64,128]{2,1,0:T(8,128)(2,1)S(1)}, u32[]{:S(2)}, u32[]{:S(2)}) collective-permute-start(bf16[5,64,128]{2,1,0:T(8,128)(2,1)S(1)} %dynamic-slice_convert_fusion), channel_id=1, source_target_pairs={{0,6},{1,7},{2,4},{3,5},{4,2},{5,3},{6,0},{7,1},{8,14},{9,15},{10,... | collective-permute-start | bytes 245768 | tf_op jit(solution)/shard_map/ppermute | solution.py:684
  8.4 15.9 %collective-permute-start.4 = (bf16[20,32,256]{2,1,0:T(8,128)(2,1)S(1)}, bf16[20,32,256]{2,1,0:T(8,128)(2,1)S(1)}, u32[]{:S(2)}, u32[]{:S(2)}) collective-permute-start(bf16[20,32,256]{2,1,0:T(8,128)(2,1)S(1)} %get-tuple-element.99), channel_id=1, source_target_pairs={{8,16},{16,8},{9,17},{17,9},{10,18},{18,10},{11,19},{19,11},{12,20... | collective-permute-start | bytes 983048 | tf_op jit(solution)/shard_map/ppermute | solution.py:699
  11.0 14.7 %copy-start = (bf16[10,64,128]{2,1,0:T(8,128)(2,1)}, bf16[10,64,128]{2,1,0:T(8,128)(2,1)S(1)}, u32[]{:S(2)}) copy-start(bf16[10,64,128]{2,1,0:T(8,128)(2,1)S(1)} %pad_maximum_fusion.4.refs_9_) | copy-start | bytes 491524
  13.6 2.7 %collective-permute-start.7 = (bf16[10,64,128]{2,1,0:T(8,128)(2,1)S(1)}, bf16[10,64,128]{2,1,0:T(8,128)(2,1)S(1)}, u32[]{:S(2)}, u32[]{:S(2)}) collective-permute-start(bf16[10,64,128]{2,1,0:T(8,128)(2,1)S(1)} %pad_maximum_fusion.4.refs_9_), channel_id=1, source_target_pairs={{0,8},{8,0},{16,24},{24,16},{1,9},{9,1},{17,25},{25,17},{2,10},{10... | collective-permute-start | bytes 491528 | tf_op jit(solution)/shard_map/ppermute | solution.py:684
  14.2 10.2 %collective-permute-start.3 = (bf16[20,32,256]{2,1,0:T(8,128)(2,1)S(1)}, bf16[20,32,256]{2,1,0:T(8,128)(2,1)S(1)}, u32[]{:S(2)}, u32[]{:S(2)}) collective-permute-start(bf16[20,32,256]{2,1,0:T(8,128)(2,1)S(1)} %get-tuple-element.100), channel_id=1, source_target_pairs={{0,8},{8,0},{16,24},{24,16},{1,9},{9,1},{17,25},{25,17},{2,10},{10... | collective-permute-start | bytes 983048 | tf_op jit(solution)/shard_map/ppermute | solution.py:684
  14.3 7.0 %collective-permute-start.5 = (bf16[10,64,128]{2,1,0:T(8,128)(2,1)S(1)}, bf16[10,64,128]{2,1,0:T(8,128)(2,1)S(1)}, u32[]{:S(2)}, u32[]{:S(2)}) collective-permute-start(bf16[10,64,128]{2,1,0:T(8,128)(2,1)S(1)} %pad_maximum_fusion.4.refs_9_), channel_id=1, source_target_pairs={{0,1},{1,0},{2,3},{3,2},{4,5},{5,4},{6,7},{7,6},{8,9},{9,8},{10,11... | collective-permute-start | bytes 491528 | tf_op jit(solution)/shard_map/ppermute | solution.py:684
  15.8 8.5 %collective-permute-start.6 = (bf16[10,64,128]{2,1,0:T(8,128)(2,1)S(1)}, bf16[10,64,128]{2,1,0:T(8,128)(2,1)S(1)}, u32[]{:S(2)}, u32[]{:S(2)}) collective-permute-start(bf16[10,64,128]{2,1,0:T(8,128)(2,1)S(1)} %pad_maximum_fusion.5.refs_10_), channel_id=1, source_target_pairs={{0,1},{1,0},{2,3},{3,2},{4,5},{5,4},{6,7},{7,6},{8,9},{9,8},{10,11... | collective-permute-start | bytes 491528 | tf_op jit(solution)/shard_map/ppermute | solution.py:684
  16.3 8.0 %collective-permute-start.8 = (bf16[10,64,128]{2,1,0:T(8,128)(2,1)S(1)}, bf16[10,64,128]{2,1,0:T(8,128)(2,1)S(1)}, u32[]{:S(2)}, u32[]{:S(2)}) collective-permute-start(bf16[10,64,128]{2,1,0:T(8,128)(2,1)S(1)} %pad_maximum_fusion.5.refs_10_), channel_id=1, source_target_pairs={{0,8},{8,0},{16,24},{24,16},{1,9},{9,1},{17,25},{25,17},{2,10},{10... | collective-permute-start | bytes 491528 | tf_op jit(solution)/shard_map/ppermute | solution.py:684
  21.3 3.1 %collective-permute-start.9 = (bf16[10,64,128]{2,1,0:T(8,128)(2,1)S(1)}, bf16[10,64,128]{2,1,0:T(8,128)(2,1)S(1)}, u32[]{:S(2)}, u32[]{:S(2)}) collective-permute-start(bf16[10,64,128]{2,1,0:T(8,128)(2,1)S(1)} %collective-permute-done.5.refs_11_), channel_id=1, source_target_pairs={{0,8},{8,0},{16,24},{24,16},{1,9},{9,1},{17,25},{25,17},{2,10},{10... | collective-permute-start | bytes 491528 | tf_op jit(solution)/shard_map/ppermute | solution.py:684
  24.3 1.4 %collective-permute-start.10 = (bf16[10,64,128]{2,1,0:T(8,128)(2,1)S(1)}, bf16[10,64,128]{2,1,0:T(8,128)(2,1)S(1)}, u32[]{:S(2)}, u32[]{:S(2)}) collective-permute-start(bf16[10,64,128]{2,1,0:T(8,128)(2,1)S(1)} %collective-permute-done.6.refs_12_), channel_id=1, source_target_pairs={{0,8},{8,0},{16,24},{24,16},{1,9},{9,1},{17,25},{25,17},{2,10},{10... | collective-permute-start | bytes 491528 | tf_op jit(solution)/shard_map/ppermute | solution.py:684
  62.6 2.5 %collective-permute-start.11 = (bf16[2,1424,128]{2,1,0:T(8,128)(2,1)}, bf16[2,1424,128]{2,1,0:T(8,128)(2,1)S(1)}, u32[]{:S(2)}, u32[]{:S(2)}) collective-permute-start(bf16[2,1424,128]{2,1,0:T(8,128)(2,1)} %get-tuple-element.65), channel_id=1, source_target_pairs={{0,8},{8,0},{16,24},{24,16},{1,9},{9,1},{17,25},{25,17},{2,10},{10... | collective-permute-start | bytes 2187272 | tf_op jit(solution)/shard_map/ppermute | solution.py:684
  66.6 13.5 %collective-permute-start.12 = (bf16[784,128]{1,0:T(8,128)(2,1)S(1)}, bf16[784,128]{1,0:T(8,128)(2,1)S(1)}, u32[]{:S(2)}, u32[]{:S(2)}) collective-permute-start(bf16[784,128]{1,0:T(8,128)(2,1)S(1)} %get-tuple-element.118), channel_id=1, source_target_pairs={{0,1},{1,0},{2,3},{3,2},{4,5},{5,4},{6,7},{7,6},{8,9},{9,8},{10,11... | collective-permute-start | bytes 602120 | tf_op jit(solution)/shard_map/ppermute | solution.py:760
  68.2 11.9 %collective-permute-start.14 = (bf16[784,128]{1,0:T(8,128)(2,1)S(1)}, bf16[784,128]{1,0:T(8,128)(2,1)S(1)}, u32[]{:S(2)}, u32[]{:S(2)}) collective-permute-start(bf16[784,128]{1,0:T(8,128)(2,1)S(1)} %get-tuple-element.116), channel_id=1, source_target_pairs={{0,17},{1,16},{2,19},{3,18},{4,21},{5,20},{6,23},{7,22},{8,25},{9,... | collective-permute-start | bytes 602120 | tf_op jit(solution)/shard_map/ppermute | solution.py:760
  69.4 10.8 %collective-permute-start.13 = (bf16[784,128]{1,0:T(8,128)(2,1)S(1)}, bf16[784,128]{1,0:T(8,128)(2,1)S(1)}, u32[]{:S(2)}, u32[]{:S(2)}) collective-permute-start(bf16[784,128]{1,0:T(8,128)(2,1)S(1)} %get-tuple-element.117), channel_id=1, source_target_pairs={{0,16},{1,17},{2,18},{3,19},{4,20},{5,21},{6,22},{7,23},{8,24},{9,... | collective-permute-start | bytes 602120 | tf_op jit(solution)/shard_map/ppermute | solution.py:760
  80.3 5.2 %collective-permute-start.15 = (bf16[304,128]{1,0:T(8,128)(2,1)S(1)}, bf16[304,128]{1,0:T(8,128)(2,1)S(1)}, u32[]{:S(2)}, u32[]{:S(2)}) collective-permute-start(bf16[304,128]{1,0:T(8,128)(2,1)S(1)} %get-tuple-element.113), channel_id=1, source_target_pairs={{0,2},{1,3},{2,0},{3,1},{4,6},{5,7},{6,4},{7,5},{8,10},{9,11},{10,... | collective-permute-start | bytes 233480 | tf_op jit(solution)/shard_map/ppermute | solution.py:684
  81.1 8.4 %collective-permute-start.16 = (bf16[304,128]{1,0:T(8,128)(2,1)S(1)}, bf16[304,128]{1,0:T(8,128)(2,1)S(1)}, u32[]{:S(2)}, u32[]{:S(2)}) collective-permute-start(bf16[304,128]{1,0:T(8,128)(2,1)S(1)} %get-tuple-element.114), channel_id=1, source_target_pairs={{0,4},{1,5},{2,6},{3,7},{4,0},{5,1},{6,2},{7,3},{8,12},{9,13},{10,... | collective-permute-start | bytes 233480 | tf_op jit(solution)/shard_map/ppermute | solution.py:684
  84.6 6.3 %collective-permute-start.17 = (bf16[304,128]{1,0:T(8,128)(2,1)S(1)}, bf16[304,128]{1,0:T(8,128)(2,1)S(1)}, u32[]{:S(2)}, u32[]{:S(2)}) collective-permute-start(bf16[304,128]{1,0:T(8,128)(2,1)S(1)} %get-tuple-element.115), channel_id=1, source_target_pairs={{0,6},{1,7},{2,4},{3,5},{4,2},{5,3},{6,0},{7,1},{8,14},{9,15},{10,... | collective-permute-start | bytes 233480 | tf_op jit(solution)/shard_map/ppermute | solution.py:684
  84.8 8.1 %collective-permute-start.21 = (bf16[20,32,256]{2,1,0:T(8,128)(2,1)S(1)}, bf16[20,32,256]{2,1,0:T(8,128)(2,1)S(1)}, u32[]{:S(2)}, u32[]{:S(2)}) collective-permute-start(bf16[20,32,256]{2,1,0:T(8,128)(2,1)S(1)} %copy-done.17), channel_id=1, source_target_pairs={{0,8},{8,0},{16,24},{24,16},{1,9},{9,1},{17,25},{25,17},{2,10},{10... | collective-permute-start | bytes 983048 | tf_op jit(solution)/shard_map/ppermute | solution.py:684
  84.8 8.1 %collective-permute-start.22 = (bf16[20,32,256]{2,1,0:T(8,128)(2,1)S(1)}, bf16[20,32,256]{2,1,0:T(8,128)(2,1)S(1)}, u32[]{:S(2)}, u32[]{:S(2)}) collective-permute-start(bf16[20,32,256]{2,1,0:T(8,128)(2,1)S(1)} %copy-done.16), channel_id=1, source_target_pairs={{8,16},{16,8},{9,17},{17,9},{10,18},{18,10},{11,19},{19,11},{12,20... | collective-permute-start | bytes 983048 | tf_op jit(solution)/shard_map/ppermute | solution.py:699
  90.9 4.8 %collective-permute-start.20 = (bf16[304,128]{1,0:T(8,128)(2,1)S(1)}, bf16[304,128]{1,0:T(8,128)(2,1)S(1)}, u32[]{:S(2)}, u32[]{:S(2)}) collective-permute-start(bf16[304,128]{1,0:T(8,128)(2,1)S(1)} %add_convert_fusion.1.refs_2_), channel_id=1, source_target_pairs={{0,24},{8,16},{16,8},{24,0},{1,25},{9,17},{17,9},{25,1},{2,26},{10... | collective-permute-start | bytes 233480 | tf_op jit(solution)/shard_map/ppermute | solution.py:684
  91.0 6.0 %collective-permute-start.19 = (bf16[304,128]{1,0:T(8,128)(2,1)S(1)}, bf16[304,128]{1,0:T(8,128)(2,1)S(1)}, u32[]{:S(2)}, u32[]{:S(2)}) collective-permute-start(bf16[304,128]{1,0:T(8,128)(2,1)S(1)} %add_convert_fusion.1.refs_2_), channel_id=1, source_target_pairs={{0,16},{8,24},{16,0},{24,8},{1,17},{9,25},{17,1},{25,9},{2,18},{10... | collective-permute-start | bytes 233480 | tf_op jit(solution)/shard_map/ppermute | solution.py:684
  91.3 5.7 %collective-permute-start.18 = (bf16[304,128]{1,0:T(8,128)(2,1)S(1)}, bf16[304,128]{1,0:T(8,128)(2,1)S(1)}, u32[]{:S(2)}, u32[]{:S(2)}) collective-permute-start(bf16[304,128]{1,0:T(8,128)(2,1)S(1)} %add_convert_fusion.1.refs_2_), channel_id=1, source_target_pairs={{0,8},{8,0},{16,24},{24,16},{1,9},{9,1},{17,25},{25,17},{2,10},{10... | collective-permute-start | bytes 233480 | tf_op jit(solution)/shard_map/ppermute | solution.py:684
  (17 other events, 79.8 us)

commit v7 on v6

--- a/solution.py
+++ b/solution.py
@@ -280,7 +280,7 @@
     latent, words = code.shape
     size, half, tile = parts[0].shape
     slot_count = size * len(parts) // 2
-    batch = 5 if images % 5 == 0 else 1
+    batch = 4 if images % 4 == 0 else 1
     smem = pl.BlockSpec(memory_space=pltpu.SMEM)
     strip = pl.BlockSpec((batch, height, wide, channels), lambda i: (i, 0, 0, 0))
     line = pl.BlockSpec((batch, wide, channels), lambda i: (i, 0, 0))
@@ -519,7 +519,7 @@
     yield
 
 
-EDGE_GROUP = 4
+EDGE_GROUP = 2
 
 
 def finish_kernel(*refs):

time: 116 us -> 116 us (level)
  no operation moved by 1% of the time
where the time goes in v7:
time: 116 us; the launch traced here: 115 us
  Pallas kernels  63.6 us (55%)
  waiting for transfers between devices  23.7 us (20%)
  starting transfers between devices  19.9 us (17%)
  other arithmetic  4.53 us (4%)
  local copies, waits for them, and re-layouts  2.39 us (2%)
  between operations  1.2 us (1%)
    pallas_call x1, Pallas kernels, main_call(): pl.pallas_call(lambda *refs: main_kernel(batch, len(parts), *refs), grid=...  36.5 us
    ppermute x18, waiting for transfers between devices, swap(): return lax.ppermute(x, axis, [(i, i ^ distance) for i in range(count)])  23.7 us
    pallas_call x1, Pallas kernels, finish_call(): pl.pallas_call(finish_kernel, in_specs=[smem] + [vmem] * 21 + [hbm] * len...  17.2 us
    ppermute x18, starting transfers between devices, swap(): return lax.ppermute(x, axis, [(i, i ^ distance) for i in range(count)])  15 us
    pallas_call x1, Pallas kernels, inner_call(): pl.pallas_call(lambda *refs: inner_kernel(batch, *refs), grid=(images //...  9.99 us
    ppermute x3, starting transfers between devices, reduce_all(): piece = lax.ppermute(piece, ('strip', 'img'), pairs)  3.62 us
  transfers between devices with their start and end apart: 23, of which 9 were waited for; matrix products, arithmetic and copies ran while one was open for 3% of the time, Pallas kernels for 9%

profile of v7, /device:TPU:0, one launch (start us, length us, event | category | flops | bytes accessed | tf_op | source)
XLA Modules:
  0.0 115.4 jit_solution(5233203261748902486)
XLA Ops:
  0.7 0.9 dynamic-slice_convert_fusion
  1.6 4.1 %collective-permute-start.1 = (bf16[5,64,128]{2,1,0:T(8,128)(2,1)S(1)}, bf16[5,64,128]{2,1,0:T(8,128)(2,1)S(1)}, u32[]{:S(2)}, u32[]{:S(2)}) collective-permute-start(bf16[5,64,128]{2,1,0:T(8,128)(2,1)S(1)} %dynamic-slice_convert_fusion), channel_id=1, source_target_pairs={{0,4},{1,5},{2,6},{3,7},{4,0},{5,1},{6,2},{7,3},{8,12},{9,13},{10,... | collective-permute-start | bytes 245768 | tf_op jit(solution)/shard_map/ppermute | solution.py:684
  5.7 1.6 %collective-permute-start = (bf16[5,64,128]{2,1,0:T(8,128)(2,1)S(1)}, bf16[5,64,128]{2,1,0:T(8,128)(2,1)S(1)}, u32[]{:S(2)}, u32[]{:S(2)}) collective-permute-start(bf16[5,64,128]{2,1,0:T(8,128)(2,1)S(1)} %dynamic-slice_convert_fusion), channel_id=1, source_target_pairs={{0,2},{1,3},{2,0},{3,1},{4,6},{5,7},{6,4},{7,5},{8,10},{9,11},{10,... | collective-permute-start | bytes 245768 | tf_op jit(solution)/shard_map/ppermute | solution.py:684
  7.3 1.1 fusion.1
  9.1 1.2 %fusion.3.refs_1_ = s32[40]{0:T(128)} fusion(s32[40]{0:T(128)} %refs_2_.1, s32[]{:T(128)} %axis_index.17), kind=kLoop, calls=%fused_computation.40 | loop fusion | flops 1880 | bytes 324 | tf_op jit(solution)/shard_map/add | solution.py:725
  11.0 2.5 %collective-permute-done.2 = bf16[5,64,128]{2,1,0:T(8,128)(2,1)S(1)} collective-permute-done((bf16[5,64,128]{2,1,0:T(8,128)(2,1)S(1)}, bf16[5,64,128]{2,1,0:T(8,128)(2,1)S(1)}, u32[]{:S(2)}, u32[]{:S(2)}) %collective-permute-start.2) | collective-permute-done | bytes 81952 | tf_op jit(solution)/shard_map/ppermute | solution.py:684
  14.3 1.5 %collective-permute-start.5 = (bf16[10,64,128]{2,1,0:T(8,128)(2,1)S(1)}, bf16[10,64,128]{2,1,0:T(8,128)(2,1)S(1)}, u32[]{:S(2)}, u32[]{:S(2)}) collective-permute-start(bf16[10,64,128]{2,1,0:T(8,128)(2,1)S(1)} %pad_maximum_fusion.4.refs_9_), channel_id=1, source_target_pairs={{0,1},{1,0},{2,3},{3,2},{4,5},{5,4},{6,7},{7,6},{8,9},{9,8},{10,11... | collective-permute-start | bytes 491528 | tf_op jit(solution)/shard_map/ppermute | solution.py:684
  16.3 5.0 %collective-permute-done.5.refs_11_ = bf16[10,64,128]{2,1,0:T(8,128)(2,1)S(1)} collective-permute-done((bf16[10,64,128]{2,1,0:T(8,128)(2,1)S(1)}, bf16[10,64,128]{2,1,0:T(8,128)(2,1)S(1)}, u32[]{:S(2)}, u32[]{:S(2)}) %collective-permute-start.5) | collective-permute-done | bytes 163872 | tf_op jit(solution)/shard_map/ppermute | solution.py:684
  21.3 3.1 %collective-permute-done.6.refs_12_ = bf16[10,64,128]{2,1,0:T(8,128)(2,1)S(1)} collective-permute-done((bf16[10,64,128]{2,1,0:T(8,128)(2,1)S(1)}, bf16[10,64,128]{2,1,0:T(8,128)(2,1)S(1)}, u32[]{:S(2)}, u32[]{:S(2)}) %collective-permute-start.6) | collective-permute-done | bytes 163872 | tf_op jit(solution)/shard_map/ppermute | solution.py:684
  24.4 1.3 %collective-permute-done.10.refs_16_ = bf16[10,64,128]{2,1,0:T(8,128)(2,1)S(1)} collective-permute-done((bf16[10,64,128]{2,1,0:T(8,128)(2,1)S(1)}, bf16[10,64,128]{2,1,0:T(8,128)(2,1)S(1)}, u32[]{:S(2)}, u32[]{:S(2)}) %collective-permute-start.10) | collective-permute-done | bytes 163872 | tf_op jit(solution)/shard_map/ppermute | solution.py:684
  26.4 36.5 %main.1 = (bf16[20,8,32,256]{3,2,1,0:T(8,128)(2,1)}, bf16[20,8,32,256]{3,2,1,0:T(8,128)(2,1)}, bf16[20,8,32,256]{3,2,1,0:T(8,128)(2,1)}, bf16[20,32,256]{2,1,0:T...) custom-call(s32[2]{0:T(128)} %pad_add_fusion.refs_0_, ...), custom_call_target="tpu_custom_call" | custom-call | tf_op jit(solution)/shard_map/main/pallas_call | solution.py:298
  63.0 2.3 %collective-permute-done.11 = bf16[2,1424,128]{2,1,0:T(8,128)(2,1)S(1)} collective-permute-done((bf16[2,1424,128]{2,1,0:T(8,128)(2,1)}, bf16[2,1424,128]{2,1,0:T(8,128)(2,1)S(1)}, u32[]{:S(2)}, u32[]{:S(2)}) %collective-permute-start.11) | collective-permute-done | bytes 729120 | tf_op jit(solution)/shard_map/ppermute | solution.py:684
  65.3 1.3 %add.98 = bf16[2,1424,128]{2,1,0:T(8,128)(2,1)S(1)} add(bf16[2,1424,128]{2,1,0:T(8,128)(2,1)} %get-tuple-element.64, bf16[2,1424,128]{2,1,0:T(8,128)(2,1)S(1)} %collective-permute-done.11) | non-fusion elementwise | flops 364544 | bytes 2187264 | tf_op jit(solution)/shard_map/add | solution.py:744
  66.8 1.6 %collective-permute-start.12 = (bf16[784,128]{1,0:T(8,128)(2,1)S(1)}, bf16[784,128]{1,0:T(8,128)(2,1)S(1)}, u32[]{:S(2)}, u32[]{:S(2)}) collective-permute-start(bf16[784,128]{1,0:T(8,128)(2,1)S(1)} %get-tuple-element.118), channel_id=1, source_target_pairs={{0,1},{1,0},{2,3},{3,2},{4,5},{5,4},{6,7},{7,6},{8,9},{9,8},{10,11... | collective-permute-start | bytes 602120 | tf_op jit(solution)/shard_map/ppermute | solution.py:760
  68.4 1.1 collective-permute-start.14
  69.6 0.9 collective-permute-start.13
  70.5 10.0 %inner_lines.1.refs_28_ = bf16[20,8,32,256]{3,2,1,0:T(8,128)(2,1)} custom-call(bf16[3,768,256]{2,1,0:T(8,128)(2,1)} %get-tuple-element.70.refs_0_.refs_22_, bf16[20,8,32,256]{3,2,1,0:T(8,128)(2,1)} %refs_23_.1, bf16[20,8,32,256]{3,2,1,0:T(8,128)(2,1)} %get-tuple-element.72.refs_2_.refs_24_, bf16[20,8,32,256]{3,2,1,0:T(8,128)(2,1)} %get-tuple-element.73.refs_3_.refs_25_), custom_call_target="tpu_custom_call" | custom-call | tf_op jit(solution)/shard_map/inner_lines/pallas_call | solution.py:467
  81.4 3.5 %collective-permute-start.16 = (bf16[304,128]{1,0:T(8,128)(2,1)S(1)}, bf16[304,128]{1,0:T(8,128)(2,1)S(1)}, u32[]{:S(2)}, u32[]{:S(2)}) collective-permute-start(bf16[304,128]{1,0:T(8,128)(2,1)S(1)} %get-tuple-element.114), channel_id=1, source_target_pairs={{0,4},{1,5},{2,6},{3,7},{4,0},{5,1},{6,2},{7,3},{8,12},{9,13},{10,... | collective-permute-start | bytes 233480 | tf_op jit(solution)/shard_map/ppermute | solution.py:684
  85.9 3.9 %collective-permute-done.16 = bf16[304,128]{1,0:T(8,128)(2,1)S(1)} collective-permute-done((bf16[304,128]{1,0:T(8,128)(2,1)S(1)}, bf16[304,128]{1,0:T(8,128)(2,1)S(1)}, u32[]{:S(2)}, u32[]{:S(2)}) %collective-permute-start.16) | collective-permute-done | bytes 77856 | tf_op jit(solution)/shard_map/ppermute | solution.py:684
  89.8 1.4 %collective-permute-done.17 = bf16[304,128]{1,0:T(8,128)(2,1)S(1)} collective-permute-done((bf16[304,128]{1,0:T(8,128)(2,1)S(1)}, bf16[304,128]{1,0:T(8,128)(2,1)S(1)}, u32[]{:S(2)}, u32[]{:S(2)}) %collective-permute-start.17) | collective-permute-done | bytes 77856 | tf_op jit(solution)/shard_map/ppermute | solution.py:684
  91.7 1.5 %collective-permute-start.18 = (bf16[304,128]{1,0:T(8,128)(2,1)S(1)}, bf16[304,128]{1,0:T(8,128)(2,1)S(1)}, u32[]{:S(2)}, u32[]{:S(2)}) collective-permute-start(bf16[304,128]{1,0:T(8,128)(2,1)S(1)} %add_convert_fusion.1.refs_2_), channel_id=1, source_target_pairs={{0,8},{8,0},{16,24},{24,16},{1,9},{9,1},{17,25},{25,17},{2,10},{10... | collective-permute-start | bytes 233480 | tf_op jit(solution)/shard_map/ppermute | solution.py:684
  93.2 2.8 %collective-permute-done.20.refs_5_ = bf16[304,128]{1,0:T(8,128)(2,1)S(1)} collective-permute-done((bf16[304,128]{1,0:T(8,128)(2,1)S(1)}, bf16[304,128]{1,0:T(8,128)(2,1)S(1)}, u32[]{:S(2)}, u32[]{:S(2)}) %collective-permute-start.20) | collective-permute-done | bytes 77856 | tf_op jit(solution)/shard_map/ppermute | solution.py:684
  96.1 1.3 %collective-permute-done.19.refs_4_ = bf16[304,128]{1,0:T(8,128)(2,1)S(1)} collective-permute-done((bf16[304,128]{1,0:T(8,128)(2,1)S(1)}, bf16[304,128]{1,0:T(8,128)(2,1)S(1)}, u32[]{:S(2)}, u32[]{:S(2)}) %collective-permute-start.19) | collective-permute-done | bytes 77856 | tf_op jit(solution)/shard_map/ppermute | solution.py:684
  98.0 17.2 %finish.1 = (f32[5,128,128]{2,1,0:T(8,128)}, f32[5,128,128]{2,1,0:T(8,128)}, f32[5,128,128]{2,1,0:T(8,128)}, f32[5,128,128]{2,1,0:T(8,128)}, f32[5,128,128]{2,1,...) custom-call(s32[2]{0:T(128)} %pad_add_fusion.refs_0_, ...), custom_call_target="tpu_custom_call", output_to_operand_aliasing={{17}: (28, {})} | custom-call | tf_op jit(solution)/shard_map/finish/pallas_call | solution.py:646
  (79 shorter events, 6.5 us)
Async XLA Ops:
  1.6 9.4 %collective-permute-start.1 = (bf16[5,64,128]{2,1,0:T(8,128)(2,1)S(1)}, bf16[5,64,128]{2,1,0:T(8,128)(2,1)S(1)}, u32[]{:S(2)}, u32[]{:S(2)}) collective-permute-start(bf16[5,64,128]{2,1,0:T(8,128)(2,1)S(1)} %dynamic-slice_convert_fusion), channel_id=1, source_target_pairs={{0,4},{1,5},{2,6},{3,7},{4,0},{5,1},{6,2},{7,3},{8,12},{9,13},{10,... | collective-permute-start | bytes 245768 | tf_op jit(solution)/shard_map/ppermute | solution.py:684
  5.7 5.2 %collective-permute-start = (bf16[5,64,128]{2,1,0:T(8,128)(2,1)S(1)}, bf16[5,64,128]{2,1,0:T(8,128)(2,1)S(1)}, u32[]{:S(2)}, u32[]{:S(2)}) collective-permute-start(bf16[5,64,128]{2,1,0:T(8,128)(2,1)S(1)} %dynamic-slice_convert_fusion), channel_id=1, source_target_pairs={{0,2},{1,3},{2,0},{3,1},{4,6},{5,7},{6,4},{7,5},{8,10},{9,11},{10,... | collective-permute-start | bytes 245768 | tf_op jit(solution)/shard_map/ppermute | solution.py:684
  7.3 6.2 %collective-permute-start.2 = (bf16[5,64,128]{2,1,0:T(8,128)(2,1)S(1)}, bf16[5,64,128]{2,1,0:T(8,128)(2,1)S(1)}, u32[]{:S(2)}, u32[]{:S(2)}) collective-permute-start(bf16[5,64,128]{2,1,0:T(8,128)(2,1)S(1)} %dynamic-slice_convert_fusion), channel_id=1, source_target_pairs={{0,6},{1,7},{2,4},{3,5},{4,2},{5,3},{6,0},{7,1},{8,14},{9,15},{10,... | collective-permute-start | bytes 245768 | tf_op jit(solution)/shard_map/ppermute | solution.py:684
  8.4 15.9 %collective-permute-start.4 = (bf16[20,32,256]{2,1,0:T(8,128)(2,1)S(1)}, bf16[20,32,256]{2,1,0:T(8,128)(2,1)S(1)}, u32[]{:S(2)}, u32[]{:S(2)}) collective-permute-start(bf16[20,32,256]{2,1,0:T(8,128)(2,1)S(1)} %get-tuple-element.99), channel_id=1, source_target_pairs={{8,16},{16,8},{9,17},{17,9},{10,18},{18,10},{11,19},{19,11},{12,20... | collective-permute-start | bytes 983048 | tf_op jit(solution)/shard_map/ppermute | solution.py:699
  11.0 14.7 %copy-start = (bf16[10,64,128]{2,1,0:T(8,128)(2,1)}, bf16[10,64,128]{2,1,0:T(8,128)(2,1)S(1)}, u32[]{:S(2)}) copy-start(bf16[10,64,128]{2,1,0:T(8,128)(2,1)S(1)} %pad_maximum_fusion.4.refs_9_) | copy-start | bytes 491524
  13.6 2.7 %collective-permute-start.7 = (bf16[10,64,128]{2,1,0:T(8,128)(2,1)S(1)}, bf16[10,64,128]{2,1,0:T(8,128)(2,1)S(1)}, u32[]{:S(2)}, u32[]{:S(2)}) collective-permute-start(bf16[10,64,128]{2,1,0:T(8,128)(2,1)S(1)} %pad_maximum_fusion.4.refs_9_), channel_id=1, source_target_pairs={{0,8},{8,0},{16,24},{24,16},{1,9},{9,1},{17,25},{25,17},{2,10},{10... | collective-permute-start | bytes 491528 | tf_op jit(solution)/shard_map/ppermute | solution.py:684
  14.2 10.2 %collective-permute-start.3 = (bf16[20,32,256]{2,1,0:T(8,128)(2,1)S(1)}, bf16[20,32,256]{2,1,0:T(8,128)(2,1)S(1)}, u32[]{:S(2)}, u32[]{:S(2)}) collective-permute-start(bf16[20,32,256]{2,1,0:T(8,128)(2,1)S(1)} %get-tuple-element.100), channel_id=1, source_target_pairs={{0,8},{8,0},{16,24},{24,16},{1,9},{9,1},{17,25},{25,17},{2,10},{10... | collective-permute-start | bytes 983048 | tf_op jit(solution)/shard_map/ppermute | solution.py:684
  14.3 7.0 %collective-permute-start.5 = (bf16[10,64,128]{2,1,0:T(8,128)(2,1)S(1)}, bf16[10,64,128]{2,1,0:T(8,128)(2,1)S(1)}, u32[]{:S(2)}, u32[]{:S(2)}) collective-permute-start(bf16[10,64,128]{2,1,0:T(8,128)(2,1)S(1)} %pad_maximum_fusion.4.refs_9_), channel_id=1, source_target_pairs={{0,1},{1,0},{2,3},{3,2},{4,5},{5,4},{6,7},{7,6},{8,9},{9,8},{10,11... | collective-permute-start | bytes 491528 | tf_op jit(solution)/shard_map/ppermute | solution.py:684
  15.8 8.5 %collective-permute-start.6 = (bf16[10,64,128]{2,1,0:T(8,128)(2,1)S(1)}, bf16[10,64,128]{2,1,0:T(8,128)(2,1)S(1)}, u32[]{:S(2)}, u32[]{:S(2)}) collective-permute-start(bf16[10,64,128]{2,1,0:T(8,128)(2,1)S(1)} %pad_maximum_fusion.5.refs_10_), channel_id=1, source_target_pairs={{0,1},{1,0},{2,3},{3,2},{4,5},{5,4},{6,7},{7,6},{8,9},{9,8},{10,11... | collective-permute-start | bytes 491528 | tf_op jit(solution)/shard_map/ppermute | solution.py:684
  16.3 8.0 %collective-permute-start.8 = (bf16[10,64,128]{2,1,0:T(8,128)(2,1)S(1)}, bf16[10,64,128]{2,1,0:T(8,128)(2,1)S(1)}, u32[]{:S(2)}, u32[]{:S(2)}) collective-permute-start(bf16[10,64,128]{2,1,0:T(8,128)(2,1)S(1)} %pad_maximum_fusion.5.refs_10_), channel_id=1, source_target_pairs={{0,8},{8,0},{16,24},{24,16},{1,9},{9,1},{17,25},{25,17},{2,10},{10... | collective-permute-start | bytes 491528 | tf_op jit(solution)/shard_map/ppermute | solution.py:684
  21.3 3.1 %collective-permute-start.9 = (bf16[10,64,128]{2,1,0:T(8,128)(2,1)S(1)}, bf16[10,64,128]{2,1,0:T(8,128)(2,1)S(1)}, u32[]{:S(2)}, u32[]{:S(2)}) collective-permute-start(bf16[10,64,128]{2,1,0:T(8,128)(2,1)S(1)} %collective-permute-done.5.refs_11_), channel_id=1, source_target_pairs={{0,8},{8,0},{16,24},{24,16},{1,9},{9,1},{17,25},{25,17},{2,10},{10... | collective-permute-start | bytes 491528 | tf_op jit(solution)/shard_map/ppermute | solution.py:684
  24.3 1.4 %collective-permute-start.10 = (bf16[10,64,128]{2,1,0:T(8,128)(2,1)S(1)}, bf16[10,64,128]{2,1,0:T(8,128)(2,1)S(1)}, u32[]{:S(2)}, u32[]{:S(2)}) collective-permute-start(bf16[10,64,128]{2,1,0:T(8,128)(2,1)S(1)} %collective-permute-done.6.refs_12_), channel_id=1, source_target_pairs={{0,8},{8,0},{16,24},{24,16},{1,9},{9,1},{17,25},{25,17},{2,10},{10... | collective-permute-start | bytes 491528 | tf_op jit(solution)/shard_map/ppermute | solution.py:684
  62.8 2.5 %collective-permute-start.11 = (bf16[2,1424,128]{2,1,0:T(8,128)(2,1)}, bf16[2,1424,128]{2,1,0:T(8,128)(2,1)S(1)}, u32[]{:S(2)}, u32[]{:S(2)}) collective-permute-start(bf16[2,1424,128]{2,1,0:T(8,128)(2,1)} %get-tuple-element.65), channel_id=1, source_target_pairs={{0,8},{8,0},{16,24},{24,16},{1,9},{9,1},{17,25},{25,17},{2,10},{10... | collective-permute-start | bytes 2187272 | tf_op jit(solution)/shard_map/ppermute | solution.py:684
  66.8 13.7 %collective-permute-start.12 = (bf16[784,128]{1,0:T(8,128)(2,1)S(1)}, bf16[784,128]{1,0:T(8,128)(2,1)S(1)}, u32[]{:S(2)}, u32[]{:S(2)}) collective-permute-start(bf16[784,128]{1,0:T(8,128)(2,1)S(1)} %get-tuple-element.118), channel_id=1, source_target_pairs={{0,1},{1,0},{2,3},{3,2},{4,5},{5,4},{6,7},{7,6},{8,9},{9,8},{10,11... | collective-permute-start | bytes 602120 | tf_op jit(solution)/shard_map/ppermute | solution.py:760
  68.4 12.0 %collective-permute-start.14 = (bf16[784,128]{1,0:T(8,128)(2,1)S(1)}, bf16[784,128]{1,0:T(8,128)(2,1)S(1)}, u32[]{:S(2)}, u32[]{:S(2)}) collective-permute-start(bf16[784,128]{1,0:T(8,128)(2,1)S(1)} %get-tuple-element.116), channel_id=1, source_target_pairs={{0,17},{1,16},{2,19},{3,18},{4,21},{5,20},{6,23},{7,22},{8,25},{9,... | collective-permute-start | bytes 602120 | tf_op jit(solution)/shard_map/ppermute | solution.py:760
  69.6 10.9 %collective-permute-start.13 = (bf16[784,128]{1,0:T(8,128)(2,1)S(1)}, bf16[784,128]{1,0:T(8,128)(2,1)S(1)}, u32[]{:S(2)}, u32[]{:S(2)}) collective-permute-start(bf16[784,128]{1,0:T(8,128)(2,1)S(1)} %get-tuple-element.117), channel_id=1, source_target_pairs={{0,16},{1,17},{2,18},{3,19},{4,20},{5,21},{6,22},{7,23},{8,24},{9,... | collective-permute-start | bytes 602120 | tf_op jit(solution)/shard_map/ppermute | solution.py:760
  80.7 5.2 %collective-permute-start.15 = (bf16[304,128]{1,0:T(8,128)(2,1)S(1)}, bf16[304,128]{1,0:T(8,128)(2,1)S(1)}, u32[]{:S(2)}, u32[]{:S(2)}) collective-permute-start(bf16[304,128]{1,0:T(8,128)(2,1)S(1)} %get-tuple-element.113), channel_id=1, source_target_pairs={{0,2},{1,3},{2,0},{3,1},{4,6},{5,7},{6,4},{7,5},{8,10},{9,11},{10,... | collective-permute-start | bytes 233480 | tf_op jit(solution)/shard_map/ppermute | solution.py:684
  81.4 8.4 %collective-permute-start.16 = (bf16[304,128]{1,0:T(8,128)(2,1)S(1)}, bf16[304,128]{1,0:T(8,128)(2,1)S(1)}, u32[]{:S(2)}, u32[]{:S(2)}) collective-permute-start(bf16[304,128]{1,0:T(8,128)(2,1)S(1)} %get-tuple-element.114), channel_id=1, source_target_pairs={{0,4},{1,5},{2,6},{3,7},{4,0},{5,1},{6,2},{7,3},{8,12},{9,13},{10,... | collective-permute-start | bytes 233480 | tf_op jit(solution)/shard_map/ppermute | solution.py:684
  84.9 6.3 %collective-permute-start.17 = (bf16[304,128]{1,0:T(8,128)(2,1)S(1)}, bf16[304,128]{1,0:T(8,128)(2,1)S(1)}, u32[]{:S(2)}, u32[]{:S(2)}) collective-permute-start(bf16[304,128]{1,0:T(8,128)(2,1)S(1)} %get-tuple-element.115), channel_id=1, source_target_pairs={{0,6},{1,7},{2,4},{3,5},{4,2},{5,3},{6,0},{7,1},{8,14},{9,15},{10,... | collective-permute-start | bytes 233480 | tf_op jit(solution)/shard_map/ppermute | solution.py:684
  85.1 8.1 %collective-permute-start.21 = (bf16[20,32,256]{2,1,0:T(8,128)(2,1)S(1)}, bf16[20,32,256]{2,1,0:T(8,128)(2,1)S(1)}, u32[]{:S(2)}, u32[]{:S(2)}) collective-permute-start(bf16[20,32,256]{2,1,0:T(8,128)(2,1)S(1)} %copy-done.17), channel_id=1, source_target_pairs={{0,8},{8,0},{16,24},{24,16},{1,9},{9,1},{17,25},{25,17},{2,10},{10... | collective-permute-start | bytes 983048 | tf_op jit(solution)/shard_map/ppermute | solution.py:684
  85.2 8.1 %collective-permute-start.22 = (bf16[20,32,256]{2,1,0:T(8,128)(2,1)S(1)}, bf16[20,32,256]{2,1,0:T(8,128)(2,1)S(1)}, u32[]{:S(2)}, u32[]{:S(2)}) collective-permute-start(bf16[20,32,256]{2,1,0:T(8,128)(2,1)S(1)} %copy-done.16), channel_id=1, source_target_pairs={{8,16},{16,8},{9,17},{17,9},{10,18},{18,10},{11,19},{19,11},{12,20... | collective-permute-start | bytes 983048 | tf_op jit(solution)/shard_map/ppermute | solution.py:699
  91.3 4.8 %collective-permute-start.20 = (bf16[304,128]{1,0:T(8,128)(2,1)S(1)}, bf16[304,128]{1,0:T(8,128)(2,1)S(1)}, u32[]{:S(2)}, u32[]{:S(2)}) collective-permute-start(bf16[304,128]{1,0:T(8,128)(2,1)S(1)} %add_convert_fusion.1.refs_2_), channel_id=1, source_target_pairs={{0,24},{8,16},{16,8},{24,0},{1,25},{9,17},{17,9},{25,1},{2,26},{10... | collective-permute-start | bytes 233480 | tf_op jit(solution)/shard_map/ppermute | solution.py:684
  91.4 6.0 %collective-permute-start.19 = (bf16[304,128]{1,0:T(8,128)(2,1)S(1)}, bf16[304,128]{1,0:T(8,128)(2,1)S(1)}, u32[]{:S(2)}, u32[]{:S(2)}) collective-permute-start(bf16[304,128]{1,0:T(8,128)(2,1)S(1)} %add_convert_fusion.1.refs_2_), channel_id=1, source_target_pairs={{0,16},{8,24},{16,0},{24,8},{1,17},{9,25},{17,1},{25,9},{2,18},{10... | collective-permute-start | bytes 233480 | tf_op jit(solution)/shard_map/ppermute | solution.py:684
  91.7 5.7 %collective-permute-start.18 = (bf16[304,128]{1,0:T(8,128)(2,1)S(1)}, bf16[304,128]{1,0:T(8,128)(2,1)S(1)}, u32[]{:S(2)}, u32[]{:S(2)}) collective-permute-start(bf16[304,128]{1,0:T(8,128)(2,1)S(1)} %add_convert_fusion.1.refs_2_), channel_id=1, source_target_pairs={{0,8},{8,0},{16,24},{24,16},{1,9},{9,1},{17,25},{25,17},{2,10},{10... | collective-permute-start | bytes 233480 | tf_op jit(solution)/shard_map/ppermute | solution.py:684
  (17 other events, 80.2 us)
